TPU v7x, 512 devices: a whole 4x8x8 slice. The times are simulated.
512 devices in a mesh: doc: 4 (over x), seq: 128 (over y, z, core).
Axes of the slice: x: 4, y: 8, z: 8, core: 2. Of those that a mesh axis runs over, the one named last changes fastest.
Arguments:
- hidden_rows: bfloat16 [262144, 2048], P(('doc', 'seq')), parts along dimension 0, may hold values from -24 to 24
- w_expand: bfloat16 [2048, 8192], P(None, 'seq'), may hold values from -0.125 to 0.125
- w_contract: bfloat16 [8192, 2048], P('seq'), may hold values from -0.25 to 0.25
Outputs:
- short_out: bfloat16 [1024, 2048], P('doc', 'seq'), parts along dimension 0
There are 4 independent parts, one for each index of `doc`. A program takes and returns all parts, laid end to end along the dimension named above; an argument that names none is the same for every part. Nothing has to cross between parts.
All inputs are finite; a program needn't handle non-finite values.
Results may differ from a plain program's by a relative error of at most 0.0057.
Values may be sent and summed in bfloat16 or wider, within the bound.
No kernel may reach another device: no remote copies, remote signals or barrier semaphores. Data moves between devices by JAX's collectives and lax.ppermute only.
A program may use at most 64 MiB of HBM per device.

v0:
```python
import math

import jax
import jax.numpy as jnp
from jax import lax
from jax.sharding import PartitionSpec as P

KEEP = 256


def cosine_table(first_row, count, seq_len, keep):
    freq = jnp.arange(keep, dtype=jnp.int32)
    posit = first_row + jnp.arange(count, dtype=jnp.int32)
    phase = (2 * posit[None, :] + 1) * freq[:, None] % (4 * seq_len)
    return jnp.cos(phase.astype(jnp.float32) * (math.pi / (2.0 * seq_len))).astype(jnp.bfloat16)


def local(hidden_rows, w_expand, w_contract):
    groups = lax.axis_size("seq")
    local_rows = hidden_rows.shape[0]
    seq_len = local_rows * groups
    flipped = jnp.transpose(hidden_rows)
    columns = lax.all_to_all(flipped, "seq", split_axis=0, concat_axis=1, tiled=True)
    block_len = math.gcd(seq_len, 8192)

    def add_block(step, total):
        first_row = (step * block_len).astype(jnp.int32)
        rows_block = lax.dynamic_slice_in_dim(columns, first_row, block_len, 1)
        table_block = cosine_table(first_row, block_len, seq_len, KEEP)
        return total + lax.dot_general(
            rows_block, table_block, (((1,), (1,)), ((), ())), preferred_element_type=jnp.float32
        )

    start_sum = jnp.zeros((columns.shape[0], KEEP), jnp.float32)
    summed = jnp.transpose(lax.fori_loop(0, seq_len // block_len, add_block, start_sum))
    coeffs = (math.sqrt(2.0 / seq_len) * summed).astype(jnp.bfloat16)
    wide = coeffs.astype(jnp.float32)
    model_width = wide.shape[1] * groups
    squares = lax.psum(jnp.sum(wide * wide, axis=1), "seq")
    product = jnp.dot(
        lax.all_gather(coeffs, "seq", axis=1, tiled=True),
        w_expand,
        preferred_element_type=jnp.float32,
    )
    scale = lax.rsqrt(squares / model_width + 1e-06)
    activated = jax.nn.gelu(product * scale[:, None]).astype(jnp.bfloat16)
    branch = jnp.dot(activated, w_contract, preferred_element_type=jnp.float32)
    mine = lax.psum_scatter(branch, "seq", scatter_dimension=1, tiled=True)
    return (wide + mine).astype(jnp.bfloat16)


def solution(mesh):
    return jax.shard_map(
        local,
        mesh=mesh,
        in_specs=(P(("doc", "seq"), None), P(None, "seq"), P("seq", None)),
        out_specs=P("doc", "seq"),
        check_vma=False,
    )
```

profile of v0, /device:TPU:1, one launch (start us, length us, event | category | flops | bytes accessed | tf_op | source)
XLA Modules:
  0.0 817.2 jit_solution(612094346551430218)
XLA Ops:
  6.5 4.0 copy.6
  10.5 18.4 %all-to-all-start = ((bf16[128,16,512]{2,1,0:T(8,128)(2,1)}), bf16[128,16,512]{2,1,0:T(8,128)(2,1)S(1)}, u32[]{:S(2)}, u32[]{:S(2)}) async-start(bf16[128,16,512]{2,1,0:T(8,128)(2,1)} %bitcast.13), calls=%async_computation | async-start | bytes 4194304 | tf_op jit(solution)/shard_map/all_to_all | solution.py:23
  28.9 0.0 all-gather.2.cloned.1.call-start
  29.0 52.1 %all-to-all-done = bf16[128,16,512]{2,1,0:T(8,128)(2,1)S(1)} async-done(((bf16[128,16,512]{2,1,0:T(8,128)(2,1)}), bf16[128,16,512]{2,1,0:T(8,128)(2,1)S(1)}, u32[]{:S(2)}, u32[]{:S(2)}) %all-to-all-start) | async-done | bytes 2097184 | tf_op jit(solution)/shard_map/all_to_all | solution.py:23
  81.1 1.5 copy.8
  82.6 285.4 %while.16 = (s32[]{:T(128)}, f32[16,256]{1,0:T(8,128)S(1)}, bf16[16,65536]{1,0:T(8,128)(2,1)}, s32[]{:T(128)}, s32[]{:T(128)}, /*index=5*/s32[]{:T(128)}, s32[]{:T(128)}) while((s32[]{:T(128)}, f32[16,256]{1,0:T(8,128)S(1)}, bf16[16,65536]{1,0:T(8,128)(2,1)}, s32[]{:T(128)}, s32[]{:T(128)}, /*index=5*/s32[]{:T(128)}, ...), condition=%wide.region_1.2_spmd.clone, body=%wide.region_0.1_spmd.clone.sunk | while | flops 98598920 | bytes 360589 | solution.py:35
  82.6 35.7 %fusion.48 = f32[16,256]{1,0:T(8,128)S(1)} fusion(s32[8192]{0:T(1024)S(1)} %multiply_add_fusion.2, bf16[16,65536]{1,0:T(8,128)(2,1)} %get-tuple-element.150, s32[]{:T(128)S(6)} %select_n.47, f32[16,256]{1,0:T(8,128)S(1)} %get-tuple-element.142, pred[]{:T(512)S(6)} %compare.4), kind=kOutput, calls=%fused_computation.12.clone.1 | convolution fusion | flops 98574336 | bytes 327685 | tf_op jit(solution)/shard_map/while/body/eval_jaxpr/dot_general | solution.py:30
  118.3 35.6 %fusion.48 = f32[16,256]{1,0:T(8,128)S(1)} fusion(s32[8192]{0:T(1024)S(1)} %multiply_add_fusion.2, bf16[16,65536]{1,0:T(8,128)(2,1)} %get-tuple-element.150, s32[]{:T(128)S(6)} %select_n.47, f32[16,256]{1,0:T(8,128)S(1)} %get-tuple-element.142, pred[]{:T(512)S(6)} %compare.4), kind=kOutput, calls=%fused_computation.12.clone.1 | convolution fusion | flops 98574336 | bytes 327685 | tf_op jit(solution)/shard_map/while/body/eval_jaxpr/dot_general | solution.py:30
  153.9 35.6 %fusion.48 = f32[16,256]{1,0:T(8,128)S(1)} fusion(s32[8192]{0:T(1024)S(1)} %multiply_add_fusion.2, bf16[16,65536]{1,0:T(8,128)(2,1)} %get-tuple-element.150, s32[]{:T(128)S(6)} %select_n.47, f32[16,256]{1,0:T(8,128)S(1)} %get-tuple-element.142, pred[]{:T(512)S(6)} %compare.4), kind=kOutput, calls=%fused_computation.12.clone.1 | convolution fusion | flops 98574336 | bytes 327685 | tf_op jit(solution)/shard_map/while/body/eval_jaxpr/dot_general | solution.py:30
  189.6 35.6 %fusion.48 = f32[16,256]{1,0:T(8,128)S(1)} fusion(s32[8192]{0:T(1024)S(1)} %multiply_add_fusion.2, bf16[16,65536]{1,0:T(8,128)(2,1)} %get-tuple-element.150, s32[]{:T(128)S(6)} %select_n.47, f32[16,256]{1,0:T(8,128)S(1)} %get-tuple-element.142, pred[]{:T(512)S(6)} %compare.4), kind=kOutput, calls=%fused_computation.12.clone.1 | convolution fusion | flops 98574336 | bytes 327685 | tf_op jit(solution)/shard_map/while/body/eval_jaxpr/dot_general | solution.py:30
  225.3 35.6 %fusion.48 = f32[16,256]{1,0:T(8,128)S(1)} fusion(s32[8192]{0:T(1024)S(1)} %multiply_add_fusion.2, bf16[16,65536]{1,0:T(8,128)(2,1)} %get-tuple-element.150, s32[]{:T(128)S(6)} %select_n.47, f32[16,256]{1,0:T(8,128)S(1)} %get-tuple-element.142, pred[]{:T(512)S(6)} %compare.4), kind=kOutput, calls=%fused_computation.12.clone.1 | convolution fusion | flops 98574336 | bytes 327685 | tf_op jit(solution)/shard_map/while/body/eval_jaxpr/dot_general | solution.py:30
  261.0 35.6 %fusion.48 = f32[16,256]{1,0:T(8,128)S(1)} fusion(s32[8192]{0:T(1024)S(1)} %multiply_add_fusion.2, bf16[16,65536]{1,0:T(8,128)(2,1)} %get-tuple-element.150, s32[]{:T(128)S(6)} %select_n.47, f32[16,256]{1,0:T(8,128)S(1)} %get-tuple-element.142, pred[]{:T(512)S(6)} %compare.4), kind=kOutput, calls=%fused_computation.12.clone.1 | convolution fusion | flops 98574336 | bytes 327685 | tf_op jit(solution)/shard_map/while/body/eval_jaxpr/dot_general | solution.py:30
  296.6 35.6 %fusion.48 = f32[16,256]{1,0:T(8,128)S(1)} fusion(s32[8192]{0:T(1024)S(1)} %multiply_add_fusion.2, bf16[16,65536]{1,0:T(8,128)(2,1)} %get-tuple-element.150, s32[]{:T(128)S(6)} %select_n.47, f32[16,256]{1,0:T(8,128)S(1)} %get-tuple-element.142, pred[]{:T(512)S(6)} %compare.4), kind=kOutput, calls=%fused_computation.12.clone.1 | convolution fusion | flops 98574336 | bytes 327685 | tf_op jit(solution)/shard_map/while/body/eval_jaxpr/dot_general | solution.py:30
  332.3 35.6 %fusion.48 = f32[16,256]{1,0:T(8,128)S(1)} fusion(s32[8192]{0:T(1024)S(1)} %multiply_add_fusion.2, bf16[16,65536]{1,0:T(8,128)(2,1)} %get-tuple-element.150, s32[]{:T(128)S(6)} %select_n.47, f32[16,256]{1,0:T(8,128)S(1)} %get-tuple-element.142, pred[]{:T(512)S(6)} %compare.4), kind=kOutput, calls=%fused_computation.12.clone.1 | convolution fusion | flops 98574336 | bytes 327685 | tf_op jit(solution)/shard_map/while/body/eval_jaxpr/dot_general | solution.py:30
  367.9 0.6 fusion.32
  368.6 0.0 all-gather.2.cloned.1.call-update
  368.6 0.0 reduce-scatter.2.cloned.1.call-start
  368.6 246.8 %psum.7 = f32[256]{0:T(256)S(1)} all-reduce(f32[256]{0:T(256)S(1)} %get-tuple-element.113), channel_id=1, replica_groups=mesh['doc'=4,'seq'=128] {'seq'}, use_global_device_ids=true, to_apply=%region_3.4 | all-reduce | flops 256 | bytes 2048 | tf_op jit(solution)/shard_map/psum | solution.py:39
  615.5 0.0 all-gather.2.cloned.1.call-done
  615.5 0.0 copy-done
  615.5 3.5 fusion.26
  619.1 0.0 reduce-scatter.2.cloned.1.call-update
  619.1 190.0 %reduce-scatter.2.cloned.1.call-done = f32[256,16]{0,1:T(8,128)} async-done(((f32[256,2048]{0,1:T(8,128)}), f32[256,16]{0,1:T(8,128)}) %reduce-scatter.2.cloned.1.call-update) | async-done | bytes 16400 | tf_op jit(solution)/shard_map/reduce_scatter | solution.py:48
  809.1 1.3 fusion.33
  (15 shorter events, 0.1 us)
Async XLA Ops:
  6.5 609.0 %copy-start = (bf16[64,2048]{1,0:T(8,128)(2,1)S(1)}, bf16[64,2048]{1,0:T(8,128)(2,1)}, u32[]{:S(2)}) copy-start(bf16[64,2048]{1,0:T(8,128)(2,1)} %param.7) | copy-start | bytes 786436
  10.5 70.6 %all-to-all-start = ((bf16[128,16,512]{2,1,0:T(8,128)(2,1)}), bf16[128,16,512]{2,1,0:T(8,128)(2,1)S(1)}, u32[]{:S(2)}, u32[]{:S(2)}) async-start(bf16[128,16,512]{2,1,0:T(8,128)(2,1)} %bitcast.13), calls=%async_computation | async-start | bytes 4194304 | tf_op jit(solution)/shard_map/all_to_all | solution.py:23
  28.9 586.6 %all-gather.2.cloned.1.call-start = ((), (), s32[]{:S(2)}) async-start(), calls=%async_computation.2 | async-start | bytes 1056768 | tf_op jit(solution)/shard_map/all_gather | solution.py:41
  82.6 533.0 %copy-start.1 = (bf16[2048,64]{0,1:T(8,128)(2,1)S(1)}, bf16[2048,64]{0,1:T(8,128)(2,1)}, u32[]{:S(2)}) copy-start(bf16[2048,64]{0,1:T(8,128)(2,1)} %param.6) | copy-start | bytes 786436
  368.6 440.5 %reduce-scatter.2.cloned.1.call-start = ((), (), s32[]{:S(2)}) async-start(), calls=%async_computation.3 | async-start | bytes 2113536 | tf_op jit(solution)/shard_map/reduce_scatter | solution.py:48
  615.5 193.6 %copy-start.2 = (bf16[256,16]{0,1:T(8,128)(2,1)S(1)}, bf16[256,16]{0,1:T(8,128)(2,1)}, u32[]{:S(2)}) copy-start(bf16[256,16]{0,1:T(8,128)(2,1)} %get-tuple-element.114) | copy-start | bytes 24580
Sparse Core Ops, SparseCore 0:
  368.7 74.5 all-gather.1
  619.2 189.8 reduce-scatter.1
where the time goes:
time: 822 us; the launch traced here: 817 us
  matrix products  289 us (35%)
  blocking collectives  247 us (30%)
  waiting for transfers between devices  242 us (29%)
  starting transfers between devices  18.5 us (2%)
  between operations  13.5 us (2%)
    dot_general x8, matrix products, add_block(): lax.dot_general(rows_block, table_block, (((1,), (1,)), ((), ())), prefer...  285 us
    psum x1, blocking collectives, local(): squares = lax.psum(jnp.sum(wide * wide, axis=1), 'seq')  247 us
    reduce_scatter x1, waiting for transfers between devices, local(): mine = lax.psum_scatter(branch, 'seq', scatter_dimension=1, tiled=True)  190 us
    all_to_all x1, waiting for transfers between devices, local(): lax.all_to_all(flipped, 'seq', split_axis=0, concat_axis=1, tiled=True)  52.1 us
    all_to_all x1, starting transfers between devices, local(): lax.all_to_all(flipped, 'seq', split_axis=0, concat_axis=1, tiled=True)  18.4 us
  transfers between devices with their start and end apart: 3, of which 2 were waited for; matrix products, arithmetic and copies ran while one was open for 0% of the time, Pallas kernels for 0%

commit v1 on v0

v1 whole, which is shorter than its diff:
```python
import math

import jax
import jax.numpy as jnp
import numpy as np
from jax import lax
from jax.experimental import pallas as pl
from jax.experimental.pallas import tpu as pltpu
from jax.sharding import PartitionSpec as P

KEEP = 256
MOMENTS = 16
F32, BF16 = jnp.float32, jnp.bfloat16


def split_halves(array):
    high = np.asarray(array, np.float32).astype(jnp.bfloat16)
    low = (np.asarray(array, np.float64) - high.astype(np.float64)).astype(jnp.bfloat16)
    return high, low


def window_tables(rows, windows):
    t = (2.0 * np.arange(rows) + 1.0 - rows) / rows
    basis, _ = np.linalg.qr(np.polynomial.chebyshev.chebvander(t, MOMENTS - 1))
    basis = basis[:, list(range(0, MOMENTS, 2)) + list(range(1, MOMENTS, 2))]
    k = np.arange(KEEP)
    inner = np.pi * np.outer(k, t) / (2 * windows)
    norm = math.sqrt(2.0 / (rows * windows))
    even = norm * np.cos(inner) @ basis[:, : MOMENTS // 2]
    odd = -norm * np.sin(inner) @ basis[:, MOMENTS // 2 :]
    expand = np.concatenate([even, odd], axis=1).T.astype(np.float32)
    high, low = split_halves(basis.T)
    project = np.concatenate([high, low], axis=0)
    theta = np.pi * np.outer(2 * np.arange(windows) + 1, k) / (2 * windows)
    trig = np.concatenate([np.cos(theta), np.sin(theta)], axis=1)
    trig = trig.reshape(windows // 2, 2, 2 * KEEP).transpose(1, 0, 2)
    high, low = split_halves(trig)
    return project, expand, np.concatenate([high, low, high, low], axis=1)


def moments_kernel(project_ref, rows_ref, out_ref):
    both = jnp.dot(project_ref[...], rows_ref[...], preferred_element_type=F32)
    moments = both[:MOMENTS] + both[MOMENTS:]
    copies = jnp.concatenate([moments] * 8, axis=0)
    row = lax.broadcasted_iota(jnp.int32, (128, 128), 0) % 8
    lane = lax.broadcasted_iota(jnp.int32, (128, 128), 1) // MOMENTS
    for block in range(moments.shape[1] // 128):
        turned = copies[:, 128 * block : 128 * (block + 1)].T
        packed = jnp.where(row == lane, turned, 0.0).reshape(16, 8, 128).sum(axis=1)
        out_ref[16 * block : 16 * (block + 1), :] = packed


def coeffs_kernel(core_ref, moments_ref, trig_ref, expand_ref, out_ref):
    trig = trig_ref[0]
    sources = trig.shape[0] // 4
    expand = expand_ref[...]
    half = MOMENTS // 2
    for part in range(4):
        rows = moments_ref[pl.ds(part, sources, stride=4), :]
        high = rows.astype(BF16)
        low = (rows - high.astype(F32)).astype(BF16)
        stacked = jnp.concatenate([high, high, low, low], axis=0)
        turned = lax.dot_general(stacked, trig, (((0,), (0,)), ((), ())), preferred_element_type=F32)
        even = turned[:, :KEEP].reshape(8, MOMENTS, KEEP)[:, :half]
        odd = turned[:, KEEP:].reshape(8, MOMENTS, KEEP)[:, half:]
        out_ref[8 * part : 8 * (part + 1), :] = (even * expand[:half] + odd * expand[half:]).sum(axis=1)


def feed_forward_kernel(coeffs_ref, expand_ref, contract_ref, out_ref):
    coeffs = coeffs_ref[...]
    wide = coeffs.astype(F32)
    scale = lax.rsqrt(jnp.sum(wide * wide, axis=0, keepdims=True) / coeffs.shape[0] + 1e-06)
    expanded = jnp.dot(expand_ref[...], coeffs, preferred_element_type=F32) * scale
    activated = jax.nn.gelu(expanded).astype(BF16)
    branch = lax.dot_general(contract_ref[...], activated, (((0,), (0,)), ((), ())), preferred_element_type=F32)
    out_ref[...] = branch.astype(BF16)


def add_kernel(parts_ref, coeffs_ref, out_ref):
    total = jnp.sum(parts_ref[...].astype(F32), axis=0)
    out_ref[...] = (coeffs_ref[...].astype(F32) + total).astype(BF16)


def local(hidden_rows, w_expand, w_contract):
    rows, width = hidden_rows.shape
    windows = lax.axis_size("seq")
    chips = windows // 2
    mine = width // chips
    project, expand, trig = window_tables(rows, windows)
    same_core = [list(range(core, windows, 2)) for core in range(2)]
    pairs = [[2 * chip, 2 * chip + 1] for chip in range(chips)]
    core = lax.axis_index("seq") % 2

    def exchange(x):
        return lax.all_to_all(x, "seq", 0, 0, axis_index_groups=same_core)

    def gather_pair(x):
        return lax.all_gather(x, "seq", axis_index_groups=pairs)

    units_in = gather_pair(w_expand.T).reshape(-1, width)
    units_out = gather_pair(w_contract).reshape(-1, width)

    steps = 4
    moments = pl.pallas_call(
        moments_kernel,
        grid=(steps,),
        in_specs=[
            pl.BlockSpec((2 * MOMENTS, rows), lambda i: (0, 0)),
            pl.BlockSpec((rows, width // steps), lambda i: (0, i)),
        ],
        out_specs=pl.BlockSpec((width // 8 // steps, 128), lambda i: (i, 0)),
        out_shape=jax.ShapeDtypeStruct((width // 8, 128), F32),
    )(jnp.asarray(project), hidden_rows)
    received = exchange(moments.reshape(chips, -1, 128)).reshape(-1, 128)
    partial = pl.pallas_call(
        coeffs_kernel,
        grid_spec=pltpu.PrefetchScalarGridSpec(
            num_scalar_prefetch=1,
            grid=(1,),
            in_specs=[
                pl.BlockSpec(received.shape, lambda i, core: (0, 0)),
                pl.BlockSpec((1,) + trig.shape[1:], lambda i, core: (core[0], 0, 0)),
                pl.BlockSpec(expand.shape, lambda i, core: (0, 0)),
            ],
            out_specs=pl.BlockSpec((mine, KEEP), lambda i, core: (0, 0)),
        ),
        out_shape=jax.ShapeDtypeStruct((mine, KEEP), F32),
    )(core.astype(jnp.int32).reshape(1), received, jnp.asarray(trig), jnp.asarray(expand))
    both = gather_pair(partial)
    coeffs = (both[0] + both[1]).astype(BF16)
    coeffs = jnp.where(core == 0, coeffs[:, : KEEP // 2], coeffs[:, KEEP // 2 :])
    spread = exchange(jnp.broadcast_to(coeffs[None], (chips,) + coeffs.shape)).reshape(width, -1)
    branch = pl.pallas_call(
        feed_forward_kernel,
        out_shape=jax.ShapeDtypeStruct(spread.shape, BF16),
    )(spread, units_in, units_out)
    parts = exchange(branch.reshape(chips, mine, -1))
    result = pl.pallas_call(
        add_kernel,
        out_shape=jax.ShapeDtypeStruct(coeffs.shape, BF16),
    )(parts, coeffs)
    halves = gather_pair(result)
    halves = jnp.where(core == 0, halves[:, : mine // 2], halves[:, mine // 2 :])
    return jnp.transpose(halves, (0, 2, 1)).reshape(KEEP, mine // 2)


def solution(mesh):
    return jax.shard_map(
        local,
        mesh=mesh,
        in_specs=(P(("doc", "seq"), None), P(None, "seq"), P("seq", None)),
        out_specs=P("doc", "seq"),
        check_vma=False,
    )
```

time: 822 us -> 97.6 us (0.12)
  matrix products: 289 us -> 0 us
  waiting for transfers between devices: 242 us -> 24.2 us
  blocking collectives: 247 us -> 37.6 us
  between operations: 13.5 us -> 0.06 us
  Pallas kernels: 0 us -> 10.5 us
    dot_general x9 -> x0, matrix products: 289 us -> none  [the longest x8 285 us: add_block(): lax.dot_general(rows_block, table_block, (((1,), (1,)), ((), ())), prefer...]
    psum x1 -> x0, blocking collectives: 247 us -> none  [local(): squares = lax.psum(jnp.sum(wide * wide, axis=1), 'seq')]
    reduce_scatter x1 -> x0, waiting for transfers between devices: 190 us -> none  [local(): mine = lax.psum_scatter(branch, 'seq', scatter_dimension=1, tiled=True)]
    all_to_all x1 -> x2, waiting for transfers between devices: 52.1 us -> 24.2 us  [exchange(): return lax.all_to_all(x, 'seq', 0, 0, axis_index_groups=same_core)]
    all_to_all x0 -> x1, blocking collectives: none -> 23.6 us  [exchange(): return lax.all_to_all(x, 'seq', 0, 0, axis_index_groups=same_core)]
    all_gather x0 -> x4, blocking collectives: none -> 14 us  [gather_pair(): return lax.all_gather(x, 'seq', axis_index_groups=pairs)]
    pallas_call x0 -> x4, Pallas kernels: none -> 10.5 us  [the longest x1 4.05 us: local(): pl.pallas_call(moments_kernel, grid=(steps,), in_specs=[pl.BlockSpec((2 *...]
    all_to_all x1 -> x2, starting transfers between devices: 18.4 us -> 21.9 us  [exchange(): return lax.all_to_all(x, 'seq', 0, 0, axis_index_groups=same_core)]
  transfers between devices with their start and end apart: 3 -> 2, of which waited for: 2 -> 2; matrix products, arithmetic and copies ran while one was open for 0% -> 0% of each run, Pallas kernels for 0% -> 0%
where the time goes in v1:
time: 97.6 us; the launch traced here: 97.2 us
  blocking collectives  37.6 us (39%)
  waiting for transfers between devices  24.2 us (25%)
  starting transfers between devices  21.9 us (22%)
  Pallas kernels  10.5 us (11%)
  local copies, waits for them, and re-layouts  2.33 us (2%)
    all_to_all x2, waiting for transfers between devices, exchange(): return lax.all_to_all(x, 'seq', 0, 0, axis_index_groups=same_core)  24.2 us
    all_to_all x1, blocking collectives, exchange(): return lax.all_to_all(x, 'seq', 0, 0, axis_index_groups=same_core)  23.6 us
    all_to_all x2, starting transfers between devices, exchange(): return lax.all_to_all(x, 'seq', 0, 0, axis_index_groups=same_core)  21.9 us
    all_gather x4, blocking collectives, gather_pair(): return lax.all_gather(x, 'seq', axis_index_groups=pairs)  14 us
    pallas_call x1, Pallas kernels, local(): pl.pallas_call(moments_kernel, grid=(steps,), in_specs=[pl.BlockSpec((2 *...  4.05 us
    pallas_call x1, Pallas kernels, local(): pl.pallas_call(feed_forward_kernel, out_shape=jax.ShapeDtypeStruct(spread...  2.78 us
  transfers between devices with their start and end apart: 2, of which 2 were waited for; matrix products, arithmetic and copies ran while one was open for 0% of the time, Pallas kernels for 0%

profile of v1, /device:TPU:1, one launch (start us, length us, event | category | flops | bytes accessed | tf_op | source)
XLA Modules:
  0.0 97.2 jit_solution(10736956262399129385)
XLA Ops:
  0.0 0.0 copy-start.2
  0.0 4.1 %shard_map.64 = f32[256,128]{1,0:T(8,128)} custom-call(bf16[32,512]{1,0:T(8,128)(2,1)} %constant.24.clone.project_ref, bf16[512,2048]{1,0:T(8,128)(2,1)} %rows_ref.1), custom_call_target="tpu_custom_call" | custom-call | tf_op jit(solution)/shard_map/pallas_call | solution.py:104
  4.1 0.0 copy-start.3
  4.1 17.3 %all-to-all-start = ((f32[64,4,128]{2,1,0:T(4,128)}), f32[64,4,128]{2,1,0:T(4,128)S(1)}, u32[]{:S(2)}, u32[]{:S(2)}) async-start(f32[64,4,128]{2,1,0:T(4,128)} %bitcast.16), calls=%async_computation | async-start | bytes 262144 | tf_op jit(solution)/shard_map/all_to_all | solution.py:95
  21.3 11.5 %all-to-all-done = f32[64,4,128]{2,1,0:T(4,128)S(1)} async-done(((f32[64,4,128]{2,1,0:T(4,128)}), f32[64,4,128]{2,1,0:T(4,128)S(1)}, u32[]{:S(2)}, u32[]{:S(2)}) %all-to-all-start) | async-done | bytes 131104 | tf_op jit(solution)/shard_map/all_to_all | solution.py:95
  32.8 0.0 copy-start.1
  32.8 0.6 copy-done.1
  33.5 1.9 %shard_map.65 = f32[32,256]{1,0:T(8,128)} custom-call(s32[1]{0:T(128)} %bitcast.core_ref, f32[256,128]{1,0:T(8,128)} %bitcast.15, bf16[2,256,512]{2,1,0:T(8,128)(2,1)} %constant.25.clone.trig_ref, f32[16,256]{1,0:T(8,128)} %constant.26.clone.expand_ref), custom_call_target="tpu_custom_call" | custom-call | tf_op jit(solution)/shard_map/pallas_call | solution.py:115
  35.4 3.9 %all-gather = f32[64,256]{1,0:T(8,128)S(1)} all-gather(f32[32,256]{1,0:T(8,128)} %shard_map.65), channel_id=2, replica_groups={{0,1},{2,3},{4,5},{6,7},{8,9},{10,11},{12,13},{14,15},{16,17},{18,19},{..., dimensions={0}, use_global_device_ids=true | all-gather | bytes 98304 | tf_op jit(solution)/shard_map/all_gather | solution.py:98
  39.3 0.0 copy-start.4
  39.3 0.9 broadcast_in_dim.2
  40.2 4.6 %all-to-all-start.1 = ((bf16[64,32,128]{2,1,0:T(8,128)(2,1)}), bf16[64,32,128]{2,1,0:T(8,128)(2,1)S(1)}, u32[]{:S(2)}, u32[]{:S(2)}) async-start(bf16[64,32,128]{2,1,0:T(8,128)(2,1)} %broadcast_in_dim.2), calls=%async_computation.1 | async-start | bytes 1048576 | tf_op jit(solution)/shard_map/all_to_all | solution.py:95
  44.8 0.0 copy-done.2
  44.8 2.3 %all-gather.1.expand_ref = bf16[128,2048]{1,0:T(8,128)(2,1)} all-gather(bf16[64,2048]{1,0:T(8,128)(2,1)S(1)} %bitcast.17), channel_id=3, replica_groups={{0,1},{2,3},{4,5},{6,7},{8,9},{10,11},{12,13},{14,15},{16,17},{18,19},{..., dimensions={0}, use_global_device_ids=true | all-gather | bytes 786432 | tf_op jit(solution)/shard_map/all_gather | solution.py:98
  47.2 0.0 copy-done.3
  47.2 2.3 %all-gather.2.contract_ref = bf16[128,2048]{1,0:T(8,128)(2,1)} all-gather(bf16[64,2048]{1,0:T(8,128)(2,1)S(1)} %copy-done.3), channel_id=4, replica_groups={{0,1},{2,3},{4,5},{6,7},{8,9},{10,11},{12,13},{14,15},{16,17},{18,19},{..., dimensions={0}, use_global_device_ids=true | all-gather | bytes 786432 | tf_op jit(solution)/shard_map/all_gather | solution.py:98
  49.5 12.7 %all-to-all-done.1 = bf16[64,32,128]{2,1,0:T(8,128)(2,1)S(1)} async-done(((bf16[64,32,128]{2,1,0:T(8,128)(2,1)}), bf16[64,32,128]{2,1,0:T(8,128)(2,1)S(1)}, u32[]{:S(2)}, u32[]{:S(2)}) %all-to-all-start.1) | async-done | bytes 524320 | tf_op jit(solution)/shard_map/all_to_all | solution.py:95
  62.1 0.8 copy-done
  62.9 2.8 %shard_map.66 = bf16[2048,128]{1,0:T(8,128)(2,1)} custom-call(bf16[2048,128]{1,0:T(8,128)(2,1)} %bitcast.13, bf16[128,2048]{1,0:T(8,128)(2,1)} %all-gather.1.expand_ref, bf16[128,2048]{1,0:T(8,128)(2,1)} %all-gather.2.contract_ref), custom_call_target="tpu_custom_call" | custom-call | tf_op jit(solution)/shard_map/pallas_call | solution.py:133
  65.7 0.0 copy-done.4
  65.7 23.6 %all_to_all.15.parts_ref = bf16[64,32,128]{2,1,0:T(8,128)(2,1)} all-to-all(bf16[64,32,128]{2,1,0:T(8,128)(2,1)} %bitcast.14), channel_id=1, replica_groups={{0,2,4,6,8,10,12,14,16,18,20,22,24,26,28,30,32,34,36,38,40,42,44,46,48,..., dimensions={0} | all-to-all | bytes 1048576 | tf_op jit(solution)/shard_map/all_to_all | solution.py:95
  89.3 1.7 %shard_map.67 = bf16[32,128]{1,0:T(8,128)(2,1)} custom-call(bf16[64,32,128]{2,1,0:T(8,128)(2,1)} %all_to_all.15.parts_ref, bf16[32,128]{1,0:T(8,128)(2,1)} %copy-done.4), custom_call_target="tpu_custom_call" | custom-call | tf_op jit(solution)/shard_map/pallas_call | solution.py:138
  91.0 5.5 %all-gather.3 = bf16[64,128]{1,0:T(8,128)(2,1)S(1)} all-gather(bf16[32,128]{1,0:T(8,128)(2,1)} %shard_map.67), channel_id=5, replica_groups={{0,1},{2,3},{4,5},{6,7},{8,9},{10,11},{12,13},{14,15},{16,17},{18,19},{..., dimensions={0}, use_global_device_ids=true | all-gather | bytes 24576 | tf_op jit(solution)/shard_map/all_gather | solution.py:98
  96.5 0.6 copy_bitcast_fusion
  (3 shorter events, 0.0 us)
Async XLA Ops:
  0.0 44.8 %copy-start.2 = (bf16[2048,64]{0,1:T(8,128)(2,1)S(1)}, bf16[2048,64]{0,1:T(8,128)(2,1)}, u32[]{:S(2)}) copy-start(bf16[2048,64]{0,1:T(8,128)(2,1)} %param.7) | copy-start | bytes 786436
  4.1 43.1 %copy-start.3 = (bf16[64,2048]{1,0:T(8,128)(2,1)S(1)}, bf16[64,2048]{1,0:T(8,128)(2,1)}, u32[]{:S(2)}) copy-start(bf16[64,2048]{1,0:T(8,128)(2,1)} %param.8) | copy-start | bytes 786436
  4.1 28.8 %all-to-all-start = ((f32[64,4,128]{2,1,0:T(4,128)}), f32[64,4,128]{2,1,0:T(4,128)S(1)}, u32[]{:S(2)}, u32[]{:S(2)}) async-start(f32[64,4,128]{2,1,0:T(4,128)} %bitcast.16), calls=%async_computation | async-start | bytes 262144 | tf_op jit(solution)/shard_map/all_to_all | solution.py:95
  32.8 0.7 copy-start.1
  39.3 26.4 %copy-start.4 = (bf16[32,128]{1,0:T(8,128)(2,1)}, bf16[32,128]{1,0:T(8,128)(2,1)S(1)}, u32[]{:S(2)}) copy-start(bf16[32,128]{1,0:T(8,128)(2,1)S(1)} %slice_select_fusion.1.coeffs_ref) | copy-start | bytes 24580
  40.2 21.9 %all-to-all-start.1 = ((bf16[64,32,128]{2,1,0:T(8,128)(2,1)}), bf16[64,32,128]{2,1,0:T(8,128)(2,1)S(1)}, u32[]{:S(2)}, u32[]{:S(2)}) async-start(bf16[64,32,128]{2,1,0:T(8,128)(2,1)} %broadcast_in_dim.2), calls=%async_computation.1 | async-start | bytes 1048576 | tf_op jit(solution)/shard_map/all_to_all | solution.py:95
  62.1 0.8 copy-start

commit v2 on v1

--- a/solution.py
+++ b/solution.py
@@ -66,18 +66,45 @@
         out_ref[8 * part : 8 * (part + 1), :] = (even * expand[:half] + odd * expand[half:]).sum(axis=1)
 
 
-def feed_forward_kernel(coeffs_ref, expand_ref, contract_ref, out_ref):
-    coeffs = coeffs_ref[...]
+def spread_kernel(core_ref, both_ref, coeffs_ref, out_ref):
+    total = both_ref[0] + both_ref[1]
+    half = total.shape[1] // 2
+    mine = jnp.where(core_ref[0] == 0, total[:, :half], total[:, half:])
+    coeffs_ref[...] = mine.astype(BF16)
+    low, high = mine[:16], mine[16:]
+    left = lax.broadcasted_iota(jnp.int32, low.shape, 1) < half // 2
+    first = jnp.where(left, low, pltpu.roll(high, half // 2, 1)).astype(BF16)
+    second = jnp.where(left, pltpu.roll(low, half // 2, 1), high).astype(BF16)
+    pair = jnp.stack([first, second])
+    out_ref[...] = jnp.broadcast_to(pair[None], (out_ref.shape[0] // 2,) + pair.shape).reshape(out_ref.shape)
+
+
+def feed_forward_kernel(coeffs_ref, *refs):
+    weights, out_ref = refs[:-1], refs[-1]
+    units = weights[0].shape[0] // 2
+    packed = coeffs_ref[...]
+    kept = packed.shape[2] // 2
+    width = packed.shape[0] * 32
+    coeffs = jnp.concatenate([packed[:, :, :kept], packed[:, :, kept:]], axis=1).reshape(width, kept)
     wide = coeffs.astype(F32)
-    scale = lax.rsqrt(jnp.sum(wide * wide, axis=0, keepdims=True) / coeffs.shape[0] + 1e-06)
-    expanded = jnp.dot(expand_ref[...], coeffs, preferred_element_type=F32) * scale
-    activated = jax.nn.gelu(expanded).astype(BF16)
-    branch = lax.dot_general(contract_ref[...], activated, (((0,), (0,)), ((), ())), preferred_element_type=F32)
-    out_ref[...] = branch.astype(BF16)
+    scale = lax.rsqrt(jnp.sum(wide * wide, axis=0, keepdims=True) / width + 1e-06)
+    branch = jnp.zeros((width, kept), F32)
+    for ref in weights:
+        expanded = jnp.dot(ref[:units, :], coeffs, preferred_element_type=F32) * scale
+        activated = jax.nn.gelu(expanded).astype(BF16)
+        branch += lax.dot_general(ref[units:, :], activated, (((0,), (0,)), ((), ())), preferred_element_type=F32)
+    parts = branch.reshape(-1, 32, kept)
+    out_ref[...] = jnp.concatenate([parts[:, :16], parts[:, 16:]], axis=2).astype(BF16)
 
 
 def add_kernel(parts_ref, coeffs_ref, out_ref):
-    total = jnp.sum(parts_ref[...].astype(F32), axis=0)
+    sources, rows, lanes = parts_ref.shape
+    sums = jnp.sum(parts_ref[...].astype(F32).reshape(sources // 2, 2, rows, lanes), axis=0)
+    first, second = sums[0], sums[1]
+    left = lax.broadcasted_iota(jnp.int32, first.shape, 1) < lanes // 2
+    low = jnp.where(left, first, pltpu.roll(second, lanes // 2, 1))
+    high = jnp.where(left, pltpu.roll(first, lanes // 2, 1), second)
+    total = jnp.concatenate([low, high], axis=0)
     out_ref[...] = (coeffs_ref[...].astype(F32) + total).astype(BF16)
 
 
@@ -97,8 +124,10 @@
     def gather_pair(x):
         return lax.all_gather(x, "seq", axis_index_groups=pairs)
 
-    units_in = gather_pair(w_expand.T).reshape(-1, width)
-    units_out = gather_pair(w_contract).reshape(-1, width)
+    own = jnp.concatenate([w_expand.T, w_contract], axis=0)
+    beside = lax.ppermute(own, "seq", [(i, i ^ 2) for i in range(windows)])
+    other_core = [(i, i ^ 1) for i in range(windows)]
+    weights = [own, beside, lax.ppermute(own, "seq", other_core), lax.ppermute(beside, "seq", other_core)]
 
     steps = 4
     moments = pl.pallas_call(
@@ -127,18 +156,30 @@
         out_shape=jax.ShapeDtypeStruct((mine, KEEP), F32),
     )(core.astype(jnp.int32).reshape(1), received, jnp.asarray(trig), jnp.asarray(expand))
     both = gather_pair(partial)
-    coeffs = (both[0] + both[1]).astype(BF16)
-    coeffs = jnp.where(core == 0, coeffs[:, : KEEP // 2], coeffs[:, KEEP // 2 :])
-    spread = exchange(jnp.broadcast_to(coeffs[None], (chips,) + coeffs.shape)).reshape(width, -1)
+    coeffs, spread = pl.pallas_call(
+        spread_kernel,
+        grid_spec=pltpu.PrefetchScalarGridSpec(
+            num_scalar_prefetch=1,
+            grid=(1,),
+            in_specs=[pl.BlockSpec(both.shape, lambda i, core: (0, 0, 0))],
+            out_specs=[
+                pl.BlockSpec((mine, KEEP // 2), lambda i, core: (0, 0)),
+                pl.BlockSpec((chips, mine // 2, KEEP // 2), lambda i, core: (0, 0, 0)),
+            ],
+        ),
+        out_shape=[
+            jax.ShapeDtypeStruct((mine, KEEP // 2), BF16),
+            jax.ShapeDtypeStruct((chips, mine // 2, KEEP // 2), BF16),
+        ],
+    )(core.astype(jnp.int32).reshape(1), both)
     branch = pl.pallas_call(
         feed_forward_kernel,
         out_shape=jax.ShapeDtypeStruct(spread.shape, BF16),
-    )(spread, units_in, units_out)
-    parts = exchange(branch.reshape(chips, mine, -1))
+    )(exchange(spread), *weights)
     result = pl.pallas_call(
         add_kernel,
         out_shape=jax.ShapeDtypeStruct(coeffs.shape, BF16),
-    )(parts, coeffs)
+    )(exchange(branch), coeffs)
     halves = gather_pair(result)
     halves = jnp.where(core == 0, halves[:, : mine // 2], halves[:, mine // 2 :])
     return jnp.transpose(halves, (0, 2, 1)).reshape(KEEP, mine // 2)

time: 97.6 us -> 98.8 us (1.012)
  blocking collectives: 37.6 us -> 8.4 us
  starting transfers between devices: 21.9 us -> 37.4 us
  waiting for transfers between devices: 24.2 us -> 34.3 us
  Pallas kernels: 10.5 us -> 13.4 us
  other arithmetic: 0.62 us -> 1.67 us
    all_to_all x1 -> x0, blocking collectives: 23.6 us -> none  [exchange(): return lax.all_to_all(x, 'seq', 0, 0, axis_index_groups=same_core)]
    ppermute x0 -> x3, starting transfers between devices: none -> 12.2 us  [the longest x1 4.83 us: local(): beside = lax.ppermute(own, 'seq', [(i, i ^ 2) for i in range(windows)])]
    all_to_all x2 -> x3, waiting for transfers between devices: 24.2 us -> 34.3 us  [exchange(): return lax.all_to_all(x, 'seq', 0, 0, axis_index_groups=same_core)]
    all_gather x4 -> x2, blocking collectives: 14 us -> 8.4 us  [gather_pair(): return lax.all_gather(x, 'seq', axis_index_groups=pairs)]
    all_to_all x2 -> x3, starting transfers between devices: 21.9 us -> 25.2 us  [exchange(): return lax.all_to_all(x, 'seq', 0, 0, axis_index_groups=same_core)]
    pallas_call x0 -> x1, Pallas kernels: none -> 1.64 us  [local(): pl.pallas_call(spread_kernel, grid_spec=pltpu.PrefetchScalarGridSpec(num_...]
    unnamed x10 -> x14, local copies, waits for them, and re-layouts: 1.45 us -> 2.88 us
    pallas_call x1, Pallas kernels: 2.78 us -> 4.14 us  [local(): pl.pallas_call(feed_forward_kernel, out_shape=jax.ShapeDtypeStruct(spread...]
  transfers between devices with their start and end apart: 2 -> 6, of which waited for: 2 -> 3; matrix products, arithmetic and copies ran while one was open for 0% -> 0% of each run, Pallas kernels for 0% -> 8%
where the time goes in v2:
time: 98.8 us; the launch traced here: 98.2 us
  starting transfers between devices  37.4 us (38%)
  waiting for transfers between devices  34.3 us (35%)
  Pallas kernels  13.4 us (14%)
  blocking collectives  8.4 us (9%)
  local copies, waits for them, and re-layouts  2.88 us (3%)
  other arithmetic  1.67 us (2%)
    all_to_all x3, waiting for transfers between devices, exchange(): return lax.all_to_all(x, 'seq', 0, 0, axis_index_groups=same_core)  34.3 us
    all_to_all x3, starting transfers between devices, exchange(): return lax.all_to_all(x, 'seq', 0, 0, axis_index_groups=same_core)  25.2 us
    all_gather x2, blocking collectives, gather_pair(): return lax.all_gather(x, 'seq', axis_index_groups=pairs)  8.4 us
    ppermute x1, starting transfers between devices, local(): beside = lax.ppermute(own, 'seq', [(i, i ^ 2) for i in range(windows)])  4.83 us
    ppermute x1, starting transfers between devices, local(): lax.ppermute(beside, 'seq', other_core)  4.23 us
    pallas_call x1, Pallas kernels, local(): pl.pallas_call(feed_forward_kernel, out_shape=jax.ShapeDtypeStruct(spread...  4.14 us
    pallas_call x1, Pallas kernels, local(): pl.pallas_call(moments_kernel, grid=(steps,), in_specs=[pl.BlockSpec((2 *...  4.03 us
    ppermute x1, starting transfers between devices, local(): lax.ppermute(own, 'seq', other_core)  3.14 us
  transfers between devices with their start and end apart: 6, of which 3 were waited for; matrix products, arithmetic and copies ran while one was open for 0% of the time, Pallas kernels for 8%

profile of v2, /device:TPU:1, one launch (start us, length us, event | category | flops | bytes accessed | tf_op | source)
XLA Modules:
  0.0 98.2 jit_solution(10165749374758219660)
XLA Ops:
  0.0 1.1 %pad_maximum_fusion.refs_0_ = bf16[128,2048]{1,0:T(8,128)(2,1)S(1)} fusion(bf16[64,2048]{1,0:T(8,128)(2,1)} %param.8, bf16[64,2048]{1,0:T(8,128)(2,1)} %bitcast.15), kind=kLoop, calls=%fused_computation | loop fusion | flops 1048576 | bytes 1048576 | tf_op jit(solution)/shard_map/concatenate | solution.py:127
  1.1 4.8 %collective-permute-start = (bf16[128,2048]{1,0:T(8,128)(2,1)S(1)}, bf16[128,2048]{1,0:T(8,128)(2,1)S(1)}, u32[]{:S(2)}, u32[]{:S(2)}) collective-permute-start(bf16[128,2048]{1,0:T(8,128)(2,1)S(1)} %pad_maximum_fusion.refs_0_), channel_id=1, source_target_pairs={{0,2},{1,3},{2,0},{3,1},{4,6},{5,7},{6,4},{7,5},{8,10},{9,11},{10,... | collective-permute-start | bytes 1572872 | tf_op jit(solution)/shard_map/ppermute | solution.py:128
  5.9 4.0 %shard_map.64 = f32[256,128]{1,0:T(8,128)} custom-call(bf16[32,512]{1,0:T(8,128)(2,1)} %constant.24.clone.project_ref, bf16[512,2048]{1,0:T(8,128)(2,1)} %rows_ref.1), custom_call_target="tpu_custom_call" | custom-call | tf_op jit(solution)/shard_map/pallas_call | solution.py:133
  10.0 15.4 %all-to-all-start = ((f32[64,4,128]{2,1,0:T(4,128)}), f32[64,4,128]{2,1,0:T(4,128)S(1)}, u32[]{:S(2)}, u32[]{:S(2)}) async-start(f32[64,4,128]{2,1,0:T(4,128)} %bitcast.13), calls=%async_computation | async-start | bytes 262144 | tf_op jit(solution)/shard_map/all_to_all | solution.py:122
  25.4 3.1 %collective-permute-start.1 = (bf16[128,2048]{1,0:T(8,128)(2,1)S(1)}, bf16[128,2048]{1,0:T(8,128)(2,1)S(1)}, u32[]{:S(2)}, u32[]{:S(2)}) collective-permute-start(bf16[128,2048]{1,0:T(8,128)(2,1)S(1)} %pad_maximum_fusion.refs_0_), channel_id=1, source_target_pairs={{0,1},{1,0},{2,3},{3,2},{4,5},{5,4},{6,7},{7,6},{8,9},{9,8},{10,11... | collective-permute-start | bytes 1572872 | tf_op jit(solution)/shard_map/ppermute | solution.py:130
  28.5 8.3 %all-to-all-done = f32[64,4,128]{2,1,0:T(4,128)S(1)} async-done(((f32[64,4,128]{2,1,0:T(4,128)}), f32[64,4,128]{2,1,0:T(4,128)S(1)}, u32[]{:S(2)}, u32[]{:S(2)}) %all-to-all-start) | async-done | bytes 131104 | tf_op jit(solution)/shard_map/all_to_all | solution.py:122
  36.9 0.7 copy-done.6
  37.5 1.9 %shard_map.65 = f32[32,256]{1,0:T(8,128)} custom-call(s32[1]{0:T(128)} %bitcast.core_ref, f32[256,128]{1,0:T(8,128)} %bitcast.12, bf16[2,256,512]{2,1,0:T(8,128)(2,1)} %constant.25.clone.trig_ref, f32[16,256]{1,0:T(8,128)} %constant.26.clone.expand_ref), custom_call_target="tpu_custom_call" | custom-call | tf_op jit(solution)/shard_map/pallas_call | solution.py:144
  39.5 0.0 collective-permute-done.refs_1_
  39.5 4.2 %collective-permute-start.2 = (bf16[128,2048]{1,0:T(8,128)(2,1)S(1)}, bf16[128,2048]{1,0:T(8,128)(2,1)S(1)}, u32[]{:S(2)}, u32[]{:S(2)}) collective-permute-start(bf16[128,2048]{1,0:T(8,128)(2,1)S(1)} %collective-permute-done.refs_1_), channel_id=1, source_target_pairs={{0,1},{1,0},{2,3},{3,2},{4,5},{5,4},{6,7},{7,6},{8,9},{9,8},{10,11... | collective-permute-start | bytes 1572872 | tf_op jit(solution)/shard_map/ppermute | solution.py:130
  43.7 3.2 %all-gather = f32[64,256]{1,0:T(8,128)} all-gather(f32[32,256]{1,0:T(8,128)} %shard_map.65), channel_id=2, replica_groups={{0,1},{2,3},{4,5},{6,7},{8,9},{10,11},{12,13},{14,15},{16,17},{18,19},{..., dimensions={0}, use_global_device_ids=true | all-gather | bytes 98304 | tf_op jit(solution)/shard_map/all_gather | solution.py:125
  46.9 1.6 %shard_map.66 = (bf16[32,128]{1,0:T(8,128)(2,1)}, bf16[64,16,128]{2,1,0:T(8,128)(2,1)}) custom-call(s32[1]{0:T(128)} %bitcast.core_ref, f32[2,32,256]{2,1,0:T(8,128)} %bitcast.14), custom_call_target="tpu_custom_call" | custom-call | tf_op jit(solution)/shard_map/pallas_call | solution.py:159
  48.6 4.6 %all-to-all-start.1 = ((bf16[64,16,128]{2,1,0:T(8,128)(2,1)}), bf16[64,16,128]{2,1,0:T(8,128)(2,1)S(1)}, u32[]{:S(2)}, u32[]{:S(2)}) async-start(bf16[64,16,128]{2,1,0:T(8,128)(2,1)} %get-tuple-element.7), calls=%async_computation.1 | async-start | bytes 524288 | tf_op jit(solution)/shard_map/all_to_all | solution.py:122
  53.2 0.0 collective-permute-done.1.refs_2_
  53.2 13.5 %all-to-all-done.1.coeffs_ref = bf16[64,16,128]{2,1,0:T(8,128)(2,1)S(1)} async-done(((bf16[64,16,128]{2,1,0:T(8,128)(2,1)}), bf16[64,16,128]{2,1,0:T(8,128)(2,1)S(1)}, u32[]{:S(2)}, u32[]{:S(2)}) %all-to-all-start.1) | async-done | bytes 262176 | tf_op jit(solution)/shard_map/all_to_all | solution.py:122
  66.7 0.7 copy-done.1
  67.4 0.8 copy-done.5
  68.2 4.1 %shard_map.67 = bf16[64,16,128]{2,1,0:T(8,128)(2,1)} custom-call(bf16[64,16,128]{2,1,0:T(8,128)(2,1)} %copy-done.1, bf16[128,2048]{1,0:T(8,128)(2,1)} %copy-done, bf16[128,2048]{1,0:T(8,128)(2,1)} %copy-done.3, bf16[128,2048]{1,0:T(8,128)(2,1)} %copy-done.4, bf16[128,2048]{1,0:T(8,128)(2,1)} %copy-done.5), custom_call_target="tpu_custom_call" | custom-call | tf_op jit(solution)/shard_map/pallas_call | solution.py:175
  72.4 5.2 %all-to-all-start.2 = ((bf16[64,16,128]{2,1,0:T(8,128)(2,1)}), bf16[64,16,128]{2,1,0:T(8,128)(2,1)S(1)}, u32[]{:S(2)}, u32[]{:S(2)}) async-start(bf16[64,16,128]{2,1,0:T(8,128)(2,1)} %shard_map.67), calls=%async_computation.2 | async-start | bytes 524288 | tf_op jit(solution)/shard_map/all_to_all | solution.py:122
  77.6 12.5 %all-to-all-done.2.parts_ref = bf16[64,16,128]{2,1,0:T(8,128)(2,1)S(1)} async-done(((bf16[64,16,128]{2,1,0:T(8,128)(2,1)}), bf16[64,16,128]{2,1,0:T(8,128)(2,1)S(1)}, u32[]{:S(2)}, u32[]{:S(2)}) %all-to-all-start.2) | async-done | bytes 262176 | tf_op jit(solution)/shard_map/all_to_all | solution.py:122
  90.0 0.7 copy-done.2
  90.7 1.7 %shard_map.68 = bf16[32,128]{1,0:T(8,128)(2,1)} custom-call(bf16[64,16,128]{2,1,0:T(8,128)(2,1)} %copy-done.2, bf16[32,128]{1,0:T(8,128)(2,1)} %get-tuple-element.8.coeffs_ref), custom_call_target="tpu_custom_call" | custom-call | tf_op jit(solution)/shard_map/pallas_call | solution.py:179
  92.4 5.2 %all-gather.1 = bf16[64,128]{1,0:T(8,128)(2,1)S(1)} all-gather(bf16[32,128]{1,0:T(8,128)(2,1)} %shard_map.68), channel_id=3, replica_groups={{0,1},{2,3},{4,5},{6,7},{8,9},{10,11},{12,13},{14,15},{16,17},{18,19},{..., dimensions={0}, use_global_device_ids=true | all-gather | bytes 24576 | tf_op jit(solution)/shard_map/all_gather | solution.py:125
  97.6 0.6 copy_bitcast_fusion
  (11 shorter events, 0.0 us)
Async XLA Ops:
  1.1 65.6 %copy-start = (bf16[128,2048]{1,0:T(8,128)(2,1)}, bf16[128,2048]{1,0:T(8,128)(2,1)S(1)}, u32[]{:S(2)}) copy-start(bf16[128,2048]{1,0:T(8,128)(2,1)S(1)} %pad_maximum_fusion.refs_0_) | copy-start | bytes 1572868
  1.1 38.4 %collective-permute-start = (bf16[128,2048]{1,0:T(8,128)(2,1)S(1)}, bf16[128,2048]{1,0:T(8,128)(2,1)S(1)}, u32[]{:S(2)}, u32[]{:S(2)}) collective-permute-start(bf16[128,2048]{1,0:T(8,128)(2,1)S(1)} %pad_maximum_fusion.refs_0_), channel_id=1, source_target_pairs={{0,2},{1,3},{2,0},{3,1},{4,6},{5,7},{6,4},{7,5},{8,10},{9,11},{10,... | collective-permute-start | bytes 1572872 | tf_op jit(solution)/shard_map/ppermute | solution.py:128
  10.0 26.9 %all-to-all-start = ((f32[64,4,128]{2,1,0:T(4,128)}), f32[64,4,128]{2,1,0:T(4,128)S(1)}, u32[]{:S(2)}, u32[]{:S(2)}) async-start(f32[64,4,128]{2,1,0:T(4,128)} %bitcast.13), calls=%async_computation | async-start | bytes 262144 | tf_op jit(solution)/shard_map/all_to_all | solution.py:122
  25.4 27.8 %collective-permute-start.1 = (bf16[128,2048]{1,0:T(8,128)(2,1)S(1)}, bf16[128,2048]{1,0:T(8,128)(2,1)S(1)}, u32[]{:S(2)}, u32[]{:S(2)}) collective-permute-start(bf16[128,2048]{1,0:T(8,128)(2,1)S(1)} %pad_maximum_fusion.refs_0_), channel_id=1, source_target_pairs={{0,1},{1,0},{2,3},{3,2},{4,5},{5,4},{6,7},{7,6},{8,9},{9,8},{10,11... | collective-permute-start | bytes 1572872 | tf_op jit(solution)/shard_map/ppermute | solution.py:130
  36.9 0.7 copy-start.6
  39.5 27.2 %copy-start.3 = (bf16[128,2048]{1,0:T(8,128)(2,1)}, bf16[128,2048]{1,0:T(8,128)(2,1)S(1)}, u32[]{:S(2)}) copy-start(bf16[128,2048]{1,0:T(8,128)(2,1)S(1)} %collective-permute-done.refs_1_) | copy-start | bytes 1572868
  39.5 27.2 %collective-permute-start.2 = (bf16[128,2048]{1,0:T(8,128)(2,1)S(1)}, bf16[128,2048]{1,0:T(8,128)(2,1)S(1)}, u32[]{:S(2)}, u32[]{:S(2)}) collective-permute-start(bf16[128,2048]{1,0:T(8,128)(2,1)S(1)} %collective-permute-done.refs_1_), channel_id=1, source_target_pairs={{0,1},{1,0},{2,3},{3,2},{4,5},{5,4},{6,7},{7,6},{8,9},{9,8},{10,11... | collective-permute-start | bytes 1572872 | tf_op jit(solution)/shard_map/ppermute | solution.py:130
  48.6 18.1 %all-to-all-start.1 = ((bf16[64,16,128]{2,1,0:T(8,128)(2,1)}), bf16[64,16,128]{2,1,0:T(8,128)(2,1)S(1)}, u32[]{:S(2)}, u32[]{:S(2)}) async-start(bf16[64,16,128]{2,1,0:T(8,128)(2,1)} %get-tuple-element.7), calls=%async_computation.1 | async-start | bytes 524288 | tf_op jit(solution)/shard_map/all_to_all | solution.py:122
  53.2 13.5 %copy-start.4 = (bf16[128,2048]{1,0:T(8,128)(2,1)}, bf16[128,2048]{1,0:T(8,128)(2,1)S(1)}, u32[]{:S(2)}) copy-start(bf16[128,2048]{1,0:T(8,128)(2,1)S(1)} %collective-permute-done.1.refs_2_) | copy-start | bytes 1572868
  66.7 0.7 copy-start.1
  67.4 0.8 copy-start.5
  72.4 17.6 %all-to-all-start.2 = ((bf16[64,16,128]{2,1,0:T(8,128)(2,1)}), bf16[64,16,128]{2,1,0:T(8,128)(2,1)S(1)}, u32[]{:S(2)}, u32[]{:S(2)}) async-start(bf16[64,16,128]{2,1,0:T(8,128)(2,1)} %shard_map.67), calls=%async_computation.2 | async-start | bytes 524288 | tf_op jit(solution)/shard_map/all_to_all | solution.py:122
  90.0 0.7 copy-start.2

commit v3 on v2

--- a/solution.py
+++ b/solution.py
@@ -11,6 +11,9 @@
 KEEP = 256
 MOMENTS = 16
 F32, BF16 = jnp.float32, jnp.bfloat16
+VMEM = pl.BlockSpec(memory_space=pltpu.VMEM)
+SMEM = pl.BlockSpec(memory_space=pltpu.SMEM)
+ANY = pl.BlockSpec(memory_space=pl.ANY)
 
 
 def split_halves(array):
@@ -38,20 +41,29 @@
     return project, expand, np.concatenate([high, low, high, low], axis=1)
 
 
-def moments_kernel(project_ref, rows_ref, out_ref):
+def moments_kernel(project_ref, rows_ref, w_expand_ref, w_contract_ref, out_ref, weights_ref, sems):
+    units = w_expand_ref.shape[0]
+    copies = [
+        pltpu.make_async_copy(w_expand_ref, weights_ref.at[pl.ds(0, units)], sems.at[0]),
+        pltpu.make_async_copy(w_contract_ref, weights_ref.at[pl.ds(units, units)], sems.at[1]),
+    ]
+    for copy in copies:
+        copy.start()
     both = jnp.dot(project_ref[...], rows_ref[...], preferred_element_type=F32)
     moments = both[:MOMENTS] + both[MOMENTS:]
-    copies = jnp.concatenate([moments] * 8, axis=0)
+    spread = jnp.concatenate([moments] * 8, axis=0)
     row = lax.broadcasted_iota(jnp.int32, (128, 128), 0) % 8
     lane = lax.broadcasted_iota(jnp.int32, (128, 128), 1) // MOMENTS
     for block in range(moments.shape[1] // 128):
-        turned = copies[:, 128 * block : 128 * (block + 1)].T
+        turned = spread[:, 128 * block : 128 * (block + 1)].T
         packed = jnp.where(row == lane, turned, 0.0).reshape(16, 8, 128).sum(axis=1)
         out_ref[16 * block : 16 * (block + 1), :] = packed
+    for copy in copies:
+        copy.wait()
 
 
 def coeffs_kernel(core_ref, moments_ref, trig_ref, expand_ref, out_ref):
-    trig = trig_ref[0]
+    trig = trig_ref[core_ref[0]]
     sources = trig.shape[0] // 4
     expand = expand_ref[...]
     half = MOMENTS // 2
@@ -66,7 +78,7 @@
         out_ref[8 * part : 8 * (part + 1), :] = (even * expand[:half] + odd * expand[half:]).sum(axis=1)
 
 
-def spread_kernel(core_ref, both_ref, coeffs_ref, out_ref):
+def spread_kernel(core_ref, both_ref, weights_ref, coeffs_ref, out_ref, same_weights_ref):
     total = both_ref[0] + both_ref[1]
     half = total.shape[1] // 2
     mine = jnp.where(core_ref[0] == 0, total[:, :half], total[:, half:])
@@ -88,13 +100,16 @@
     coeffs = jnp.concatenate([packed[:, :, :kept], packed[:, :, kept:]], axis=1).reshape(width, kept)
     wide = coeffs.astype(F32)
     scale = lax.rsqrt(jnp.sum(wide * wide, axis=0, keepdims=True) / width + 1e-06)
-    branch = jnp.zeros((width, kept), F32)
+    activated = []
     for ref in weights:
         expanded = jnp.dot(ref[:units, :], coeffs, preferred_element_type=F32) * scale
-        activated = jax.nn.gelu(expanded).astype(BF16)
-        branch += lax.dot_general(ref[units:, :], activated, (((0,), (0,)), ((), ())), preferred_element_type=F32)
-    parts = branch.reshape(-1, 32, kept)
-    out_ref[...] = jnp.concatenate([parts[:, :16], parts[:, 16:]], axis=2).astype(BF16)
+        activated.append(jax.nn.gelu(expanded))
+    activated = jnp.concatenate(activated, axis=0).T.astype(BF16)
+    contract = jnp.concatenate([ref[units:, :] for ref in weights], axis=0)
+    branch = jnp.dot(activated, contract, preferred_element_type=F32)
+    for block in range(width // 128):
+        turned = branch[:, 128 * block : 128 * (block + 1)].T.reshape(4, 32, kept)
+        out_ref[4 * block : 4 * (block + 1)] = jnp.concatenate([turned[:, :16], turned[:, 16:]], axis=2).astype(BF16)
 
 
 def add_kernel(parts_ref, coeffs_ref, out_ref):
@@ -124,62 +139,50 @@
     def gather_pair(x):
         return lax.all_gather(x, "seq", axis_index_groups=pairs)
 
-    own = jnp.concatenate([w_expand.T, w_contract], axis=0)
+    def kernel(body, out_shape, in_specs, **rest):
+        out_specs = rest.pop("out_specs", None)
+        if out_specs is None:
+            out_specs = jax.tree.map(lambda _: VMEM, out_shape)
+        params = pltpu.CompilerParams(vmem_limit_bytes=12 << 20)
+        return pl.pallas_call(
+            body, out_shape=out_shape, in_specs=in_specs, out_specs=out_specs, compiler_params=params, **rest
+        )
+
+    core_index = core.astype(jnp.int32).reshape(1)
+    moments, own = kernel(
+        moments_kernel,
+        [
+            jax.ShapeDtypeStruct((width // 8, 128), F32),
+            jax.ShapeDtypeStruct((2 * w_contract.shape[0], width), BF16),
+        ],
+        [VMEM, VMEM, ANY, ANY],
+        out_specs=[VMEM, ANY],
+        scratch_shapes=[pltpu.SemaphoreType.DMA((2,))],
+    )(jnp.asarray(project), hidden_rows, w_expand.T, w_contract)
+    received = exchange(moments.reshape(chips, -1, 128)).reshape(-1, 128)
+    other_core = [(i, i ^ 1) for i in range(windows)]
     beside = lax.ppermute(own, "seq", [(i, i ^ 2) for i in range(windows)])
-    other_core = [(i, i ^ 1) for i in range(windows)]
-    weights = [own, beside, lax.ppermute(own, "seq", other_core), lax.ppermute(beside, "seq", other_core)]
-
-    steps = 4
-    moments = pl.pallas_call(
-        moments_kernel,
-        grid=(steps,),
-        in_specs=[
-            pl.BlockSpec((2 * MOMENTS, rows), lambda i: (0, 0)),
-            pl.BlockSpec((rows, width // steps), lambda i: (0, i)),
-        ],
-        out_specs=pl.BlockSpec((width // 8 // steps, 128), lambda i: (i, 0)),
-        out_shape=jax.ShapeDtypeStruct((width // 8, 128), F32),
-    )(jnp.asarray(project), hidden_rows)
-    received = exchange(moments.reshape(chips, -1, 128)).reshape(-1, 128)
-    partial = pl.pallas_call(
-        coeffs_kernel,
-        grid_spec=pltpu.PrefetchScalarGridSpec(
-            num_scalar_prefetch=1,
-            grid=(1,),
-            in_specs=[
-                pl.BlockSpec(received.shape, lambda i, core: (0, 0)),
-                pl.BlockSpec((1,) + trig.shape[1:], lambda i, core: (core[0], 0, 0)),
-                pl.BlockSpec(expand.shape, lambda i, core: (0, 0)),
-            ],
-            out_specs=pl.BlockSpec((mine, KEEP), lambda i, core: (0, 0)),
-        ),
-        out_shape=jax.ShapeDtypeStruct((mine, KEEP), F32),
-    )(core.astype(jnp.int32).reshape(1), received, jnp.asarray(trig), jnp.asarray(expand))
+    across = lax.ppermute(own, "seq", other_core)
+    partial = kernel(
+        coeffs_kernel, jax.ShapeDtypeStruct((mine, KEEP), F32), [SMEM, VMEM, VMEM, VMEM]
+    )(core_index, received, jnp.asarray(trig), jnp.asarray(expand))
     both = gather_pair(partial)
-    coeffs, spread = pl.pallas_call(
+    coeffs, spread, beside = kernel(
         spread_kernel,
-        grid_spec=pltpu.PrefetchScalarGridSpec(
-            num_scalar_prefetch=1,
-            grid=(1,),
-            in_specs=[pl.BlockSpec(both.shape, lambda i, core: (0, 0, 0))],
-            out_specs=[
-                pl.BlockSpec((mine, KEEP // 2), lambda i, core: (0, 0)),
-                pl.BlockSpec((chips, mine // 2, KEEP // 2), lambda i, core: (0, 0, 0)),
-            ],
-        ),
-        out_shape=[
+        [
             jax.ShapeDtypeStruct((mine, KEEP // 2), BF16),
             jax.ShapeDtypeStruct((chips, mine // 2, KEEP // 2), BF16),
+            jax.ShapeDtypeStruct(beside.shape, BF16),
         ],
-    )(core.astype(jnp.int32).reshape(1), both)
-    branch = pl.pallas_call(
-        feed_forward_kernel,
-        out_shape=jax.ShapeDtypeStruct(spread.shape, BF16),
+        [SMEM, VMEM, ANY],
+        out_specs=[VMEM, VMEM, ANY],
+        input_output_aliases={2: 2},
+    )(core_index, both, beside)
+    weights = [own, beside, across, lax.ppermute(beside, "seq", other_core)]
+    branch = kernel(
+        feed_forward_kernel, jax.ShapeDtypeStruct(spread.shape, BF16), [VMEM] * 5
     )(exchange(spread), *weights)
-    result = pl.pallas_call(
-        add_kernel,
-        out_shape=jax.ShapeDtypeStruct(coeffs.shape, BF16),
-    )(exchange(branch), coeffs)
+    result = kernel(add_kernel, jax.ShapeDtypeStruct(coeffs.shape, BF16), [VMEM, VMEM])(exchange(branch), coeffs)
     halves = gather_pair(result)
     halves = jnp.where(core == 0, halves[:, : mine // 2], halves[:, mine // 2 :])
     return jnp.transpose(halves, (0, 2, 1)).reshape(KEEP, mine // 2)

time: 98.8 us -> 88.7 us (0.90)
  Pallas kernels: 13.4 us -> 4.49 us
  starting transfers between devices: 37.4 us -> 35.4 us
  local copies, waits for them, and re-layouts: 2.88 us -> 4.25 us
  other arithmetic: 1.67 us -> 0.6 us
    pallas_call x5, Pallas kernels: 13.4 us -> 4.49 us  [the longest x1 1.93 us: local(): kernel(feed_forward_kernel, jax.ShapeDtypeStruct(spread.shape, BF16), [VM...]
    ppermute x2, starting transfers between devices: 7.38 us -> 5.39 us  [the longest x1 3.15 us: local(): across = lax.ppermute(own, 'seq', other_core)]
    unnamed x14 -> x12, local copies, waits for them, and re-layouts: 2.88 us -> 4.25 us
    concatenate x1 -> x0, other arithmetic: 1.07 us -> none  [local(): own = jnp.concatenate([w_expand.T, w_contract], axis=0)]
  transfers between devices with their start and end apart: 6 -> 6, of which waited for: 3 -> 3; matrix products, arithmetic and copies ran while one was open for 0% -> 0% of each run, Pallas kernels for 8% -> 1%
where the time goes in v3:
time: 88.7 us; the launch traced here: 88.1 us
  starting transfers between devices  35.4 us (40%)
  waiting for transfers between devices  34.4 us (39%)
  blocking collectives  8.88 us (10%)
  Pallas kernels  4.49 us (5%)
  local copies, waits for them, and re-layouts  4.25 us (5%)
    all_to_all x3, waiting for transfers between devices, exchange(): return lax.all_to_all(x, 'seq', 0, 0, axis_index_groups=same_core)  34.4 us
    all_to_all x3, starting transfers between devices, exchange(): return lax.all_to_all(x, 'seq', 0, 0, axis_index_groups=same_core)  25.2 us
    all_gather x2, blocking collectives, gather_pair(): return lax.all_gather(x, 'seq', axis_index_groups=pairs)  8.88 us
    ppermute x1, starting transfers between devices, local(): beside = lax.ppermute(own, 'seq', [(i, i ^ 2) for i in range(windows)])  4.83 us
    unnamed x12, local copies, waits for them, and re-layouts  4.25 us
    ppermute x1, starting transfers between devices, local(): across = lax.ppermute(own, 'seq', other_core)  3.15 us
    ppermute x1, starting transfers between devices, local(): weights = [own, beside, across, lax.ppermute(beside, 'seq', other_core)]  2.24 us
    pallas_call x1, Pallas kernels, local(): kernel(feed_forward_kernel, jax.ShapeDtypeStruct(spread.shape, BF16), [VM...  1.93 us
  transfers between devices with their start and end apart: 6, of which 3 were waited for; matrix products, arithmetic and copies ran while one was open for 0% of the time, Pallas kernels for 1%

profile of v3, /device:TPU:1, one launch (start us, length us, event | category | flops | bytes accessed | tf_op | source)
XLA Modules:
  0.0 88.1 jit_solution(15921102534989964867)
XLA Ops:
  0.0 1.6 %copy-done = bf16[512,2048]{1,0:T(8,128)(2,1)S(1)} copy-done((bf16[512,2048]{1,0:T(8,128)(2,1)S(1)}, bf16[512,2048]{1,0:T(8,128)(2,1)}, u32[]{:S(2)}) %copy-start) | copy-done | bytes 2097176
  1.6 0.9 %copy-done.2 = bf16[2048,64]{0,1:T(8,128)(2,1)S(1)} copy-done((bf16[2048,64]{0,1:T(8,128)(2,1)S(1)}, bf16[2048,64]{0,1:T(8,128)(2,1)}, u32[]{:S(2)}) %copy-start.2) | copy-done | bytes 262168
  2.5 0.9 %copy-done.3 = bf16[64,2048]{1,0:T(8,128)(2,1)S(1)} copy-done((bf16[64,2048]{1,0:T(8,128)(2,1)S(1)}, bf16[64,2048]{1,0:T(8,128)(2,1)}, u32[]{:S(2)}) %copy-start.3) | copy-done | bytes 262168
  3.5 0.8 copy-done.4
  4.3 1.3 %shard_map.64 = (f32[256,128]{1,0:T(8,128)}, bf16[128,2048]{1,0:T(8,128)(2,1)S(1)}) custom-call(bf16[32,512]{1,0:T(8,128)(2,1)S(1)} %copy-done.4, bf16[512,2048]{1,0:T(8,128)(2,1)S(1)} %copy-done, bf16[64,2048]{1,0:T(8,128)(2,1)S(1)} %bitcast.14, bf16[64,2048]{1,0:T(8,128)(2,1)S(1)} %copy-done.3), custom_call_target="tpu_custom_call" | custom-call | tf_op jit(solution)/shard_map/pallas_call | solution.py:152
  5.6 4.8 %collective-permute-start = (bf16[128,2048]{1,0:T(8,128)(2,1)S(1)}, bf16[128,2048]{1,0:T(8,128)(2,1)S(1)}, u32[]{:S(2)}, u32[]{:S(2)}) collective-permute-start(bf16[128,2048]{1,0:T(8,128)(2,1)S(1)} %get-tuple-element.11.refs_0_), channel_id=1, source_target_pairs={{0,2},{1,3},{2,0},{3,1},{4,6},{5,7},{6,4},{7,5},{8,10},{9,11},{10,... | collective-permute-start | bytes 1572872 | tf_op jit(solution)/shard_map/ppermute | solution.py:164
  10.4 15.4 %all-to-all-start = ((f32[64,4,128]{2,1,0:T(4,128)}), f32[64,4,128]{2,1,0:T(4,128)S(1)}, u32[]{:S(2)}, u32[]{:S(2)}) async-start(f32[64,4,128]{2,1,0:T(4,128)} %bitcast.2), calls=%async_computation | async-start | bytes 262144 | tf_op jit(solution)/shard_map/all_to_all | solution.py:137
  25.8 3.1 %collective-permute-start.1 = (bf16[128,2048]{1,0:T(8,128)(2,1)S(1)}, bf16[128,2048]{1,0:T(8,128)(2,1)S(1)}, u32[]{:S(2)}, u32[]{:S(2)}) collective-permute-start(bf16[128,2048]{1,0:T(8,128)(2,1)S(1)} %get-tuple-element.11.refs_0_), channel_id=1, source_target_pairs={{0,1},{1,0},{2,3},{3,2},{4,5},{5,4},{6,7},{7,6},{8,9},{9,8},{10,11... | collective-permute-start | bytes 1572872 | tf_op jit(solution)/shard_map/ppermute | solution.py:165
  29.0 8.3 %all-to-all-done = f32[64,4,128]{2,1,0:T(4,128)S(1)} async-done(((f32[64,4,128]{2,1,0:T(4,128)}), f32[64,4,128]{2,1,0:T(4,128)S(1)}, u32[]{:S(2)}, u32[]{:S(2)}) %all-to-all-start) | async-done | bytes 131104 | tf_op jit(solution)/shard_map/all_to_all | solution.py:137
  37.4 0.3 shard_map.65
  37.7 3.8 %all-gather = f32[64,256]{1,0:T(8,128)S(1)} all-gather(f32[32,256]{1,0:T(8,128)S(1)} %shard_map.65), channel_id=2, replica_groups={{0,1},{2,3},{4,5},{6,7},{8,9},{10,11},{12,13},{14,15},{16,17},{18,19},{..., dimensions={0}, use_global_device_ids=true | all-gather | bytes 98304 | tf_op jit(solution)/shard_map/all_gather | solution.py:140
  41.5 0.0 collective-permute-done.weights_ref
  41.6 0.8 shard_map.66
  42.3 2.2 %collective-permute-start.2 = (bf16[128,2048]{1,0:T(8,128)(2,1)S(1)}, bf16[128,2048]{1,0:T(8,128)(2,1)S(1)}, u32[]{:S(2)}, u32[]{:S(2)}) collective-permute-start(bf16[128,2048]{1,0:T(8,128)(2,1)S(1)} %get-tuple-element.13.refs_1_), channel_id=1, source_target_pairs={{0,1},{1,0},{2,3},{3,2},{4,5},{5,4},{6,7},{7,6},{8,9},{9,8},{10,11... | collective-permute-start | bytes 1572872 | tf_op jit(solution)/shard_map/ppermute | solution.py:181
  44.6 4.6 %all-to-all-start.1 = ((bf16[64,16,128]{2,1,0:T(8,128)(2,1)}), bf16[64,16,128]{2,1,0:T(8,128)(2,1)S(1)}, u32[]{:S(2)}, u32[]{:S(2)}) async-start(bf16[64,16,128]{2,1,0:T(8,128)(2,1)} %get-tuple-element.12), calls=%async_computation.1 | async-start | bytes 524288 | tf_op jit(solution)/shard_map/all_to_all | solution.py:137
  49.2 0.0 collective-permute-done.1.refs_2_
  49.2 13.6 %all-to-all-done.1.coeffs_ref = bf16[64,16,128]{2,1,0:T(8,128)(2,1)S(1)} async-done(((bf16[64,16,128]{2,1,0:T(8,128)(2,1)}), bf16[64,16,128]{2,1,0:T(8,128)(2,1)S(1)}, u32[]{:S(2)}, u32[]{:S(2)}) %all-to-all-start.1) | async-done | bytes 262176 | tf_op jit(solution)/shard_map/all_to_all | solution.py:137
  62.8 0.0 collective-permute-done.2.refs_3_
  62.9 1.9 %shard_map.67 = bf16[64,16,128]{2,1,0:T(8,128)(2,1)} custom-call(bf16[64,16,128]{2,1,0:T(8,128)(2,1)S(1)} %all-to-all-done.1.coeffs_ref, bf16[128,2048]{1,0:T(8,128)(2,1)S(1)} %get-tuple-element.11.refs_0_, bf16[128,2048]{1,0:T(8,128)(2,1)S(1)} %get-tuple-element.13.refs_1_, bf16[128,2048]{1,0:T(8,128)(2,1)S(1)} %collective-permute-done.1.refs_2_, ...), custom_call_target="tpu_custom_call" | custom-call | tf_op jit(solution)/shard_map/pallas_call | solution.py:182
  64.8 5.2 %all-to-all-start.2 = ((bf16[64,16,128]{2,1,0:T(8,128)(2,1)}), bf16[64,16,128]{2,1,0:T(8,128)(2,1)S(1)}, u32[]{:S(2)}, u32[]{:S(2)}) async-start(bf16[64,16,128]{2,1,0:T(8,128)(2,1)} %shard_map.67), calls=%async_computation.2 | async-start | bytes 524288 | tf_op jit(solution)/shard_map/all_to_all | solution.py:137
  69.9 12.4 %all-to-all-done.2.parts_ref = bf16[64,16,128]{2,1,0:T(8,128)(2,1)S(1)} async-done(((bf16[64,16,128]{2,1,0:T(8,128)(2,1)}), bf16[64,16,128]{2,1,0:T(8,128)(2,1)S(1)}, u32[]{:S(2)}, u32[]{:S(2)}) %all-to-all-start.2) | async-done | bytes 262176 | tf_op jit(solution)/shard_map/all_to_all | solution.py:137
  82.4 0.1 shard_map.68
  82.5 5.0 %all-gather.1 = bf16[64,128]{1,0:T(8,128)(2,1)S(1)} all-gather(bf16[32,128]{1,0:T(8,128)(2,1)S(1)} %shard_map.68), channel_id=3, replica_groups={{0,1},{2,3},{4,5},{6,7},{8,9},{10,11},{12,13},{14,15},{16,17},{18,19},{..., dimensions={0}, use_global_device_ids=true | all-gather | bytes 24576 | tf_op jit(solution)/shard_map/all_gather | solution.py:140
  87.5 0.6 copy_bitcast_fusion
  (8 shorter events, 0.0 us)
Async XLA Ops:
  0.0 1.6 %copy-start = (bf16[512,2048]{1,0:T(8,128)(2,1)S(1)}, bf16[512,2048]{1,0:T(8,128)(2,1)}, u32[]{:S(2)}) copy-start(bf16[512,2048]{1,0:T(8,128)(2,1)} %rows_ref.1) | copy-start | bytes 6291460
  1.6 0.9 %copy-start.2 = (bf16[2048,64]{0,1:T(8,128)(2,1)S(1)}, bf16[2048,64]{0,1:T(8,128)(2,1)}, u32[]{:S(2)}) copy-start(bf16[2048,64]{0,1:T(8,128)(2,1)} %param.7) | copy-start | bytes 786436
  2.5 0.9 %copy-start.3 = (bf16[64,2048]{1,0:T(8,128)(2,1)S(1)}, bf16[64,2048]{1,0:T(8,128)(2,1)}, u32[]{:S(2)}) copy-start(bf16[64,2048]{1,0:T(8,128)(2,1)} %w_contract_ref.1) | copy-start | bytes 786436
  3.5 0.8 copy-start.4
  4.3 33.1 %copy-start.1 = (bf16[2,256,512]{2,1,0:T(8,128)(2,1)S(1)}, bf16[2,256,512]{2,1,0:T(8,128)(2,1)}, u32[]{:S(2)}) copy-start(bf16[2,256,512]{2,1,0:T(8,128)(2,1)} %constant.25.clone.trig_ref) | copy-start | bytes 1572868
  4.3 33.1 %copy-start.5 = (f32[16,256]{1,0:T(8,128)S(1)}, f32[16,256]{1,0:T(8,128)}, u32[]{:S(2)}) copy-start(f32[16,256]{1,0:T(8,128)} %constant.26.clone.expand_ref) | copy-start | bytes 49156
  5.6 36.0 %collective-permute-start = (bf16[128,2048]{1,0:T(8,128)(2,1)S(1)}, bf16[128,2048]{1,0:T(8,128)(2,1)S(1)}, u32[]{:S(2)}, u32[]{:S(2)}) collective-permute-start(bf16[128,2048]{1,0:T(8,128)(2,1)S(1)} %get-tuple-element.11.refs_0_), channel_id=1, source_target_pairs={{0,2},{1,3},{2,0},{3,1},{4,6},{5,7},{6,4},{7,5},{8,10},{9,11},{10,... | collective-permute-start | bytes 1572872 | tf_op jit(solution)/shard_map/ppermute | solution.py:164
  10.4 26.9 %all-to-all-start = ((f32[64,4,128]{2,1,0:T(4,128)}), f32[64,4,128]{2,1,0:T(4,128)S(1)}, u32[]{:S(2)}, u32[]{:S(2)}) async-start(f32[64,4,128]{2,1,0:T(4,128)} %bitcast.2), calls=%async_computation | async-start | bytes 262144 | tf_op jit(solution)/shard_map/all_to_all | solution.py:137
  25.8 23.4 %collective-permute-start.1 = (bf16[128,2048]{1,0:T(8,128)(2,1)S(1)}, bf16[128,2048]{1,0:T(8,128)(2,1)S(1)}, u32[]{:S(2)}, u32[]{:S(2)}) collective-permute-start(bf16[128,2048]{1,0:T(8,128)(2,1)S(1)} %get-tuple-element.11.refs_0_), channel_id=1, source_target_pairs={{0,1},{1,0},{2,3},{3,2},{4,5},{5,4},{6,7},{7,6},{8,9},{9,8},{10,11... | collective-permute-start | bytes 1572872 | tf_op jit(solution)/shard_map/ppermute | solution.py:165
  42.3 20.5 %collective-permute-start.2 = (bf16[128,2048]{1,0:T(8,128)(2,1)S(1)}, bf16[128,2048]{1,0:T(8,128)(2,1)S(1)}, u32[]{:S(2)}, u32[]{:S(2)}) collective-permute-start(bf16[128,2048]{1,0:T(8,128)(2,1)S(1)} %get-tuple-element.13.refs_1_), channel_id=1, source_target_pairs={{0,1},{1,0},{2,3},{3,2},{4,5},{5,4},{6,7},{7,6},{8,9},{9,8},{10,11... | collective-permute-start | bytes 1572872 | tf_op jit(solution)/shard_map/ppermute | solution.py:181
  44.6 18.3 %all-to-all-start.1 = ((bf16[64,16,128]{2,1,0:T(8,128)(2,1)}), bf16[64,16,128]{2,1,0:T(8,128)(2,1)S(1)}, u32[]{:S(2)}, u32[]{:S(2)}) async-start(bf16[64,16,128]{2,1,0:T(8,128)(2,1)} %get-tuple-element.12), calls=%async_computation.1 | async-start | bytes 524288 | tf_op jit(solution)/shard_map/all_to_all | solution.py:137
  64.8 17.6 %all-to-all-start.2 = ((bf16[64,16,128]{2,1,0:T(8,128)(2,1)}), bf16[64,16,128]{2,1,0:T(8,128)(2,1)S(1)}, u32[]{:S(2)}, u32[]{:S(2)}) async-start(bf16[64,16,128]{2,1,0:T(8,128)(2,1)} %shard_map.67), calls=%async_computation.2 | async-start | bytes 524288 | tf_op jit(solution)/shard_map/all_to_all | solution.py:137

commit v4 on v3

v4 whole, which is shorter than its diff:
```python
import math

import jax
import jax.numpy as jnp
import numpy as np
from jax import lax
from jax.experimental import pallas as pl
from jax.experimental.pallas import tpu as pltpu
from jax.sharding import PartitionSpec as P

KEEP = 256
MOMENTS = 16
F32, BF16 = jnp.float32, jnp.bfloat16
VMEM = pl.BlockSpec(memory_space=pltpu.VMEM)
SMEM = pl.BlockSpec(memory_space=pltpu.SMEM)
ANY = pl.BlockSpec(memory_space=pl.ANY)


def split_halves(array):
    high = np.asarray(array, np.float32).astype(jnp.bfloat16)
    low = (np.asarray(array, np.float64) - high.astype(np.float64)).astype(jnp.bfloat16)
    return high, low


def window_tables(rows, windows):
    t = (2.0 * np.arange(rows) + 1.0 - rows) / rows
    basis, _ = np.linalg.qr(np.polynomial.chebyshev.chebvander(t, MOMENTS - 1))
    basis = basis[:, list(range(0, MOMENTS, 2)) + list(range(1, MOMENTS, 2))]
    k = np.arange(KEEP)
    inner = np.pi * np.outer(k, t) / (2 * windows)
    norm = math.sqrt(2.0 / (rows * windows))
    even = norm * np.cos(inner) @ basis[:, : MOMENTS // 2]
    odd = -norm * np.sin(inner) @ basis[:, MOMENTS // 2 :]
    expand = np.concatenate([even, odd], axis=1).T.astype(np.float32)
    high, low = split_halves(basis.T)
    project = np.concatenate([high, low], axis=0)
    theta = np.pi * np.outer(2 * np.arange(windows) + 1, k) / (2 * windows)
    trig = np.concatenate([np.cos(theta), np.sin(theta)], axis=1)
    trig = trig.reshape(windows // 2, 2, 2 * KEEP).transpose(1, 0, 2)
    high, low = split_halves(trig)
    return project, expand, np.concatenate([high, low, high, low], axis=1)


def moments_kernel(project_hbm, rows_hbm, out_ref, project_ref, held, loaded):
    steps, _, columns = held.shape
    first = pltpu.make_async_copy(project_hbm, project_ref, loaded.at[steps])
    loads = [
        pltpu.make_async_copy(rows_hbm.at[:, pl.ds(step * columns, columns)], held.at[step], loaded.at[step])
        for step in range(steps)
    ]
    for copy in [first] + loads:
        copy.start()
    row = lax.broadcasted_iota(jnp.int32, (128, 128), 0) % 8
    lane = lax.broadcasted_iota(jnp.int32, (128, 128), 1) // MOMENTS
    first.wait()
    project = project_ref[...]
    for step in range(steps):
        loads[step].wait()
        both = jnp.dot(project, held[step], preferred_element_type=F32)
        moments = both[:MOMENTS] + both[MOMENTS:]
        spread = jnp.concatenate([moments] * 8, axis=0)
        for block in range(columns // 128):
            turned = spread[:, 128 * block : 128 * (block + 1)].T
            packed = jnp.where(row == lane, turned, 0.0).reshape(16, 8, 128).sum(axis=1)
            top = step * columns // 8 + 16 * block
            out_ref[top : top + 16, :] = packed


def coeffs_kernel(core_ref, moments_ref, trig_ref, expand_ref, out_ref):
    trig = trig_ref[core_ref[0]]
    sources = trig.shape[0] // 4
    expand = expand_ref[...]
    half = MOMENTS // 2
    for part in range(4):
        rows = moments_ref[pl.ds(part, sources, stride=4), :]
        high = rows.astype(BF16)
        low = (rows - high.astype(F32)).astype(BF16)
        stacked = jnp.concatenate([high, high, low, low], axis=0)
        turned = lax.dot_general(stacked, trig, (((0,), (0,)), ((), ())), preferred_element_type=F32)
        even = turned[:, :KEEP].reshape(8, MOMENTS, KEEP)[:, :half]
        odd = turned[:, KEEP:].reshape(8, MOMENTS, KEEP)[:, half:]
        out_ref[8 * part : 8 * (part + 1), :] = (even * expand[:half] + odd * expand[half:]).sum(axis=1)


def spread_kernel(core_ref, both_ref, coeffs_ref, out_ref):
    total = both_ref[0] + both_ref[1]
    half = total.shape[1] // 2
    mine = jnp.where(core_ref[0] == 0, total[:, :half], total[:, half:])
    coeffs_ref[...] = jnp.where(core_ref[0] == 0, total[:16], total[16:]).astype(BF16)
    low, high = mine[:16], mine[16:]
    left = lax.broadcasted_iota(jnp.int32, low.shape, 1) < half // 2
    first = jnp.where(left, low, pltpu.roll(high, half // 2, 1)).astype(BF16)
    second = jnp.where(left, pltpu.roll(low, half // 2, 1), high).astype(BF16)
    pair = jnp.stack([first, second])
    out_ref[...] = jnp.broadcast_to(pair[None], (out_ref.shape[0] // 2,) + pair.shape).reshape(out_ref.shape)


def feed_forward_kernel(coeffs_ref, *refs):
    weights, out_ref = refs[:-1], refs[-1]
    packed = coeffs_ref[...]
    kept = packed.shape[2] // 2
    width = packed.shape[0] * 32
    coeffs = jnp.concatenate([packed[:, :, :kept], packed[:, :, kept:]], axis=1).reshape(width, kept)
    wide = coeffs.astype(F32)
    scale = lax.rsqrt(jnp.sum(wide * wide, axis=0, keepdims=True) / width + 1e-06)
    branch = jnp.zeros((kept, width), F32)
    for expand_ref, contract_ref in zip(weights[::2], weights[1::2]):
        expanded = jnp.dot(expand_ref[...], coeffs, preferred_element_type=F32) * scale
        activated = jax.nn.gelu(expanded).T.astype(BF16)
        branch += jnp.dot(activated, contract_ref[...], preferred_element_type=F32)
    for block in range(width // 128):
        turned = branch[:, 128 * block : 128 * (block + 1)].T.reshape(8, 16, kept)
        out_ref[8 * block : 8 * (block + 1)] = jnp.concatenate([turned[:, :8], turned[:, 8:]], axis=2).astype(BF16)


def add_kernel(parts_ref, coeffs_ref, out_ref):
    sources, rows, lanes = parts_ref.shape
    sums = jnp.sum(parts_ref[...].astype(F32).reshape(sources // 4, 4, rows, lanes), axis=0)
    left = lax.broadcasted_iota(jnp.int32, (rows, lanes), 1) < lanes // 2
    for core in range(2):
        first, second = sums[core], sums[2 + core]
        low = jnp.where(left, first, pltpu.roll(second, lanes // 2, 1))
        high = jnp.where(left, pltpu.roll(first, lanes // 2, 1), second)
        total = jnp.concatenate([low, high], axis=0)
        columns = pl.ds(lanes * core, lanes)
        out_ref[:, columns] = (coeffs_ref[:, columns].astype(F32) + total).astype(BF16)


def local(hidden_rows, w_expand, w_contract):
    rows, width = hidden_rows.shape
    windows = lax.axis_size("seq")
    chips = windows // 2
    mine = width // chips
    project, expand, trig = window_tables(rows, windows)
    same_core = [list(range(core, windows, 2)) for core in range(2)]
    pairs = [[2 * chip, 2 * chip + 1] for chip in range(chips)]
    core = lax.axis_index("seq") % 2

    def exchange(x):
        return lax.all_to_all(x, "seq", 0, 0, axis_index_groups=same_core)

    def gather_pair(x):
        return lax.all_gather(x, "seq", axis_index_groups=pairs)

    def kernel(body, out_shape, in_specs, vmem=12, **rest):
        out_specs = rest.pop("out_specs", None)
        if out_specs is None:
            out_specs = jax.tree.map(lambda _: VMEM, out_shape)
        params = pltpu.CompilerParams(vmem_limit_bytes=vmem << 20)
        return pl.pallas_call(
            body, out_shape=out_shape, in_specs=in_specs, out_specs=out_specs, compiler_params=params, **rest
        )

    core_index = core.astype(jnp.int32).reshape(1)
    moments = kernel(
        moments_kernel,
        jax.ShapeDtypeStruct((width // 8, 128), F32),
        [ANY, ANY],
        vmem=60,
        scratch_shapes=[
            pltpu.VMEM(project.shape, BF16),
            pltpu.VMEM((2, rows, width // 2), BF16),
            pltpu.SemaphoreType.DMA((3,)),
        ],
    )(jnp.asarray(project), hidden_rows)
    received = exchange(moments.reshape(chips, -1, 128)).reshape(-1, 128)
    beside = [(i, i ^ 2) for i in range(windows)]
    w_expand = w_expand.T
    weights = [w_expand, w_contract, lax.ppermute(w_expand, "seq", beside), lax.ppermute(w_contract, "seq", beside)]
    weights = [gather_pair(x).reshape(-1, width) for x in weights]
    partial = kernel(
        coeffs_kernel, jax.ShapeDtypeStruct((mine, KEEP), F32), [SMEM, VMEM, VMEM, VMEM]
    )(core_index, received, jnp.asarray(trig), jnp.asarray(expand))
    both = gather_pair(partial)
    coeffs, spread = kernel(
        spread_kernel,
        [
            jax.ShapeDtypeStruct((mine // 2, KEEP), BF16),
            jax.ShapeDtypeStruct((chips, mine // 2, KEEP // 2), BF16),
        ],
        [SMEM, VMEM],
    )(core_index, both)
    branch = kernel(
        feed_forward_kernel, jax.ShapeDtypeStruct((windows, mine // 4, KEEP // 2), BF16), [VMEM] * 5
    )(exchange(spread), *weights)
    parts = lax.all_to_all(branch, "seq", 0, 0)
    return kernel(add_kernel, jax.ShapeDtypeStruct(coeffs.shape, BF16), [VMEM, VMEM])(parts, coeffs).T


def solution(mesh):
    return jax.shard_map(
        local,
        mesh=mesh,
        in_specs=(P(("doc", "seq"), None), P(None, "seq"), P("seq", None)),
        out_specs=P("doc", "seq"),
        check_vma=False,
    )
```

time: 88.7 us -> 81 us (0.913)
  blocking collectives: 8.88 us -> 36.1 us
  waiting for transfers between devices: 34.4 us -> 10.3 us
  starting transfers between devices: 35.4 us -> 27.9 us
  local copies, waits for them, and re-layouts: 4.25 us -> 0.02 us
  Pallas kernels: 4.49 us -> 5.94 us
    all_to_all x3 -> x2, waiting for transfers between devices: 34.4 us -> 10.3 us  [exchange(): return lax.all_to_all(x, 'seq', 0, 0, axis_index_groups=same_core)]
    all_to_all x0 -> x1, blocking collectives: none -> 23.4 us  [local(): parts = lax.all_to_all(branch, 'seq', 0, 0)]
    ppermute x3 -> x2, starting transfers between devices: 10.2 us -> 5.28 us  [the longest x1 2.92 us: local(): lax.ppermute(w_expand, 'seq', beside)]
    unnamed x12 -> x8, local copies, waits for them, and re-layouts: 4.25 us -> 0.02 us
    all_gather x2 -> x5, blocking collectives: 8.88 us -> 12.7 us  [gather_pair(): return lax.all_gather(x, 'seq', axis_index_groups=pairs)]
    all_to_all x3 -> x2, starting transfers between devices: 25.2 us -> 22.7 us  [exchange(): return lax.all_to_all(x, 'seq', 0, 0, axis_index_groups=same_core)]
  transfers between devices with their start and end apart: 6 -> 4, of which waited for: 3 -> 2; matrix products, arithmetic and copies ran while one was open for 0% -> 0% of each run, Pallas kernels for 1% -> 1%
where the time goes in v4:
time: 81 us; the launch traced here: 80.4 us
  blocking collectives  36.1 us (45%)
  starting transfers between devices  27.9 us (34%)
  waiting for transfers between devices  10.3 us (13%)
  Pallas kernels  5.94 us (7%)
    all_to_all x1, blocking collectives, local(): parts = lax.all_to_all(branch, 'seq', 0, 0)  23.4 us
    all_to_all x2, starting transfers between devices, exchange(): return lax.all_to_all(x, 'seq', 0, 0, axis_index_groups=same_core)  22.7 us
    all_gather x5, blocking collectives, gather_pair(): return lax.all_gather(x, 'seq', axis_index_groups=pairs)  12.7 us
    all_to_all x2, waiting for transfers between devices, exchange(): return lax.all_to_all(x, 'seq', 0, 0, axis_index_groups=same_core)  10.3 us
    ppermute x1, starting transfers between devices, local(): lax.ppermute(w_expand, 'seq', beside)  2.92 us
    pallas_call x1, Pallas kernels, local(): kernel(moments_kernel, jax.ShapeDtypeStruct((width // 8, 128), F32), [ANY...  2.86 us
    ppermute x1, starting transfers between devices, local(): lax.ppermute(w_contract, 'seq', beside)  2.36 us
  transfers between devices with their start and end apart: 4, of which 2 were waited for; matrix products, arithmetic and copies ran while one was open for 0% of the time, Pallas kernels for 1%

profile of v4, /device:TPU:1, one launch (start us, length us, event | category | flops | bytes accessed | tf_op | source)
XLA Modules:
  0.0 80.4 jit_solution(16056824586619335201)
XLA Ops:
  0.0 0.0 copy-start.3
  0.0 2.9 %shard_map.64 = f32[256,128]{1,0:T(8,128)} custom-call(bf16[32,512]{1,0:T(8,128)(2,1)} %constant.23.clone.project_hbm, bf16[512,2048]{1,0:T(8,128)(2,1)} %rows_hbm.1), custom_call_target="tpu_custom_call" | custom-call | tf_op jit(solution)/shard_map/pallas_call | solution.py:155
  2.9 17.1 %all-to-all-start = ((f32[64,4,128]{2,1,0:T(4,128)}), f32[64,4,128]{2,1,0:T(4,128)S(1)}, u32[]{:S(2)}, u32[]{:S(2)}) async-start(f32[64,4,128]{2,1,0:T(4,128)} %bitcast.8), calls=%async_computation | async-start | bytes 262144 | tf_op jit(solution)/shard_map/all_to_all | solution.py:140
  20.0 0.0 copy-done.2
  20.1 2.9 %collective-permute-start = (bf16[64,2048]{1,0:T(8,128)(2,1)S(1)}, bf16[64,2048]{1,0:T(8,128)(2,1)S(1)}, u32[]{:S(2)}, u32[]{:S(2)}) collective-permute-start(bf16[64,2048]{1,0:T(8,128)(2,1)S(1)} %bitcast.9), channel_id=1, source_target_pairs={{0,2},{1,3},{2,0},{3,1},{4,6},{5,7},{6,4},{7,5},{8,10},{9,11},{10,... | collective-permute-start | bytes 786440 | tf_op jit(solution)/shard_map/ppermute | solution.py:169
  23.0 0.0 copy-done.3
  23.0 2.4 %collective-permute-start.1 = (bf16[64,2048]{1,0:T(8,128)(2,1)S(1)}, bf16[64,2048]{1,0:T(8,128)(2,1)S(1)}, u32[]{:S(2)}, u32[]{:S(2)}) collective-permute-start(bf16[64,2048]{1,0:T(8,128)(2,1)S(1)} %copy-done.3), channel_id=1, source_target_pairs={{0,2},{1,3},{2,0},{3,1},{4,6},{5,7},{6,4},{7,5},{8,10},{9,11},{10,... | collective-permute-start | bytes 786440 | tf_op jit(solution)/shard_map/ppermute | solution.py:169
  25.4 6.2 %all-to-all-done = f32[64,4,128]{2,1,0:T(4,128)S(1)} async-done(((f32[64,4,128]{2,1,0:T(4,128)}), f32[64,4,128]{2,1,0:T(4,128)S(1)}, u32[]{:S(2)}, u32[]{:S(2)}) %all-to-all-start) | async-done | bytes 131104 | tf_op jit(solution)/shard_map/all_to_all | solution.py:140
  31.6 0.0 copy-done.1
  31.6 0.0 copy-done
  31.6 0.3 shard_map.65
  31.9 3.8 %all-gather = f32[64,256]{1,0:T(8,128)S(1)} all-gather(f32[32,256]{1,0:T(8,128)S(1)} %shard_map.65), channel_id=2, replica_groups={{0,1},{2,3},{4,5},{6,7},{8,9},{10,11},{12,13},{14,15},{16,17},{18,19},{..., dimensions={0}, use_global_device_ids=true | all-gather | bytes 98304 | tf_op jit(solution)/shard_map/all_gather | solution.py:143
  35.7 0.8 shard_map.66
  36.5 5.5 %all-to-all-start.1 = ((bf16[64,16,128]{2,1,0:T(8,128)(2,1)}), bf16[64,16,128]{2,1,0:T(8,128)(2,1)S(1)}, u32[]{:S(2)}, u32[]{:S(2)}) async-start(bf16[64,16,128]{2,1,0:T(8,128)(2,1)} %get-tuple-element.7), calls=%async_computation.1 | async-start | bytes 524288 | tf_op jit(solution)/shard_map/all_to_all | solution.py:140
  42.0 2.4 %all-gather.1.refs_0_ = bf16[128,2048]{1,0:T(8,128)(2,1)S(1)} all-gather(bf16[64,2048]{1,0:T(8,128)(2,1)S(1)} %bitcast.10), channel_id=3, replica_groups={{0,1},{2,3},{4,5},{6,7},{8,9},{10,11},{12,13},{14,15},{16,17},{18,19},{..., dimensions={0}, use_global_device_ids=true | all-gather | bytes 786432 | tf_op jit(solution)/shard_map/all_gather | solution.py:143
  44.4 2.2 %all-gather.2.refs_1_ = bf16[128,2048]{1,0:T(8,128)(2,1)S(1)} all-gather(bf16[64,2048]{1,0:T(8,128)(2,1)S(1)} %copy-done.3), channel_id=4, replica_groups={{0,1},{2,3},{4,5},{6,7},{8,9},{10,11},{12,13},{14,15},{16,17},{18,19},{..., dimensions={0}, use_global_device_ids=true | all-gather | bytes 786432 | tf_op jit(solution)/shard_map/all_gather | solution.py:143
  46.6 0.0 collective-permute-done
  46.6 2.2 %all-gather.3.refs_2_ = bf16[128,2048]{1,0:T(8,128)(2,1)S(1)} all-gather(bf16[64,2048]{1,0:T(8,128)(2,1)S(1)} %collective-permute-done), channel_id=5, replica_groups={{0,1},{2,3},{4,5},{6,7},{8,9},{10,11},{12,13},{14,15},{16,17},{18,19},{..., dimensions={0}, use_global_device_ids=true | all-gather | bytes 786432 | tf_op jit(solution)/shard_map/all_gather | solution.py:143
  48.8 0.0 collective-permute-done.1
  48.8 2.2 %all-gather.4.refs_3_ = bf16[128,2048]{1,0:T(8,128)(2,1)S(1)} all-gather(bf16[64,2048]{1,0:T(8,128)(2,1)S(1)} %collective-permute-done.1), channel_id=6, replica_groups={{0,1},{2,3},{4,5},{6,7},{8,9},{10,11},{12,13},{14,15},{16,17},{18,19},{..., dimensions={0}, use_global_device_ids=true | all-gather | bytes 786432 | tf_op jit(solution)/shard_map/all_gather | solution.py:143
  51.0 4.1 %all-to-all-done.1.coeffs_ref = bf16[64,16,128]{2,1,0:T(8,128)(2,1)S(1)} async-done(((bf16[64,16,128]{2,1,0:T(8,128)(2,1)}), bf16[64,16,128]{2,1,0:T(8,128)(2,1)S(1)}, u32[]{:S(2)}, u32[]{:S(2)}) %all-to-all-start.1) | async-done | bytes 262176 | tf_op jit(solution)/shard_map/all_to_all | solution.py:140
  55.1 1.2 %shard_map.67 = bf16[128,8,128]{2,1,0:T(8,128)(2,1)S(1)} custom-call(bf16[64,16,128]{2,1,0:T(8,128)(2,1)S(1)} %all-to-all-done.1.coeffs_ref, bf16[128,2048]{1,0:T(8,128)(2,1)S(1)} %all-gather.1.refs_0_, bf16[128,2048]{1,0:T(8,128)(2,1)S(1)} %all-gather.2.refs_1_, bf16[128,2048]{1,0:T(8,128)(2,1)S(1)} %all-gather.3.refs_2_, ...), custom_call_target="tpu_custom_call" | custom-call | tf_op jit(solution)/shard_map/pallas_call | solution.py:183
  56.3 23.4 %all_to_all.15.parts_ref = bf16[128,8,128]{2,1,0:T(8,128)(2,1)S(1)} all-to-all(bf16[128,8,128]{2,1,0:T(8,128)(2,1)S(1)} %shard_map.67), channel_id=1, replica_groups=mesh['doc'=4,'seq'=128] {'seq'}, dimensions={0} | all-to-all | bytes 524288 | tf_op jit(solution)/shard_map/all_to_all | solution.py:186
  79.7 0.7 shard_map.68
  (3 shorter events, 0.0 us)
Async XLA Ops:
  0.0 31.6 %copy-start.1 = (f32[16,256]{1,0:T(8,128)S(1)}, f32[16,256]{1,0:T(8,128)}, u32[]{:S(2)}) copy-start(f32[16,256]{1,0:T(8,128)} %constant.25.clone.expand_ref) | copy-start | bytes 49156
  0.0 31.6 %copy-start = (bf16[2,256,512]{2,1,0:T(8,128)(2,1)S(1)}, bf16[2,256,512]{2,1,0:T(8,128)(2,1)}, u32[]{:S(2)}) copy-start(bf16[2,256,512]{2,1,0:T(8,128)(2,1)} %constant.24.clone.trig_ref) | copy-start | bytes 1572868
  0.0 20.0 %copy-start.2 = (bf16[2048,64]{0,1:T(8,128)(2,1)S(1)}, bf16[2048,64]{0,1:T(8,128)(2,1)}, u32[]{:S(2)}) copy-start(bf16[2048,64]{0,1:T(8,128)(2,1)} %param.7) | copy-start | bytes 786436
  0.0 23.0 %copy-start.3 = (bf16[64,2048]{1,0:T(8,128)(2,1)S(1)}, bf16[64,2048]{1,0:T(8,128)(2,1)}, u32[]{:S(2)}) copy-start(bf16[64,2048]{1,0:T(8,128)(2,1)} %param.8) | copy-start | bytes 786436
  2.9 28.7 %all-to-all-start = ((f32[64,4,128]{2,1,0:T(4,128)}), f32[64,4,128]{2,1,0:T(4,128)S(1)}, u32[]{:S(2)}, u32[]{:S(2)}) async-start(f32[64,4,128]{2,1,0:T(4,128)} %bitcast.8), calls=%async_computation | async-start | bytes 262144 | tf_op jit(solution)/shard_map/all_to_all | solution.py:140
  20.1 26.6 %collective-permute-start = (bf16[64,2048]{1,0:T(8,128)(2,1)S(1)}, bf16[64,2048]{1,0:T(8,128)(2,1)S(1)}, u32[]{:S(2)}, u32[]{:S(2)}) collective-permute-start(bf16[64,2048]{1,0:T(8,128)(2,1)S(1)} %bitcast.9), channel_id=1, source_target_pairs={{0,2},{1,3},{2,0},{3,1},{4,6},{5,7},{6,4},{7,5},{8,10},{9,11},{10,... | collective-permute-start | bytes 786440 | tf_op jit(solution)/shard_map/ppermute | solution.py:169
  23.0 25.8 %collective-permute-start.1 = (bf16[64,2048]{1,0:T(8,128)(2,1)S(1)}, bf16[64,2048]{1,0:T(8,128)(2,1)S(1)}, u32[]{:S(2)}, u32[]{:S(2)}) collective-permute-start(bf16[64,2048]{1,0:T(8,128)(2,1)S(1)} %copy-done.3), channel_id=1, source_target_pairs={{0,2},{1,3},{2,0},{3,1},{4,6},{5,7},{6,4},{7,5},{8,10},{9,11},{10,... | collective-permute-start | bytes 786440 | tf_op jit(solution)/shard_map/ppermute | solution.py:169
  36.5 18.6 %all-to-all-start.1 = ((bf16[64,16,128]{2,1,0:T(8,128)(2,1)}), bf16[64,16,128]{2,1,0:T(8,128)(2,1)S(1)}, u32[]{:S(2)}, u32[]{:S(2)}) async-start(bf16[64,16,128]{2,1,0:T(8,128)(2,1)} %get-tuple-element.7), calls=%async_computation.1 | async-start | bytes 524288 | tf_op jit(solution)/shard_map/all_to_all | solution.py:140

commit v5 on v4

--- a/solution.py
+++ b/solution.py
@@ -9,6 +9,7 @@
 from jax.sharding import PartitionSpec as P
 
 KEEP = 256
+TURN = 36
 MOMENTS = 16
 F32, BF16 = jnp.float32, jnp.bfloat16
 VMEM = pl.BlockSpec(memory_space=pltpu.VMEM)
@@ -22,7 +23,7 @@
     return high, low
 
 
-def window_tables(rows, windows):
+def window_tables(rows, windows, turn):
     t = (2.0 * np.arange(rows) + 1.0 - rows) / rows
     basis, _ = np.linalg.qr(np.polynomial.chebyshev.chebvander(t, MOMENTS - 1))
     basis = basis[:, list(range(0, MOMENTS, 2)) + list(range(1, MOMENTS, 2))]
@@ -36,7 +37,7 @@
     project = np.concatenate([high, low], axis=0)
     theta = np.pi * np.outer(2 * np.arange(windows) + 1, k) / (2 * windows)
     trig = np.concatenate([np.cos(theta), np.sin(theta)], axis=1)
-    trig = trig.reshape(windows // 2, 2, 2 * KEEP).transpose(1, 0, 2)
+    trig = np.roll(trig.reshape(windows // 2, 2, 2 * KEEP), -turn, axis=0).transpose(1, 0, 2)
     high, low = split_halves(trig)
     return project, expand, np.concatenate([high, low, high, low], axis=1)
 
@@ -62,7 +63,7 @@
         for block in range(columns // 128):
             turned = spread[:, 128 * block : 128 * (block + 1)].T
             packed = jnp.where(row == lane, turned, 0.0).reshape(16, 8, 128).sum(axis=1)
-            top = step * columns // 8 + 16 * block
+            top = (step * columns // 8 + 16 * block - 4 * TURN) % out_ref.shape[0]
             out_ref[top : top + 16, :] = packed
 
 
@@ -98,6 +99,7 @@
 def feed_forward_kernel(coeffs_ref, *refs):
     weights, out_ref = refs[:-1], refs[-1]
     packed = coeffs_ref[...]
+    packed = jnp.concatenate([packed[-TURN:], packed[:-TURN]], axis=0)
     kept = packed.shape[2] // 2
     width = packed.shape[0] * 32
     coeffs = jnp.concatenate([packed[:, :, :kept], packed[:, :, kept:]], axis=1).reshape(width, kept)
@@ -110,7 +112,8 @@
         branch += jnp.dot(activated, contract_ref[...], preferred_element_type=F32)
     for block in range(width // 128):
         turned = branch[:, 128 * block : 128 * (block + 1)].T.reshape(8, 16, kept)
-        out_ref[8 * block : 8 * (block + 1)] = jnp.concatenate([turned[:, :8], turned[:, 8:]], axis=2).astype(BF16)
+        first = (8 * block - 2 * TURN) % out_ref.shape[0]
+        out_ref[first : first + 8] = jnp.concatenate([turned[:, :8], turned[:, 8:]], axis=2).astype(BF16)
 
 
 def add_kernel(parts_ref, coeffs_ref, out_ref):
@@ -131,13 +134,13 @@
     windows = lax.axis_size("seq")
     chips = windows // 2
     mine = width // chips
-    project, expand, trig = window_tables(rows, windows)
-    same_core = [list(range(core, windows, 2)) for core in range(2)]
+    project, expand, trig = window_tables(rows, windows, TURN)
     pairs = [[2 * chip, 2 * chip + 1] for chip in range(chips)]
     core = lax.axis_index("seq") % 2
 
-    def exchange(x):
-        return lax.all_to_all(x, "seq", 0, 0, axis_index_groups=same_core)
+    def exchange(x, step=2):
+        groups = [[(2 * TURN + i) % windows for i in range(core, windows, step)] for core in range(step)]
+        return lax.all_to_all(x, "seq", 0, 0, axis_index_groups=groups)
 
     def gather_pair(x):
         return lax.all_gather(x, "seq", axis_index_groups=pairs)
@@ -183,7 +186,7 @@
     branch = kernel(
         feed_forward_kernel, jax.ShapeDtypeStruct((windows, mine // 4, KEEP // 2), BF16), [VMEM] * 5
     )(exchange(spread), *weights)
-    parts = lax.all_to_all(branch, "seq", 0, 0)
+    parts = exchange(branch, step=1)
     return kernel(add_kernel, jax.ShapeDtypeStruct(coeffs.shape, BF16), [VMEM, VMEM])(parts, coeffs).T
 
 

time: 81 us -> 76.3 us (0.942)
  waiting for transfers between devices: 10.3 us -> 0.01 us
  starting transfers between devices: 27.9 us -> 37.5 us
  blocking collectives: 36.1 us -> 32.4 us
    all_to_all x2, waiting for transfers between devices: 10.3 us -> 0.01 us  [exchange(): return lax.all_to_all(x, 'seq', 0, 0, axis_index_groups=groups)]
    all_to_all x2, starting transfers between devices: 22.7 us -> 32.2 us  [exchange(): return lax.all_to_all(x, 'seq', 0, 0, axis_index_groups=groups)]
    all_to_all x1, blocking collectives: 23.4 us -> 19.9 us  [exchange(): return lax.all_to_all(x, 'seq', 0, 0, axis_index_groups=groups)]
  transfers between devices with their start and end apart: 4 -> 4, of which waited for: 2 -> 0; matrix products, arithmetic and copies ran while one was open for 0% -> 0% of each run, Pallas kernels for 1% -> 2%
where the time goes in v5:
time: 76.3 us; the launch traced here: 76 us
  starting transfers between devices  37.5 us (49%)
  blocking collectives  32.4 us (42%)
  Pallas kernels  5.95 us (8%)
    all_to_all x2, starting transfers between devices, exchange(): return lax.all_to_all(x, 'seq', 0, 0, axis_index_groups=groups)  32.2 us
    all_to_all x1, blocking collectives, exchange(): return lax.all_to_all(x, 'seq', 0, 0, axis_index_groups=groups)  19.9 us
    all_gather x5, blocking collectives, gather_pair(): return lax.all_gather(x, 'seq', axis_index_groups=pairs)  12.5 us
    ppermute x1, starting transfers between devices, local(): lax.ppermute(w_contract, 'seq', beside)  3.08 us
    pallas_call x1, Pallas kernels, local(): kernel(moments_kernel, jax.ShapeDtypeStruct((width // 8, 128), F32), [ANY...  2.86 us
    ppermute x1, starting transfers between devices, local(): lax.ppermute(w_expand, 'seq', beside)  2.2 us
  transfers between devices with their start and end apart: 4, of which 0 were waited for; matrix products, arithmetic and copies ran while one was open for 0% of the time, Pallas kernels for 2%

profile of v5, /device:TPU:1, one launch (start us, length us, event | category | flops | bytes accessed | tf_op | source)
XLA Modules:
  0.0 76.0 jit_solution(15725271378956656516)
XLA Ops:
  0.0 0.0 copy-start.3
  0.0 2.9 %shard_map.64 = f32[256,128]{1,0:T(8,128)} custom-call(bf16[32,512]{1,0:T(8,128)(2,1)} %constant.23.clone.project_hbm, bf16[512,2048]{1,0:T(8,128)(2,1)} %rows_hbm.1), custom_call_target="tpu_custom_call" | custom-call | tf_op jit(solution)/shard_map/pallas_call | solution.py:158
  2.9 20.1 %all-to-all-start = ((f32[64,4,128]{2,1,0:T(4,128)}), f32[64,4,128]{2,1,0:T(4,128)S(1)}, u32[]{:S(2)}, u32[]{:S(2)}) async-start(f32[64,4,128]{2,1,0:T(4,128)} %bitcast.8), calls=%async_computation | async-start | bytes 262144 | tf_op jit(solution)/shard_map/all_to_all | solution.py:143
  23.0 0.0 copy-done.2
  23.0 2.2 %collective-permute-start = (bf16[64,2048]{1,0:T(8,128)(2,1)S(1)}, bf16[64,2048]{1,0:T(8,128)(2,1)S(1)}, u32[]{:S(2)}, u32[]{:S(2)}) collective-permute-start(bf16[64,2048]{1,0:T(8,128)(2,1)S(1)} %bitcast.9), channel_id=1, source_target_pairs={{0,2},{1,3},{2,0},{3,1},{4,6},{5,7},{6,4},{7,5},{8,10},{9,11},{10,... | collective-permute-start | bytes 786440 | tf_op jit(solution)/shard_map/ppermute | solution.py:172
  25.2 0.0 copy-done.3
  25.2 3.1 %collective-permute-start.1 = (bf16[64,2048]{1,0:T(8,128)(2,1)S(1)}, bf16[64,2048]{1,0:T(8,128)(2,1)S(1)}, u32[]{:S(2)}, u32[]{:S(2)}) collective-permute-start(bf16[64,2048]{1,0:T(8,128)(2,1)S(1)} %copy-done.3), channel_id=1, source_target_pairs={{0,2},{1,3},{2,0},{3,1},{4,6},{5,7},{6,4},{7,5},{8,10},{9,11},{10,... | collective-permute-start | bytes 786440 | tf_op jit(solution)/shard_map/ppermute | solution.py:172
  28.3 0.0 all-to-all-done
  28.3 0.0 copy-done.1
  28.3 0.0 copy-done
  28.3 0.3 shard_map.65
  28.7 3.3 %all-gather = f32[64,256]{1,0:T(8,128)S(1)} all-gather(f32[32,256]{1,0:T(8,128)S(1)} %shard_map.65), channel_id=2, replica_groups={{0,1},{2,3},{4,5},{6,7},{8,9},{10,11},{12,13},{14,15},{16,17},{18,19},{..., dimensions={0}, use_global_device_ids=true | all-gather | bytes 98304 | tf_op jit(solution)/shard_map/all_gather | solution.py:146
  32.0 0.8 %shard_map.66 = (bf16[16,256]{1,0:T(8,128)(2,1)S(1)}, bf16[64,16,128]{2,1,0:T(8,128)(2,1)}) custom-call(s32[1]{0:T(128)} %bitcast.core_ref, f32[2,32,256]{2,1,0:T(8,128)S(1)} %bitcast.7), custom_call_target="tpu_custom_call" | custom-call | tf_op jit(solution)/shard_map/pallas_call | solution.py:178
  32.8 12.1 %all-to-all-start.1 = ((bf16[64,16,128]{2,1,0:T(8,128)(2,1)}), bf16[64,16,128]{2,1,0:T(8,128)(2,1)S(1)}, u32[]{:S(2)}, u32[]{:S(2)}) async-start(bf16[64,16,128]{2,1,0:T(8,128)(2,1)} %get-tuple-element.7), calls=%async_computation.1 | async-start | bytes 524288 | tf_op jit(solution)/shard_map/all_to_all | solution.py:143
  44.9 2.7 %all-gather.1.refs_0_ = bf16[128,2048]{1,0:T(8,128)(2,1)S(1)} all-gather(bf16[64,2048]{1,0:T(8,128)(2,1)S(1)} %bitcast.10), channel_id=3, replica_groups={{0,1},{2,3},{4,5},{6,7},{8,9},{10,11},{12,13},{14,15},{16,17},{18,19},{..., dimensions={0}, use_global_device_ids=true | all-gather | bytes 786432 | tf_op jit(solution)/shard_map/all_gather | solution.py:146
  47.6 2.2 %all-gather.2.refs_1_ = bf16[128,2048]{1,0:T(8,128)(2,1)S(1)} all-gather(bf16[64,2048]{1,0:T(8,128)(2,1)S(1)} %copy-done.3), channel_id=4, replica_groups={{0,1},{2,3},{4,5},{6,7},{8,9},{10,11},{12,13},{14,15},{16,17},{18,19},{..., dimensions={0}, use_global_device_ids=true | all-gather | bytes 786432 | tf_op jit(solution)/shard_map/all_gather | solution.py:146
  49.8 0.0 collective-permute-done
  49.8 2.2 %all-gather.3.refs_2_ = bf16[128,2048]{1,0:T(8,128)(2,1)S(1)} all-gather(bf16[64,2048]{1,0:T(8,128)(2,1)S(1)} %collective-permute-done), channel_id=5, replica_groups={{0,1},{2,3},{4,5},{6,7},{8,9},{10,11},{12,13},{14,15},{16,17},{18,19},{..., dimensions={0}, use_global_device_ids=true | all-gather | bytes 786432 | tf_op jit(solution)/shard_map/all_gather | solution.py:146
  51.9 0.0 collective-permute-done.1
  52.0 2.2 %all-gather.4.refs_3_ = bf16[128,2048]{1,0:T(8,128)(2,1)S(1)} all-gather(bf16[64,2048]{1,0:T(8,128)(2,1)S(1)} %collective-permute-done.1), channel_id=6, replica_groups={{0,1},{2,3},{4,5},{6,7},{8,9},{10,11},{12,13},{14,15},{16,17},{18,19},{..., dimensions={0}, use_global_device_ids=true | all-gather | bytes 786432 | tf_op jit(solution)/shard_map/all_gather | solution.py:146
  54.1 0.0 all-to-all-done.1.coeffs_ref
  54.1 1.2 %shard_map.67 = bf16[128,8,128]{2,1,0:T(8,128)(2,1)S(1)} custom-call(bf16[64,16,128]{2,1,0:T(8,128)(2,1)S(1)} %all-to-all-done.1.coeffs_ref, bf16[128,2048]{1,0:T(8,128)(2,1)S(1)} %all-gather.1.refs_0_, bf16[128,2048]{1,0:T(8,128)(2,1)S(1)} %all-gather.2.refs_1_, bf16[128,2048]{1,0:T(8,128)(2,1)S(1)} %all-gather.3.refs_2_, ...), custom_call_target="tpu_custom_call" | custom-call | tf_op jit(solution)/shard_map/pallas_call | solution.py:186
  55.4 19.9 %all_to_all.15.parts_ref = bf16[128,8,128]{2,1,0:T(8,128)(2,1)S(1)} all-to-all(bf16[128,8,128]{2,1,0:T(8,128)(2,1)S(1)} %shard_map.67), channel_id=1, replica_groups={{72,73,74,75,76,77,78,79,80,81,82,83,84,85,86,87,88,89,90,91,92,93,94,9..., dimensions={0} | all-to-all | bytes 524288 | tf_op jit(solution)/shard_map/all_to_all | solution.py:143
  75.3 0.7 shard_map.68
  (3 shorter events, 0.0 us)
Async XLA Ops:
  0.0 28.3 %copy-start.1 = (f32[16,256]{1,0:T(8,128)S(1)}, f32[16,256]{1,0:T(8,128)}, u32[]{:S(2)}) copy-start(f32[16,256]{1,0:T(8,128)} %constant.25.clone.expand_ref) | copy-start | bytes 49156
  0.0 28.3 %copy-start = (bf16[2,256,512]{2,1,0:T(8,128)(2,1)S(1)}, bf16[2,256,512]{2,1,0:T(8,128)(2,1)}, u32[]{:S(2)}) copy-start(bf16[2,256,512]{2,1,0:T(8,128)(2,1)} %constant.24.clone.trig_ref) | copy-start | bytes 1572868
  0.0 23.0 %copy-start.2 = (bf16[2048,64]{0,1:T(8,128)(2,1)S(1)}, bf16[2048,64]{0,1:T(8,128)(2,1)}, u32[]{:S(2)}) copy-start(bf16[2048,64]{0,1:T(8,128)(2,1)} %param.7) | copy-start | bytes 786436
  0.0 25.2 %copy-start.3 = (bf16[64,2048]{1,0:T(8,128)(2,1)S(1)}, bf16[64,2048]{1,0:T(8,128)(2,1)}, u32[]{:S(2)}) copy-start(bf16[64,2048]{1,0:T(8,128)(2,1)} %param.8) | copy-start | bytes 786436
  2.9 25.4 %all-to-all-start = ((f32[64,4,128]{2,1,0:T(4,128)}), f32[64,4,128]{2,1,0:T(4,128)S(1)}, u32[]{:S(2)}, u32[]{:S(2)}) async-start(f32[64,4,128]{2,1,0:T(4,128)} %bitcast.8), calls=%async_computation | async-start | bytes 262144 | tf_op jit(solution)/shard_map/all_to_all | solution.py:143
  23.0 26.8 %collective-permute-start = (bf16[64,2048]{1,0:T(8,128)(2,1)S(1)}, bf16[64,2048]{1,0:T(8,128)(2,1)S(1)}, u32[]{:S(2)}, u32[]{:S(2)}) collective-permute-start(bf16[64,2048]{1,0:T(8,128)(2,1)S(1)} %bitcast.9), channel_id=1, source_target_pairs={{0,2},{1,3},{2,0},{3,1},{4,6},{5,7},{6,4},{7,5},{8,10},{9,11},{10,... | collective-permute-start | bytes 786440 | tf_op jit(solution)/shard_map/ppermute | solution.py:172
  25.2 26.7 %collective-permute-start.1 = (bf16[64,2048]{1,0:T(8,128)(2,1)S(1)}, bf16[64,2048]{1,0:T(8,128)(2,1)S(1)}, u32[]{:S(2)}, u32[]{:S(2)}) collective-permute-start(bf16[64,2048]{1,0:T(8,128)(2,1)S(1)} %copy-done.3), channel_id=1, source_target_pairs={{0,2},{1,3},{2,0},{3,1},{4,6},{5,7},{6,4},{7,5},{8,10},{9,11},{10,... | collective-permute-start | bytes 786440 | tf_op jit(solution)/shard_map/ppermute | solution.py:172
  32.8 21.3 %all-to-all-start.1 = ((bf16[64,16,128]{2,1,0:T(8,128)(2,1)}), bf16[64,16,128]{2,1,0:T(8,128)(2,1)S(1)}, u32[]{:S(2)}, u32[]{:S(2)}) async-start(bf16[64,16,128]{2,1,0:T(8,128)(2,1)} %get-tuple-element.7), calls=%async_computation.1 | async-start | bytes 524288 | tf_op jit(solution)/shard_map/all_to_all | solution.py:143

commit v6 on v5

--- a/solution.py
+++ b/solution.py
@@ -96,24 +96,37 @@
     out_ref[...] = jnp.broadcast_to(pair[None], (out_ref.shape[0] // 2,) + pair.shape).reshape(out_ref.shape)
 
 
-def feed_forward_kernel(coeffs_ref, *refs):
+def stack_kernel(expand_ref, contract_ref, out_ref):
+    units = expand_ref.shape[0]
+    out_ref[:units, :] = expand_ref[...]
+    out_ref[units:, :] = contract_ref[...]
+
+
+def scale_kernel(packed_ref, scale_ref):
+    wide = packed_ref[...].astype(F32)
+    sums = jnp.sum(wide * wide, axis=(0, 1))[None]
+    lanes = sums.shape[1]
+    sums += pltpu.roll(sums, lanes // 2, 1)
+    scale_ref[...] = lax.rsqrt(sums / (wide.size // (lanes // 2)) + 1e-06)
+
+
+def feed_forward_kernel(packed_ref, scale_ref, *refs):
     weights, out_ref = refs[:-1], refs[-1]
-    packed = coeffs_ref[...]
-    packed = jnp.concatenate([packed[-TURN:], packed[:-TURN]], axis=0)
+    units = weights[0].shape[0] // 2
+    packed = jnp.concatenate([packed_ref[-TURN:], packed_ref[:-TURN]], axis=0)
     kept = packed.shape[2] // 2
     width = packed.shape[0] * 32
     coeffs = jnp.concatenate([packed[:, :, :kept], packed[:, :, kept:]], axis=1).reshape(width, kept)
-    wide = coeffs.astype(F32)
-    scale = lax.rsqrt(jnp.sum(wide * wide, axis=0, keepdims=True) / width + 1e-06)
-    branch = jnp.zeros((kept, width), F32)
-    for expand_ref, contract_ref in zip(weights[::2], weights[1::2]):
-        expanded = jnp.dot(expand_ref[...], coeffs, preferred_element_type=F32) * scale
-        activated = jax.nn.gelu(expanded).T.astype(BF16)
-        branch += jnp.dot(activated, contract_ref[...], preferred_element_type=F32)
-    for block in range(width // 128):
-        turned = branch[:, 128 * block : 128 * (block + 1)].T.reshape(8, 16, kept)
-        first = (8 * block - 2 * TURN) % out_ref.shape[0]
-        out_ref[first : first + 8] = jnp.concatenate([turned[:, :8], turned[:, 8:]], axis=2).astype(BF16)
+    expand = jnp.concatenate([ref[:units, :] for ref in weights], axis=0)
+    expanded = jnp.dot(expand, coeffs, preferred_element_type=F32) * scale_ref[:, :kept]
+    activated = jax.nn.gelu(expanded).T.astype(BF16)
+    for start in range(0, width, 256):
+        contract = jnp.concatenate([ref[units:, start : start + 256] for ref in weights], axis=0)
+        branch = jnp.dot(activated, contract, preferred_element_type=F32)
+        for half in range(2):
+            turned = branch[:, 128 * half : 128 * (half + 1)].T.reshape(8, 16, kept)
+            first = (start // 16 + 8 * half - 2 * TURN) % out_ref.shape[0]
+            out_ref[first : first + 8] = jnp.concatenate([turned[:, :8], turned[:, 8:]], axis=2).astype(BF16)
 
 
 def add_kernel(parts_ref, coeffs_ref, out_ref):
@@ -167,10 +180,12 @@
         ],
     )(jnp.asarray(project), hidden_rows)
     received = exchange(moments.reshape(chips, -1, 128)).reshape(-1, 128)
-    beside = [(i, i ^ 2) for i in range(windows)]
-    w_expand = w_expand.T
-    weights = [w_expand, w_contract, lax.ppermute(w_expand, "seq", beside), lax.ppermute(w_contract, "seq", beside)]
-    weights = [gather_pair(x).reshape(-1, width) for x in weights]
+    own = kernel(
+        stack_kernel, jax.ShapeDtypeStruct((2 * w_contract.shape[0], width), BF16), [VMEM, VMEM]
+    )(w_expand.T, w_contract)
+    beside = lax.ppermute(own, "seq", [(i, i ^ 2) for i in range(windows)])
+    other_core = [(i, i ^ 1) for i in range(windows)]
+    weights = [own, beside, lax.ppermute(own, "seq", other_core), lax.ppermute(beside, "seq", other_core)]
     partial = kernel(
         coeffs_kernel, jax.ShapeDtypeStruct((mine, KEEP), F32), [SMEM, VMEM, VMEM, VMEM]
     )(core_index, received, jnp.asarray(trig), jnp.asarray(expand))
@@ -183,9 +198,16 @@
         ],
         [SMEM, VMEM],
     )(core_index, both)
+    gathered = exchange(spread)
+    scale = kernel(
+        scale_kernel,
+        jax.ShapeDtypeStruct((1, KEEP // 2), F32),
+        [VMEM],
+        cost_estimate=pl.CostEstimate(flops=2 * 10**10, bytes_accessed=1 << 20, transcendentals=0),
+    )(gathered)
     branch = kernel(
-        feed_forward_kernel, jax.ShapeDtypeStruct((windows, mine // 4, KEEP // 2), BF16), [VMEM] * 5
-    )(exchange(spread), *weights)
+        feed_forward_kernel, jax.ShapeDtypeStruct((windows, mine // 4, KEEP // 2), BF16), [VMEM] * 6
+    )(gathered, scale, *weights)
     parts = exchange(branch, step=1)
     return kernel(add_kernel, jax.ShapeDtypeStruct(coeffs.shape, BF16), [VMEM, VMEM])(parts, coeffs).T
 

time: 76.3 us -> 72.9 us (0.955)
  blocking collectives: 32.4 us -> 23.6 us
  waiting for transfers between devices: 0.01 us -> 2.9 us
  starting transfers between devices: 37.5 us -> 39.8 us
    all_gather x5 -> x1, blocking collectives: 12.5 us -> 3.35 us  [gather_pair(): return lax.all_gather(x, 'seq', axis_index_groups=pairs)]
    all_to_all x2, waiting for transfers between devices: 0.01 us -> 2.89 us  [exchange(): return lax.all_to_all(x, 'seq', 0, 0, axis_index_groups=groups)]
    ppermute x2 -> x3, starting transfers between devices: 5.28 us -> 6.66 us  [the longest x1 2.54 us: local(): lax.ppermute(own, 'seq', other_core)]
    all_to_all x2, starting transfers between devices: 32.2 us -> 33.1 us  [exchange(): return lax.all_to_all(x, 'seq', 0, 0, axis_index_groups=groups)]
  transfers between devices with their start and end apart: 4 -> 5, of which waited for: 0 -> 2; matrix products, arithmetic and copies ran while one was open for 0% -> 0% of each run, Pallas kernels for 2% -> 2%
where the time goes in v6:
time: 72.9 us; the launch traced here: 72.6 us
  starting transfers between devices  39.8 us (55%)
  blocking collectives  23.6 us (32%)
  Pallas kernels  6.19 us (8%)
  waiting for transfers between devices  2.9 us (4%)
    all_to_all x2, starting transfers between devices, exchange(): return lax.all_to_all(x, 'seq', 0, 0, axis_index_groups=groups)  33.1 us
    all_to_all x1, blocking collectives, exchange(): return lax.all_to_all(x, 'seq', 0, 0, axis_index_groups=groups)  20.2 us
    all_gather x1, blocking collectives, gather_pair(): return lax.all_gather(x, 'seq', axis_index_groups=pairs)  3.35 us
    all_to_all x2, waiting for transfers between devices, exchange(): return lax.all_to_all(x, 'seq', 0, 0, axis_index_groups=groups)  2.89 us
    pallas_call x1, Pallas kernels, local(): kernel(moments_kernel, jax.ShapeDtypeStruct((width // 8, 128), F32), [ANY...  2.86 us
    ppermute x1, starting transfers between devices, local(): lax.ppermute(own, 'seq', other_core)  2.54 us
    ppermute x1, starting transfers between devices, local(): beside = lax.ppermute(own, 'seq', [(i, i ^ 2) for i in range(windows)])  2.2 us
    ppermute x1, starting transfers between devices, local(): lax.ppermute(beside, 'seq', other_core)  1.92 us
  transfers between devices with their start and end apart: 5, of which 2 were waited for; matrix products, arithmetic and copies ran while one was open for 0% of the time, Pallas kernels for 2%

profile of v6, /device:TPU:1, one launch (start us, length us, event | category | flops | bytes accessed | tf_op | source)
XLA Modules:
  0.0 72.6 jit_solution(17300090532953108960)
XLA Ops:
  0.0 0.0 copy-start.3
  0.0 0.0 copy-start.1
  0.0 2.9 %shard_map.64 = f32[256,128]{1,0:T(8,128)} custom-call(bf16[32,512]{1,0:T(8,128)(2,1)} %constant.23.clone.project_hbm, bf16[512,2048]{1,0:T(8,128)(2,1)} %rows_hbm.1), custom_call_target="tpu_custom_call" | custom-call | tf_op jit(solution)/shard_map/pallas_call | solution.py:171
  2.9 20.1 %all-to-all-start = ((f32[64,4,128]{2,1,0:T(4,128)}), f32[64,4,128]{2,1,0:T(4,128)S(1)}, u32[]{:S(2)}, u32[]{:S(2)}) async-start(f32[64,4,128]{2,1,0:T(4,128)} %bitcast.9), calls=%async_computation | async-start | bytes 262144 | tf_op jit(solution)/shard_map/all_to_all | solution.py:156
  23.0 0.0 copy-done.2
  23.0 0.0 copy-done.1
  23.0 2.2 %collective-permute-start = (bf16[128,2048]{1,0:T(8,128)(2,1)S(1)}, bf16[128,2048]{1,0:T(8,128)(2,1)S(1)}, u32[]{:S(2)}, u32[]{:S(2)}) collective-permute-start(bf16[128,2048]{1,0:T(8,128)(2,1)S(1)} %shard_map.68.refs_0_), channel_id=1, source_target_pairs={{0,2},{1,3},{2,0},{3,1},{4,6},{5,7},{6,4},{7,5},{8,10},{9,11},{10,... | collective-permute-start | bytes 1572872 | tf_op jit(solution)/shard_map/ppermute | solution.py:186
  25.3 0.5 all-to-all-done
  25.8 0.0 copy-done.3
  25.8 0.0 copy-done
  25.8 0.3 shard_map.65
  26.1 3.4 %all-gather = f32[64,256]{1,0:T(8,128)S(1)} all-gather(f32[32,256]{1,0:T(8,128)S(1)} %shard_map.65), channel_id=2, replica_groups={{0,1},{2,3},{4,5},{6,7},{8,9},{10,11},{12,13},{14,15},{16,17},{18,19},{..., dimensions={0}, use_global_device_ids=true | all-gather | bytes 98304 | tf_op jit(solution)/shard_map/all_gather | solution.py:159
  29.5 0.8 %shard_map.66 = (bf16[16,256]{1,0:T(8,128)(2,1)S(1)}, bf16[64,16,128]{2,1,0:T(8,128)(2,1)}) custom-call(s32[1]{0:T(128)} %bitcast.core_ref, f32[2,32,256]{2,1,0:T(8,128)S(1)} %bitcast.7), custom_call_target="tpu_custom_call" | custom-call | tf_op jit(solution)/shard_map/pallas_call | solution.py:193
  30.3 13.0 %all-to-all-start.1 = ((bf16[64,16,128]{2,1,0:T(8,128)(2,1)}), bf16[64,16,128]{2,1,0:T(8,128)(2,1)S(1)}, u32[]{:S(2)}, u32[]{:S(2)}) async-start(bf16[64,16,128]{2,1,0:T(8,128)(2,1)} %get-tuple-element.7), calls=%async_computation.1 | async-start | bytes 524288 | tf_op jit(solution)/shard_map/all_to_all | solution.py:156
  43.3 2.5 %collective-permute-start.1 = (bf16[128,2048]{1,0:T(8,128)(2,1)S(1)}, bf16[128,2048]{1,0:T(8,128)(2,1)S(1)}, u32[]{:S(2)}, u32[]{:S(2)}) collective-permute-start(bf16[128,2048]{1,0:T(8,128)(2,1)S(1)} %shard_map.68.refs_0_), channel_id=1, source_target_pairs={{0,1},{1,0},{2,3},{3,2},{4,5},{5,4},{6,7},{7,6},{8,9},{9,8},{10,11... | collective-permute-start | bytes 1572872 | tf_op jit(solution)/shard_map/ppermute | solution.py:188
  45.9 0.0 collective-permute-done.refs_1_
  45.9 1.9 %collective-permute-start.2 = (bf16[128,2048]{1,0:T(8,128)(2,1)S(1)}, bf16[128,2048]{1,0:T(8,128)(2,1)S(1)}, u32[]{:S(2)}, u32[]{:S(2)}) collective-permute-start(bf16[128,2048]{1,0:T(8,128)(2,1)S(1)} %collective-permute-done.refs_1_), channel_id=1, source_target_pairs={{0,1},{1,0},{2,3},{3,2},{4,5},{5,4},{6,7},{7,6},{8,9},{9,8},{10,11... | collective-permute-start | bytes 1572872 | tf_op jit(solution)/shard_map/ppermute | solution.py:188
  47.8 2.4 %all-to-all-done.1.packed_ref = bf16[64,16,128]{2,1,0:T(8,128)(2,1)S(1)} async-done(((bf16[64,16,128]{2,1,0:T(8,128)(2,1)}), bf16[64,16,128]{2,1,0:T(8,128)(2,1)S(1)}, u32[]{:S(2)}, u32[]{:S(2)}) %all-to-all-start.1) | async-done | bytes 262176 | tf_op jit(solution)/shard_map/all_to_all | solution.py:156
  50.2 0.2 shard_map.67.scale_ref
  50.4 0.0 collective-permute-done.1.refs_2_
  50.4 0.0 collective-permute-done.2.refs_3_
  50.4 1.2 %shard_map.69 = bf16[128,8,128]{2,1,0:T(8,128)(2,1)S(1)} custom-call(bf16[64,16,128]{2,1,0:T(8,128)(2,1)S(1)} %all-to-all-done.1.packed_ref, f32[1,128]{1,0:T(1,128)S(1)} %shard_map.67.scale_ref, bf16[128,2048]{1,0:T(8,128)(2,1)S(1)} %shard_map.68.refs_0_, bf16[128,2048]{1,0:T(8,128)(2,1)S(1)} %collective-permute-done.refs_1_, ...), custom_call_target="tpu_custom_call" | custom-call | tf_op jit(solution)/shard_map/pallas_call | solution.py:208
  51.6 20.2 %all_to_all.15.parts_ref = bf16[128,8,128]{2,1,0:T(8,128)(2,1)S(1)} all-to-all(bf16[128,8,128]{2,1,0:T(8,128)(2,1)S(1)} %shard_map.69), channel_id=1, replica_groups={{72,73,74,75,76,77,78,79,80,81,82,83,84,85,86,87,88,89,90,91,92,93,94,9..., dimensions={0} | all-to-all | bytes 524288 | tf_op jit(solution)/shard_map/all_to_all | solution.py:156
  71.8 0.7 shard_map.70
  (3 shorter events, 0.0 us)
Async XLA Ops:
  0.0 25.8 %copy-start.3 = (f32[16,256]{1,0:T(8,128)S(1)}, f32[16,256]{1,0:T(8,128)}, u32[]{:S(2)}) copy-start(f32[16,256]{1,0:T(8,128)} %constant.25.clone.expand_ref) | copy-start | bytes 49156
  0.0 25.8 %copy-start = (bf16[2,256,512]{2,1,0:T(8,128)(2,1)S(1)}, bf16[2,256,512]{2,1,0:T(8,128)(2,1)}, u32[]{:S(2)}) copy-start(bf16[2,256,512]{2,1,0:T(8,128)(2,1)} %constant.24.clone.trig_ref) | copy-start | bytes 1572868
  0.0 23.0 %copy-start.2 = (bf16[64,2048]{1,0:T(8,128)(2,1)S(1)}, bf16[64,2048]{1,0:T(8,128)(2,1)}, u32[]{:S(2)}) copy-start(bf16[64,2048]{1,0:T(8,128)(2,1)} %contract_ref.1) | copy-start | bytes 786436
  0.0 23.0 %copy-start.1 = (bf16[2048,64]{0,1:T(8,128)(2,1)S(1)}, bf16[2048,64]{0,1:T(8,128)(2,1)}, u32[]{:S(2)}) copy-start(bf16[2048,64]{0,1:T(8,128)(2,1)} %param.7) | copy-start | bytes 786436
  2.9 22.9 %all-to-all-start = ((f32[64,4,128]{2,1,0:T(4,128)}), f32[64,4,128]{2,1,0:T(4,128)S(1)}, u32[]{:S(2)}, u32[]{:S(2)}) async-start(f32[64,4,128]{2,1,0:T(4,128)} %bitcast.9), calls=%async_computation | async-start | bytes 262144 | tf_op jit(solution)/shard_map/all_to_all | solution.py:156
  23.0 22.8 %collective-permute-start = (bf16[128,2048]{1,0:T(8,128)(2,1)S(1)}, bf16[128,2048]{1,0:T(8,128)(2,1)S(1)}, u32[]{:S(2)}, u32[]{:S(2)}) collective-permute-start(bf16[128,2048]{1,0:T(8,128)(2,1)S(1)} %shard_map.68.refs_0_), channel_id=1, source_target_pairs={{0,2},{1,3},{2,0},{3,1},{4,6},{5,7},{6,4},{7,5},{8,10},{9,11},{10,... | collective-permute-start | bytes 1572872 | tf_op jit(solution)/shard_map/ppermute | solution.py:186
  30.3 19.9 %all-to-all-start.1 = ((bf16[64,16,128]{2,1,0:T(8,128)(2,1)}), bf16[64,16,128]{2,1,0:T(8,128)(2,1)S(1)}, u32[]{:S(2)}, u32[]{:S(2)}) async-start(bf16[64,16,128]{2,1,0:T(8,128)(2,1)} %get-tuple-element.7), calls=%async_computation.1 | async-start | bytes 524288 | tf_op jit(solution)/shard_map/all_to_all | solution.py:156
  43.3 7.1 %collective-permute-start.1 = (bf16[128,2048]{1,0:T(8,128)(2,1)S(1)}, bf16[128,2048]{1,0:T(8,128)(2,1)S(1)}, u32[]{:S(2)}, u32[]{:S(2)}) collective-permute-start(bf16[128,2048]{1,0:T(8,128)(2,1)S(1)} %shard_map.68.refs_0_), channel_id=1, source_target_pairs={{0,1},{1,0},{2,3},{3,2},{4,5},{5,4},{6,7},{7,6},{8,9},{9,8},{10,11... | collective-permute-start | bytes 1572872 | tf_op jit(solution)/shard_map/ppermute | solution.py:188
  45.9 4.5 %collective-permute-start.2 = (bf16[128,2048]{1,0:T(8,128)(2,1)S(1)}, bf16[128,2048]{1,0:T(8,128)(2,1)S(1)}, u32[]{:S(2)}, u32[]{:S(2)}) collective-permute-start(bf16[128,2048]{1,0:T(8,128)(2,1)S(1)} %collective-permute-done.refs_1_), channel_id=1, source_target_pairs={{0,1},{1,0},{2,3},{3,2},{4,5},{5,4},{6,7},{7,6},{8,9},{9,8},{10,11... | collective-permute-start | bytes 1572872 | tf_op jit(solution)/shard_map/ppermute | solution.py:188

commit v7 on v6

--- a/solution.py
+++ b/solution.py
@@ -122,11 +122,12 @@
     activated = jax.nn.gelu(expanded).T.astype(BF16)
     for start in range(0, width, 256):
         contract = jnp.concatenate([ref[units:, start : start + 256] for ref in weights], axis=0)
-        branch = jnp.dot(activated, contract, preferred_element_type=F32)
+        branch = jnp.dot(activated, contract, preferred_element_type=F32).astype(BF16)
         for half in range(2):
-            turned = branch[:, 128 * half : 128 * (half + 1)].T.reshape(8, 16, kept)
+            turned = branch[:, 128 * half : 128 * (half + 1)].T.reshape(4, 2, 16, kept)
+            turned = jnp.stack([turned[:, 1], turned[:, 0]], axis=1).reshape(8, 16, kept)
             first = (start // 16 + 8 * half - 2 * TURN) % out_ref.shape[0]
-            out_ref[first : first + 8] = jnp.concatenate([turned[:, :8], turned[:, 8:]], axis=2).astype(BF16)
+            out_ref[first : first + 8] = jnp.concatenate([turned[:, :8], turned[:, 8:]], axis=2)
 
 
 def add_kernel(parts_ref, coeffs_ref, out_ref):
@@ -134,7 +135,7 @@
     sums = jnp.sum(parts_ref[...].astype(F32).reshape(sources // 4, 4, rows, lanes), axis=0)
     left = lax.broadcasted_iota(jnp.int32, (rows, lanes), 1) < lanes // 2
     for core in range(2):
-        first, second = sums[core], sums[2 + core]
+        first, second = sums[1 - core], sums[3 - core]
         low = jnp.where(left, first, pltpu.roll(second, lanes // 2, 1))
         high = jnp.where(left, pltpu.roll(first, lanes // 2, 1), second)
         total = jnp.concatenate([low, high], axis=0)
@@ -151,8 +152,10 @@
     pairs = [[2 * chip, 2 * chip + 1] for chip in range(chips)]
     core = lax.axis_index("seq") % 2
 
-    def exchange(x, step=2):
-        groups = [[(2 * TURN + i) % windows for i in range(core, windows, step)] for core in range(step)]
+    same_core = [[(2 * TURN + i) % windows for i in range(core, windows, 2)] for core in range(2)]
+    both_cores = [[(2 * TURN + i) % windows ^ 1 for i in range(windows)]]
+
+    def exchange(x, groups=same_core):
         return lax.all_to_all(x, "seq", 0, 0, axis_index_groups=groups)
 
     def gather_pair(x):
@@ -208,7 +211,7 @@
     branch = kernel(
         feed_forward_kernel, jax.ShapeDtypeStruct((windows, mine // 4, KEEP // 2), BF16), [VMEM] * 6
     )(gathered, scale, *weights)
-    parts = exchange(branch, step=1)
+    parts = exchange(branch, both_cores)
     return kernel(add_kernel, jax.ShapeDtypeStruct(coeffs.shape, BF16), [VMEM, VMEM])(parts, coeffs).T
 
 

time: 72.9 us -> 72.5 us (level)
  no operation moved by 1% of the time
where the time goes in v7:
time: 72.5 us; the launch traced here: 72.1 us
  starting transfers between devices  39.8 us (55%)
  blocking collectives  23.2 us (32%)
  Pallas kernels  6.1 us (8%)
  waiting for transfers between devices  2.9 us (4%)
    all_to_all x2, starting transfers between devices, exchange(): return lax.all_to_all(x, 'seq', 0, 0, axis_index_groups=groups)  33.1 us
    all_to_all x1, blocking collectives, exchange(): return lax.all_to_all(x, 'seq', 0, 0, axis_index_groups=groups)  19.9 us
    all_gather x1, blocking collectives, gather_pair(): return lax.all_gather(x, 'seq', axis_index_groups=pairs)  3.35 us
    all_to_all x2, waiting for transfers between devices, exchange(): return lax.all_to_all(x, 'seq', 0, 0, axis_index_groups=groups)  2.89 us
    pallas_call x1, Pallas kernels, local(): kernel(moments_kernel, jax.ShapeDtypeStruct((width // 8, 128), F32), [ANY...  2.86 us
    ppermute x1, starting transfers between devices, local(): lax.ppermute(own, 'seq', other_core)  2.54 us
    ppermute x1, starting transfers between devices, local(): beside = lax.ppermute(own, 'seq', [(i, i ^ 2) for i in range(windows)])  2.2 us
    ppermute x1, starting transfers between devices, local(): lax.ppermute(beside, 'seq', other_core)  1.92 us
  transfers between devices with their start and end apart: 5, of which 2 were waited for; matrix products, arithmetic and copies ran while one was open for 0% of the time, Pallas kernels for 2%

profile of v7, /device:TPU:1, one launch (start us, length us, event | category | flops | bytes accessed | tf_op | source)
XLA Modules:
  0.0 72.1 jit_solution(2683728782212859219)
XLA Ops:
  0.0 0.0 copy-start.3
  0.0 0.0 copy-start.1
  0.0 2.9 %shard_map.64 = f32[256,128]{1,0:T(8,128)} custom-call(bf16[32,512]{1,0:T(8,128)(2,1)} %constant.23.clone.project_hbm, bf16[512,2048]{1,0:T(8,128)(2,1)} %rows_hbm.1), custom_call_target="tpu_custom_call" | custom-call | tf_op jit(solution)/shard_map/pallas_call | solution.py:174
  2.9 20.1 %all-to-all-start = ((f32[64,4,128]{2,1,0:T(4,128)}), f32[64,4,128]{2,1,0:T(4,128)S(1)}, u32[]{:S(2)}, u32[]{:S(2)}) async-start(f32[64,4,128]{2,1,0:T(4,128)} %bitcast.9), calls=%async_computation | async-start | bytes 262144 | tf_op jit(solution)/shard_map/all_to_all | solution.py:159
  23.0 0.0 copy-done.2
  23.0 0.0 copy-done.1
  23.0 2.2 %collective-permute-start = (bf16[128,2048]{1,0:T(8,128)(2,1)S(1)}, bf16[128,2048]{1,0:T(8,128)(2,1)S(1)}, u32[]{:S(2)}, u32[]{:S(2)}) collective-permute-start(bf16[128,2048]{1,0:T(8,128)(2,1)S(1)} %shard_map.68.refs_0_), channel_id=1, source_target_pairs={{0,2},{1,3},{2,0},{3,1},{4,6},{5,7},{6,4},{7,5},{8,10},{9,11},{10,... | collective-permute-start | bytes 1572872 | tf_op jit(solution)/shard_map/ppermute | solution.py:189
  25.3 0.5 all-to-all-done
  25.8 0.0 copy-done.3
  25.8 0.0 copy-done
  25.8 0.3 shard_map.65
  26.1 3.4 %all-gather = f32[64,256]{1,0:T(8,128)S(1)} all-gather(f32[32,256]{1,0:T(8,128)S(1)} %shard_map.65), channel_id=2, replica_groups={{0,1},{2,3},{4,5},{6,7},{8,9},{10,11},{12,13},{14,15},{16,17},{18,19},{..., dimensions={0}, use_global_device_ids=true | all-gather | bytes 98304 | tf_op jit(solution)/shard_map/all_gather | solution.py:162
  29.5 0.8 %shard_map.66 = (bf16[16,256]{1,0:T(8,128)(2,1)S(1)}, bf16[64,16,128]{2,1,0:T(8,128)(2,1)}) custom-call(s32[1]{0:T(128)} %bitcast.core_ref, f32[2,32,256]{2,1,0:T(8,128)S(1)} %bitcast.7), custom_call_target="tpu_custom_call" | custom-call | tf_op jit(solution)/shard_map/pallas_call | solution.py:196
  30.3 13.0 %all-to-all-start.1 = ((bf16[64,16,128]{2,1,0:T(8,128)(2,1)}), bf16[64,16,128]{2,1,0:T(8,128)(2,1)S(1)}, u32[]{:S(2)}, u32[]{:S(2)}) async-start(bf16[64,16,128]{2,1,0:T(8,128)(2,1)} %get-tuple-element.7), calls=%async_computation.1 | async-start | bytes 524288 | tf_op jit(solution)/shard_map/all_to_all | solution.py:159
  43.3 2.5 %collective-permute-start.1 = (bf16[128,2048]{1,0:T(8,128)(2,1)S(1)}, bf16[128,2048]{1,0:T(8,128)(2,1)S(1)}, u32[]{:S(2)}, u32[]{:S(2)}) collective-permute-start(bf16[128,2048]{1,0:T(8,128)(2,1)S(1)} %shard_map.68.refs_0_), channel_id=1, source_target_pairs={{0,1},{1,0},{2,3},{3,2},{4,5},{5,4},{6,7},{7,6},{8,9},{9,8},{10,11... | collective-permute-start | bytes 1572872 | tf_op jit(solution)/shard_map/ppermute | solution.py:191
  45.9 0.0 collective-permute-done.refs_1_
  45.9 1.9 %collective-permute-start.2 = (bf16[128,2048]{1,0:T(8,128)(2,1)S(1)}, bf16[128,2048]{1,0:T(8,128)(2,1)S(1)}, u32[]{:S(2)}, u32[]{:S(2)}) collective-permute-start(bf16[128,2048]{1,0:T(8,128)(2,1)S(1)} %collective-permute-done.refs_1_), channel_id=1, source_target_pairs={{0,1},{1,0},{2,3},{3,2},{4,5},{5,4},{6,7},{7,6},{8,9},{9,8},{10,11... | collective-permute-start | bytes 1572872 | tf_op jit(solution)/shard_map/ppermute | solution.py:191
  47.8 2.4 %all-to-all-done.1.packed_ref = bf16[64,16,128]{2,1,0:T(8,128)(2,1)S(1)} async-done(((bf16[64,16,128]{2,1,0:T(8,128)(2,1)}), bf16[64,16,128]{2,1,0:T(8,128)(2,1)S(1)}, u32[]{:S(2)}, u32[]{:S(2)}) %all-to-all-start.1) | async-done | bytes 262176 | tf_op jit(solution)/shard_map/all_to_all | solution.py:159
  50.2 0.2 shard_map.67.scale_ref
  50.4 0.0 collective-permute-done.1.refs_2_
  50.4 0.0 collective-permute-done.2.refs_3_
  50.4 1.1 %shard_map.69 = bf16[128,8,128]{2,1,0:T(8,128)(2,1)S(1)} custom-call(bf16[64,16,128]{2,1,0:T(8,128)(2,1)S(1)} %all-to-all-done.1.packed_ref, f32[1,128]{1,0:T(1,128)S(1)} %shard_map.67.scale_ref, bf16[128,2048]{1,0:T(8,128)(2,1)S(1)} %shard_map.68.refs_0_, bf16[128,2048]{1,0:T(8,128)(2,1)S(1)} %collective-permute-done.refs_1_, ...), custom_call_target="tpu_custom_call" | custom-call | tf_op jit(solution)/shard_map/pallas_call | solution.py:211
  51.5 19.9 %all_to_all.15.parts_ref = bf16[128,8,128]{2,1,0:T(8,128)(2,1)S(1)} all-to-all(bf16[128,8,128]{2,1,0:T(8,128)(2,1)S(1)} %shard_map.69), channel_id=1, replica_groups={{73,72,75,74,77,76,79,78,81,80,83,82,85,84,87,86,89,88,91,90,93,92,95,9..., dimensions={0} | all-to-all | bytes 524288 | tf_op jit(solution)/shard_map/all_to_all | solution.py:159
  71.4 0.7 shard_map.70
  (3 shorter events, 0.0 us)
Async XLA Ops:
  0.0 25.8 %copy-start.3 = (f32[16,256]{1,0:T(8,128)S(1)}, f32[16,256]{1,0:T(8,128)}, u32[]{:S(2)}) copy-start(f32[16,256]{1,0:T(8,128)} %constant.25.clone.expand_ref) | copy-start | bytes 49156
  0.0 25.8 %copy-start = (bf16[2,256,512]{2,1,0:T(8,128)(2,1)S(1)}, bf16[2,256,512]{2,1,0:T(8,128)(2,1)}, u32[]{:S(2)}) copy-start(bf16[2,256,512]{2,1,0:T(8,128)(2,1)} %constant.24.clone.trig_ref) | copy-start | bytes 1572868
  0.0 23.0 %copy-start.2 = (bf16[64,2048]{1,0:T(8,128)(2,1)S(1)}, bf16[64,2048]{1,0:T(8,128)(2,1)}, u32[]{:S(2)}) copy-start(bf16[64,2048]{1,0:T(8,128)(2,1)} %contract_ref.1) | copy-start | bytes 786436
  0.0 23.0 %copy-start.1 = (bf16[2048,64]{0,1:T(8,128)(2,1)S(1)}, bf16[2048,64]{0,1:T(8,128)(2,1)}, u32[]{:S(2)}) copy-start(bf16[2048,64]{0,1:T(8,128)(2,1)} %param.7) | copy-start | bytes 786436
  2.9 22.9 %all-to-all-start = ((f32[64,4,128]{2,1,0:T(4,128)}), f32[64,4,128]{2,1,0:T(4,128)S(1)}, u32[]{:S(2)}, u32[]{:S(2)}) async-start(f32[64,4,128]{2,1,0:T(4,128)} %bitcast.9), calls=%async_computation | async-start | bytes 262144 | tf_op jit(solution)/shard_map/all_to_all | solution.py:159
  23.0 22.8 %collective-permute-start = (bf16[128,2048]{1,0:T(8,128)(2,1)S(1)}, bf16[128,2048]{1,0:T(8,128)(2,1)S(1)}, u32[]{:S(2)}, u32[]{:S(2)}) collective-permute-start(bf16[128,2048]{1,0:T(8,128)(2,1)S(1)} %shard_map.68.refs_0_), channel_id=1, source_target_pairs={{0,2},{1,3},{2,0},{3,1},{4,6},{5,7},{6,4},{7,5},{8,10},{9,11},{10,... | collective-permute-start | bytes 1572872 | tf_op jit(solution)/shard_map/ppermute | solution.py:189
  30.3 19.9 %all-to-all-start.1 = ((bf16[64,16,128]{2,1,0:T(8,128)(2,1)}), bf16[64,16,128]{2,1,0:T(8,128)(2,1)S(1)}, u32[]{:S(2)}, u32[]{:S(2)}) async-start(bf16[64,16,128]{2,1,0:T(8,128)(2,1)} %get-tuple-element.7), calls=%async_computation.1 | async-start | bytes 524288 | tf_op jit(solution)/shard_map/all_to_all | solution.py:159
  43.3 7.1 %collective-permute-start.1 = (bf16[128,2048]{1,0:T(8,128)(2,1)S(1)}, bf16[128,2048]{1,0:T(8,128)(2,1)S(1)}, u32[]{:S(2)}, u32[]{:S(2)}) collective-permute-start(bf16[128,2048]{1,0:T(8,128)(2,1)S(1)} %shard_map.68.refs_0_), channel_id=1, source_target_pairs={{0,1},{1,0},{2,3},{3,2},{4,5},{5,4},{6,7},{7,6},{8,9},{9,8},{10,11... | collective-permute-start | bytes 1572872 | tf_op jit(solution)/shard_map/ppermute | solution.py:191
  45.9 4.5 %collective-permute-start.2 = (bf16[128,2048]{1,0:T(8,128)(2,1)S(1)}, bf16[128,2048]{1,0:T(8,128)(2,1)S(1)}, u32[]{:S(2)}, u32[]{:S(2)}) collective-permute-start(bf16[128,2048]{1,0:T(8,128)(2,1)S(1)} %collective-permute-done.refs_1_), channel_id=1, source_target_pairs={{0,1},{1,0},{2,3},{3,2},{4,5},{5,4},{6,7},{7,6},{8,9},{9,8},{10,11... | collective-permute-start | bytes 1572872 | tf_op jit(solution)/shard_map/ppermute | solution.py:191

commit v8 on v7

--- a/solution.py
+++ b/solution.py
@@ -17,13 +17,17 @@
 ANY = pl.BlockSpec(memory_space=pl.ANY)
 
 
+def group_order(chips, group):
+    return [(TURN + i) % chips ^ (1 - group) for i in range(chips)]
+
+
 def split_halves(array):
     high = np.asarray(array, np.float32).astype(jnp.bfloat16)
     low = (np.asarray(array, np.float64) - high.astype(np.float64)).astype(jnp.bfloat16)
     return high, low
 
 
-def window_tables(rows, windows, turn):
+def window_tables(rows, windows):
     t = (2.0 * np.arange(rows) + 1.0 - rows) / rows
     basis, _ = np.linalg.qr(np.polynomial.chebyshev.chebvander(t, MOMENTS - 1))
     basis = basis[:, list(range(0, MOMENTS, 2)) + list(range(1, MOMENTS, 2))]
@@ -37,16 +41,18 @@
     project = np.concatenate([high, low], axis=0)
     theta = np.pi * np.outer(2 * np.arange(windows) + 1, k) / (2 * windows)
     trig = np.concatenate([np.cos(theta), np.sin(theta)], axis=1)
-    trig = np.roll(trig.reshape(windows // 2, 2, 2 * KEEP), -turn, axis=0).transpose(1, 0, 2)
+    orders = [group_order(windows // 2, group) for group in range(2)]
+    rows_of = [[2 * chip + (chip % 2 ^ group) for chip in order] for group, order in enumerate(orders)]
+    trig = trig[np.asarray(rows_of)]
     high, low = split_halves(trig)
     return project, expand, np.concatenate([high, low, high, low], axis=1)
 
 
-def moments_kernel(project_hbm, rows_hbm, out_ref, project_ref, held, loaded):
-    steps, _, columns = held.shape
+def moments_kernel(group_ref, project_hbm, rows_hbm, out_ref, project_ref, held, loaded):
+    steps, count, columns = held.shape
     first = pltpu.make_async_copy(project_hbm, project_ref, loaded.at[steps])
     loads = [
-        pltpu.make_async_copy(rows_hbm.at[:, pl.ds(step * columns, columns)], held.at[step], loaded.at[step])
+        pltpu.make_async_copy(rows_hbm.at[pl.ds(step * count, count)], held.at[step], loaded.at[step])
         for step in range(steps)
     ]
     for copy in [first] + loads:
@@ -54,21 +60,24 @@
     row = lax.broadcasted_iota(jnp.int32, (128, 128), 0) % 8
     lane = lax.broadcasted_iota(jnp.int32, (128, 128), 1) // MOMENTS
     first.wait()
-    project = project_ref[...]
+    both = jnp.zeros((2 * MOMENTS, columns), F32)
     for step in range(steps):
         loads[step].wait()
-        both = jnp.dot(project, held[step], preferred_element_type=F32)
-        moments = both[:MOMENTS] + both[MOMENTS:]
-        spread = jnp.concatenate([moments] * 8, axis=0)
-        for block in range(columns // 128):
-            turned = spread[:, 128 * block : 128 * (block + 1)].T
-            packed = jnp.where(row == lane, turned, 0.0).reshape(16, 8, 128).sum(axis=1)
-            top = (step * columns // 8 + 16 * block - 4 * TURN) % out_ref.shape[0]
-            out_ref[top : top + 16, :] = packed
-
-
-def coeffs_kernel(core_ref, moments_ref, trig_ref, expand_ref, out_ref):
-    trig = trig_ref[core_ref[0]]
+        part = project_ref[:, step * count : (step + 1) * count]
+        both += jnp.dot(part, held[step], preferred_element_type=F32)
+    moments = both[:MOMENTS] + both[MOMENTS:]
+    spread = jnp.concatenate([moments] * 8, axis=0)
+    for block in range(columns // 128):
+        turned = spread[:, 128 * block : 128 * (block + 1)].T
+        packed = jnp.where(row == lane, turned, 0.0).reshape(16, 8, 128).sum(axis=1)
+        pairs = packed.reshape(2, 2, 4, 128)
+        swapped = jnp.stack([pairs[:, 1], pairs[:, 0]], axis=1).reshape(16, 128)
+        top = (16 * block - 4 * TURN) % out_ref.shape[0]
+        out_ref[top : top + 16, :] = jnp.where(group_ref[0] == 0, swapped, packed)
+
+
+def coeffs_kernel(group_ref, moments_ref, trig_ref, expand_ref, out_ref):
+    trig = trig_ref[group_ref[0]]
     sources = trig.shape[0] // 4
     expand = expand_ref[...]
     half = MOMENTS // 2
@@ -83,16 +92,19 @@
         out_ref[8 * part : 8 * (part + 1), :] = (even * expand[:half] + odd * expand[half:]).sum(axis=1)
 
 
-def spread_kernel(core_ref, both_ref, coeffs_ref, out_ref):
+def spread_kernel(core_ref, group_ref, both_ref, coeffs_ref, out_ref):
     total = both_ref[0] + both_ref[1]
     half = total.shape[1] // 2
-    mine = jnp.where(core_ref[0] == 0, total[:, :half], total[:, half:])
     coeffs_ref[...] = jnp.where(core_ref[0] == 0, total[:16], total[16:]).astype(BF16)
-    low, high = mine[:16], mine[16:]
-    left = lax.broadcasted_iota(jnp.int32, low.shape, 1) < half // 2
-    first = jnp.where(left, low, pltpu.roll(high, half // 2, 1)).astype(BF16)
-    second = jnp.where(left, pltpu.roll(low, half // 2, 1), high).astype(BF16)
-    pair = jnp.stack([first, second])
+    left = lax.broadcasted_iota(jnp.int32, (16, half), 1) < half // 2
+
+    def quarter(core, parity):
+        low, high = total[:16, half * core : half * (core + 1)], total[16:, half * core : half * (core + 1)]
+        even = jnp.where(left, low, pltpu.roll(high, half // 2, 1))
+        odd = jnp.where(left, pltpu.roll(low, half // 2, 1), high)
+        return jnp.where(parity == 0, even, odd).astype(BF16)
+
+    pair = jnp.stack([quarter(1, 1 - group_ref[0]), quarter(0, group_ref[0])])
     out_ref[...] = jnp.broadcast_to(pair[None], (out_ref.shape[0] // 2,) + pair.shape).reshape(out_ref.shape)
 
 
@@ -110,10 +122,13 @@
     scale_ref[...] = lax.rsqrt(sums / (wide.size // (lanes // 2)) + 1e-06)
 
 
-def feed_forward_kernel(packed_ref, scale_ref, *refs):
+def feed_forward_kernel(group_ref, packed_ref, scale_ref, *refs):
     weights, out_ref = refs[:-1], refs[-1]
     units = weights[0].shape[0] // 2
     packed = jnp.concatenate([packed_ref[-TURN:], packed_ref[:-TURN]], axis=0)
+    pairs = packed.reshape((packed.shape[0] // 2, 2) + packed.shape[1:])
+    swapped = jnp.stack([pairs[:, 1], pairs[:, 0]], axis=1).reshape(packed.shape)
+    packed = jnp.where(group_ref[0] == 0, swapped, packed)
     kept = packed.shape[2] // 2
     width = packed.shape[0] * 32
     coeffs = jnp.concatenate([packed[:, :, :kept], packed[:, :, kept:]], axis=1).reshape(width, kept)
@@ -148,14 +163,14 @@
     windows = lax.axis_size("seq")
     chips = windows // 2
     mine = width // chips
-    project, expand, trig = window_tables(rows, windows, TURN)
+    project, expand, trig = window_tables(rows, windows)
     pairs = [[2 * chip, 2 * chip + 1] for chip in range(chips)]
     core = lax.axis_index("seq") % 2
 
-    same_core = [[(2 * TURN + i) % windows for i in range(core, windows, 2)] for core in range(2)]
+    mixed = [[2 * chip + (chip % 2 ^ group) for chip in group_order(chips, group)] for group in range(2)]
     both_cores = [[(2 * TURN + i) % windows ^ 1 for i in range(windows)]]
 
-    def exchange(x, groups=same_core):
+    def exchange(x, groups=mixed):
         return lax.all_to_all(x, "seq", 0, 0, axis_index_groups=groups)
 
     def gather_pair(x):
@@ -171,17 +186,18 @@
         )
 
     core_index = core.astype(jnp.int32).reshape(1)
+    group_index = ((lax.axis_index("seq") // 2 + core) % 2).astype(jnp.int32).reshape(1)
     moments = kernel(
         moments_kernel,
         jax.ShapeDtypeStruct((width // 8, 128), F32),
-        [ANY, ANY],
+        [SMEM, ANY, ANY],
         vmem=60,
         scratch_shapes=[
             pltpu.VMEM(project.shape, BF16),
-            pltpu.VMEM((2, rows, width // 2), BF16),
-            pltpu.SemaphoreType.DMA((3,)),
+            pltpu.VMEM((4, rows // 4, width), BF16),
+            pltpu.SemaphoreType.DMA((5,)),
         ],
-    )(jnp.asarray(project), hidden_rows)
+    )(group_index, jnp.asarray(project), hidden_rows)
     received = exchange(moments.reshape(chips, -1, 128)).reshape(-1, 128)
     own = kernel(
         stack_kernel, jax.ShapeDtypeStruct((2 * w_contract.shape[0], width), BF16), [VMEM, VMEM]
@@ -191,7 +207,7 @@
     weights = [own, beside, lax.ppermute(own, "seq", other_core), lax.ppermute(beside, "seq", other_core)]
     partial = kernel(
         coeffs_kernel, jax.ShapeDtypeStruct((mine, KEEP), F32), [SMEM, VMEM, VMEM, VMEM]
-    )(core_index, received, jnp.asarray(trig), jnp.asarray(expand))
+    )(group_index, received, jnp.asarray(trig), jnp.asarray(expand))
     both = gather_pair(partial)
     coeffs, spread = kernel(
         spread_kernel,
@@ -199,8 +215,8 @@
             jax.ShapeDtypeStruct((mine // 2, KEEP), BF16),
             jax.ShapeDtypeStruct((chips, mine // 2, KEEP // 2), BF16),
         ],
-        [SMEM, VMEM],
-    )(core_index, both)
+        [SMEM, SMEM, VMEM],
+    )(core_index, group_index, both)
     gathered = exchange(spread)
     scale = kernel(
         scale_kernel,
@@ -209,8 +225,8 @@
         cost_estimate=pl.CostEstimate(flops=2 * 10**10, bytes_accessed=1 << 20, transcendentals=0),
     )(gathered)
     branch = kernel(
-        feed_forward_kernel, jax.ShapeDtypeStruct((windows, mine // 4, KEEP // 2), BF16), [VMEM] * 6
-    )(gathered, scale, *weights)
+        feed_forward_kernel, jax.ShapeDtypeStruct((windows, mine // 4, KEEP // 2), BF16), [SMEM] + [VMEM] * 6
+    )(group_index, gathered, scale, *weights)
     parts = exchange(branch, both_cores)
     return kernel(add_kernel, jax.ShapeDtypeStruct(coeffs.shape, BF16), [VMEM, VMEM])(parts, coeffs).T
 

time: 72.5 us -> 72.3 us (level)
  waiting for transfers between devices: 2.9 us -> 4.4 us
  blocking collectives: 23.2 us -> 22.2 us
    all_to_all x2, waiting for transfers between devices: 2.89 us -> 4.39 us  [exchange(): return lax.all_to_all(x, 'seq', 0, 0, axis_index_groups=groups)]
    all_gather x1, blocking collectives: 3.35 us -> 2.15 us  [gather_pair(): return lax.all_gather(x, 'seq', axis_index_groups=pairs)]
where the time goes in v8:
time: 72.3 us; the launch traced here: 72 us
  starting transfers between devices  39.1 us (54%)
  blocking collectives  22.2 us (31%)
  Pallas kernels  6.13 us (8%)
  waiting for transfers between devices  4.4 us (6%)
    all_to_all x2, starting transfers between devices, exchange(): return lax.all_to_all(x, 'seq', 0, 0, axis_index_groups=groups)  32.9 us
    all_to_all x1, blocking collectives, exchange(): return lax.all_to_all(x, 'seq', 0, 0, axis_index_groups=groups)  20 us
    all_to_all x2, waiting for transfers between devices, exchange(): return lax.all_to_all(x, 'seq', 0, 0, axis_index_groups=groups)  4.39 us
    pallas_call x1, Pallas kernels, local(): kernel(moments_kernel, jax.ShapeDtypeStruct((width // 8, 128), F32), [SME...  2.87 us
    ppermute x1, starting transfers between devices, local(): lax.ppermute(beside, 'seq', other_core)  2.41 us
    all_gather x1, blocking collectives, gather_pair(): return lax.all_gather(x, 'seq', axis_index_groups=pairs)  2.15 us
    ppermute x1, starting transfers between devices, local(): beside = lax.ppermute(own, 'seq', [(i, i ^ 2) for i in range(windows)])  1.92 us
    ppermute x1, starting transfers between devices, local(): lax.ppermute(own, 'seq', other_core)  1.92 us
  transfers between devices with their start and end apart: 5, of which 2 were waited for; matrix products, arithmetic and copies ran while one was open for 0% of the time, Pallas kernels for 2%

profile of v8, /device:TPU:1, one launch (start us, length us, event | category | flops | bytes accessed | tf_op | source)
XLA Modules:
  0.0 72.0 jit_solution(3933440695969373307)
XLA Ops:
  0.0 0.0 copy-start.3
  0.0 0.0 copy-start.1
  0.1 2.9 %shard_map.64 = f32[256,128]{1,0:T(8,128)} custom-call(s32[1]{0:T(128)} %bitcast.group_ref, bf16[32,512]{1,0:T(8,128)(2,1)} %constant.38.clone.project_hbm, bf16[512,2048]{1,0:T(8,128)(2,1)} %rows_hbm.1), custom_call_target="tpu_custom_call" | custom-call | tf_op jit(solution)/shard_map/pallas_call | solution.py:190
  2.9 20.6 %all-to-all-start = ((f32[64,4,128]{2,1,0:T(4,128)}), f32[64,4,128]{2,1,0:T(4,128)S(1)}, u32[]{:S(2)}, u32[]{:S(2)}) async-start(f32[64,4,128]{2,1,0:T(4,128)} %bitcast.10), calls=%async_computation | async-start | bytes 262144 | tf_op jit(solution)/shard_map/all_to_all | solution.py:174
  23.6 0.0 copy-done.2
  23.6 0.0 copy-done.1
  23.7 1.9 %collective-permute-start = (bf16[128,2048]{1,0:T(8,128)(2,1)S(1)}, bf16[128,2048]{1,0:T(8,128)(2,1)S(1)}, u32[]{:S(2)}, u32[]{:S(2)}) collective-permute-start(bf16[128,2048]{1,0:T(8,128)(2,1)S(1)} %shard_map.68.refs_0_), channel_id=1, source_target_pairs={{0,2},{1,3},{2,0},{3,1},{4,6},{5,7},{6,4},{7,5},{8,10},{9,11},{10,... | collective-permute-start | bytes 1572872 | tf_op jit(solution)/shard_map/ppermute | solution.py:205
  25.6 2.0 %all-to-all-done = f32[64,4,128]{2,1,0:T(4,128)S(1)} async-done(((f32[64,4,128]{2,1,0:T(4,128)}), f32[64,4,128]{2,1,0:T(4,128)S(1)}, u32[]{:S(2)}, u32[]{:S(2)}) %all-to-all-start) | async-done | bytes 131104 | tf_op jit(solution)/shard_map/all_to_all | solution.py:174
  27.6 0.0 copy-done.3
  27.6 0.0 copy-done
  27.6 0.3 shard_map.65
  27.9 2.1 %all-gather = f32[64,256]{1,0:T(8,128)S(1)} all-gather(f32[32,256]{1,0:T(8,128)S(1)} %shard_map.65), channel_id=2, replica_groups={{0,1},{2,3},{4,5},{6,7},{8,9},{10,11},{12,13},{14,15},{16,17},{18,19},{..., dimensions={0}, use_global_device_ids=true | all-gather | bytes 98304 | tf_op jit(solution)/shard_map/all_gather | solution.py:177
  30.1 0.8 %shard_map.66 = (bf16[16,256]{1,0:T(8,128)(2,1)S(1)}, bf16[64,16,128]{2,1,0:T(8,128)(2,1)}) custom-call(s32[1]{0:T(128)} %bitcast.1.core_ref, s32[1]{0:T(128)} %bitcast.group_ref, f32[2,32,256]{2,1,0:T(8,128)S(1)} %bitcast.8), custom_call_target="tpu_custom_call" | custom-call | tf_op jit(solution)/shard_map/pallas_call | solution.py:212
  30.9 12.2 %all-to-all-start.1 = ((bf16[64,16,128]{2,1,0:T(8,128)(2,1)}), bf16[64,16,128]{2,1,0:T(8,128)(2,1)S(1)}, u32[]{:S(2)}, u32[]{:S(2)}) async-start(bf16[64,16,128]{2,1,0:T(8,128)(2,1)} %get-tuple-element.7), calls=%async_computation.1 | async-start | bytes 524288 | tf_op jit(solution)/shard_map/all_to_all | solution.py:174
  43.1 1.9 %collective-permute-start.1 = (bf16[128,2048]{1,0:T(8,128)(2,1)S(1)}, bf16[128,2048]{1,0:T(8,128)(2,1)S(1)}, u32[]{:S(2)}, u32[]{:S(2)}) collective-permute-start(bf16[128,2048]{1,0:T(8,128)(2,1)S(1)} %shard_map.68.refs_0_), channel_id=1, source_target_pairs={{0,1},{1,0},{2,3},{3,2},{4,5},{5,4},{6,7},{7,6},{8,9},{9,8},{10,11... | collective-permute-start | bytes 1572872 | tf_op jit(solution)/shard_map/ppermute | solution.py:207
  45.0 0.0 collective-permute-done.refs_1_
  45.0 2.4 %collective-permute-start.2 = (bf16[128,2048]{1,0:T(8,128)(2,1)S(1)}, bf16[128,2048]{1,0:T(8,128)(2,1)S(1)}, u32[]{:S(2)}, u32[]{:S(2)}) collective-permute-start(bf16[128,2048]{1,0:T(8,128)(2,1)S(1)} %collective-permute-done.refs_1_), channel_id=1, source_target_pairs={{0,1},{1,0},{2,3},{3,2},{4,5},{5,4},{6,7},{7,6},{8,9},{9,8},{10,11... | collective-permute-start | bytes 1572872 | tf_op jit(solution)/shard_map/ppermute | solution.py:207
  47.4 2.4 %all-to-all-done.1.packed_ref = bf16[64,16,128]{2,1,0:T(8,128)(2,1)S(1)} async-done(((bf16[64,16,128]{2,1,0:T(8,128)(2,1)}), bf16[64,16,128]{2,1,0:T(8,128)(2,1)S(1)}, u32[]{:S(2)}, u32[]{:S(2)}) %all-to-all-start.1) | async-done | bytes 262176 | tf_op jit(solution)/shard_map/all_to_all | solution.py:174
  49.9 0.2 shard_map.67.scale_ref
  50.1 0.0 collective-permute-done.1.refs_2_
  50.1 0.0 collective-permute-done.2.refs_3_
  50.1 1.1 %shard_map.69 = bf16[128,8,128]{2,1,0:T(8,128)(2,1)S(1)} custom-call(s32[1]{0:T(128)} %bitcast.group_ref, bf16[64,16,128]{2,1,0:T(8,128)(2,1)S(1)} %all-to-all-done.1.packed_ref, f32[1,128]{1,0:T(1,128)S(1)} %shard_map.67.scale_ref, bf16[128,2048]{1,0:T(8,128)(2,1)S(1)} %shard_map.68.refs_0_, bf16[128,2048]{1,0:T(8,128)(2,1)S(1)} %collective-permute-done.refs_1_, ...), custom_call_target="tpu_custom_call" | custom-call | tf_op jit(solution)/shard_map/pallas_call | solution.py:227
  51.2 20.0 %all_to_all.15.parts_ref = bf16[128,8,128]{2,1,0:T(8,128)(2,1)S(1)} all-to-all(bf16[128,8,128]{2,1,0:T(8,128)(2,1)S(1)} %shard_map.69), channel_id=1, replica_groups={{73,72,75,74,77,76,79,78,81,80,83,82,85,84,87,86,89,88,91,90,93,92,95,9..., dimensions={0} | all-to-all | bytes 524288 | tf_op jit(solution)/shard_map/all_to_all | solution.py:174
  71.3 0.7 shard_map.70
  (3 shorter events, 0.0 us)
Async XLA Ops:
  0.0 27.6 %copy-start.3 = (f32[16,256]{1,0:T(8,128)S(1)}, f32[16,256]{1,0:T(8,128)}, u32[]{:S(2)}) copy-start(f32[16,256]{1,0:T(8,128)} %constant.40.clone.expand_ref) | copy-start | bytes 49156
  0.0 27.6 %copy-start = (bf16[2,256,512]{2,1,0:T(8,128)(2,1)S(1)}, bf16[2,256,512]{2,1,0:T(8,128)(2,1)}, u32[]{:S(2)}) copy-start(bf16[2,256,512]{2,1,0:T(8,128)(2,1)} %constant.39.clone.trig_ref) | copy-start | bytes 1572868
  0.0 23.6 %copy-start.2 = (bf16[64,2048]{1,0:T(8,128)(2,1)S(1)}, bf16[64,2048]{1,0:T(8,128)(2,1)}, u32[]{:S(2)}) copy-start(bf16[64,2048]{1,0:T(8,128)(2,1)} %contract_ref.1) | copy-start | bytes 786436
  0.0 23.6 %copy-start.1 = (bf16[2048,64]{0,1:T(8,128)(2,1)S(1)}, bf16[2048,64]{0,1:T(8,128)(2,1)}, u32[]{:S(2)}) copy-start(bf16[2048,64]{0,1:T(8,128)(2,1)} %param.7) | copy-start | bytes 786436
  2.9 24.6 %all-to-all-start = ((f32[64,4,128]{2,1,0:T(4,128)}), f32[64,4,128]{2,1,0:T(4,128)S(1)}, u32[]{:S(2)}, u32[]{:S(2)}) async-start(f32[64,4,128]{2,1,0:T(4,128)} %bitcast.10), calls=%async_computation | async-start | bytes 262144 | tf_op jit(solution)/shard_map/all_to_all | solution.py:174
  23.7 21.4 %collective-permute-start = (bf16[128,2048]{1,0:T(8,128)(2,1)S(1)}, bf16[128,2048]{1,0:T(8,128)(2,1)S(1)}, u32[]{:S(2)}, u32[]{:S(2)}) collective-permute-start(bf16[128,2048]{1,0:T(8,128)(2,1)S(1)} %shard_map.68.refs_0_), channel_id=1, source_target_pairs={{0,2},{1,3},{2,0},{3,1},{4,6},{5,7},{6,4},{7,5},{8,10},{9,11},{10,... | collective-permute-start | bytes 1572872 | tf_op jit(solution)/shard_map/ppermute | solution.py:205
  30.9 19.0 %all-to-all-start.1 = ((bf16[64,16,128]{2,1,0:T(8,128)(2,1)}), bf16[64,16,128]{2,1,0:T(8,128)(2,1)S(1)}, u32[]{:S(2)}, u32[]{:S(2)}) async-start(bf16[64,16,128]{2,1,0:T(8,128)(2,1)} %get-tuple-element.7), calls=%async_computation.1 | async-start | bytes 524288 | tf_op jit(solution)/shard_map/all_to_all | solution.py:174
  43.1 7.0 %collective-permute-start.1 = (bf16[128,2048]{1,0:T(8,128)(2,1)S(1)}, bf16[128,2048]{1,0:T(8,128)(2,1)S(1)}, u32[]{:S(2)}, u32[]{:S(2)}) collective-permute-start(bf16[128,2048]{1,0:T(8,128)(2,1)S(1)} %shard_map.68.refs_0_), channel_id=1, source_target_pairs={{0,1},{1,0},{2,3},{3,2},{4,5},{5,4},{6,7},{7,6},{8,9},{9,8},{10,11... | collective-permute-start | bytes 1572872 | tf_op jit(solution)/shard_map/ppermute | solution.py:207
  45.0 5.0 %collective-permute-start.2 = (bf16[128,2048]{1,0:T(8,128)(2,1)S(1)}, bf16[128,2048]{1,0:T(8,128)(2,1)S(1)}, u32[]{:S(2)}, u32[]{:S(2)}) collective-permute-start(bf16[128,2048]{1,0:T(8,128)(2,1)S(1)} %collective-permute-done.refs_1_), channel_id=1, source_target_pairs={{0,1},{1,0},{2,3},{3,2},{4,5},{5,4},{6,7},{7,6},{8,9},{9,8},{10,11... | collective-permute-start | bytes 1572872 | tf_op jit(solution)/shard_map/ppermute | solution.py:207

commit v9 on v8

--- a/solution.py
+++ b/solution.py
@@ -49,11 +49,11 @@
 
 
 def moments_kernel(group_ref, project_hbm, rows_hbm, out_ref, project_ref, held, loaded):
-    steps, count, columns = held.shape
-    first = pltpu.make_async_copy(project_hbm, project_ref, loaded.at[steps])
+    count, columns = held.shape
+    blocks = [slice(0, count // 2), slice(count // 2, 3 * count // 4), slice(3 * count // 4, count)]
+    first = pltpu.make_async_copy(project_hbm, project_ref, loaded.at[len(blocks)])
     loads = [
-        pltpu.make_async_copy(rows_hbm.at[pl.ds(step * count, count)], held.at[step], loaded.at[step])
-        for step in range(steps)
+        pltpu.make_async_copy(rows_hbm.at[block], held.at[block], loaded.at[step]) for step, block in enumerate(blocks)
     ]
     for copy in [first] + loads:
         copy.start()
@@ -61,10 +61,9 @@
     lane = lax.broadcasted_iota(jnp.int32, (128, 128), 1) // MOMENTS
     first.wait()
     both = jnp.zeros((2 * MOMENTS, columns), F32)
-    for step in range(steps):
-        loads[step].wait()
-        part = project_ref[:, step * count : (step + 1) * count]
-        both += jnp.dot(part, held[step], preferred_element_type=F32)
+    for load, block in zip(loads, blocks):
+        load.wait()
+        both += jnp.dot(project_ref[:, block], held[block], preferred_element_type=F32)
     moments = both[:MOMENTS] + both[MOMENTS:]
     spread = jnp.concatenate([moments] * 8, axis=0)
     for block in range(columns // 128):
@@ -194,8 +193,8 @@
         vmem=60,
         scratch_shapes=[
             pltpu.VMEM(project.shape, BF16),
-            pltpu.VMEM((4, rows // 4, width), BF16),
-            pltpu.SemaphoreType.DMA((5,)),
+            pltpu.VMEM((rows, width), BF16),
+            pltpu.SemaphoreType.DMA((4,)),
         ],
     )(group_index, jnp.asarray(project), hidden_rows)
     received = exchange(moments.reshape(chips, -1, 128)).reshape(-1, 128)

time: 72.3 us -> 72.4 us (level)
  no operation moved by 1% of the time
where the time goes in v9:
time: 72.4 us; the launch traced here: 72 us
  starting transfers between devices  39 us (54%)
  blocking collectives  22.3 us (31%)
  Pallas kernels  6.22 us (9%)
  waiting for transfers between devices  4.38 us (6%)
    all_to_all x2, starting transfers between devices, exchange(): return lax.all_to_all(x, 'seq', 0, 0, axis_index_groups=groups)  32.8 us
    all_to_all x1, blocking collectives, exchange(): return lax.all_to_all(x, 'seq', 0, 0, axis_index_groups=groups)  20 us
    all_to_all x2, waiting for transfers between devices, exchange(): return lax.all_to_all(x, 'seq', 0, 0, axis_index_groups=groups)  4.37 us
    pallas_call x1, Pallas kernels, local(): kernel(moments_kernel, jax.ShapeDtypeStruct((width // 8, 128), F32), [SME...  2.96 us
    ppermute x1, starting transfers between devices, local(): lax.ppermute(beside, 'seq', other_core)  2.41 us
    all_gather x1, blocking collectives, gather_pair(): return lax.all_gather(x, 'seq', axis_index_groups=pairs)  2.22 us
    ppermute x1, starting transfers between devices, local(): beside = lax.ppermute(own, 'seq', [(i, i ^ 2) for i in range(windows)])  1.92 us
    ppermute x1, starting transfers between devices, local(): lax.ppermute(own, 'seq', other_core)  1.92 us
  transfers between devices with their start and end apart: 5, of which 2 were waited for; matrix products, arithmetic and copies ran while one was open for 0% of the time, Pallas kernels for 2%

profile of v9, /device:TPU:1, one launch (start us, length us, event | category | flops | bytes accessed | tf_op | source)
XLA Modules:
  0.0 72.0 jit_solution(8835971221762998665)
XLA Ops:
  0.0 0.0 copy-start.3
  0.0 0.0 copy-start.1
  0.1 3.0 %shard_map.64 = f32[256,128]{1,0:T(8,128)} custom-call(s32[1]{0:T(128)} %bitcast.group_ref, bf16[32,512]{1,0:T(8,128)(2,1)} %constant.38.clone.project_hbm, bf16[512,2048]{1,0:T(8,128)(2,1)} %rows_hbm.1), custom_call_target="tpu_custom_call" | custom-call | tf_op jit(solution)/shard_map/pallas_call | solution.py:189
  3.0 20.6 %all-to-all-start = ((f32[64,4,128]{2,1,0:T(4,128)}), f32[64,4,128]{2,1,0:T(4,128)S(1)}, u32[]{:S(2)}, u32[]{:S(2)}) async-start(f32[64,4,128]{2,1,0:T(4,128)} %bitcast.10), calls=%async_computation | async-start | bytes 262144 | tf_op jit(solution)/shard_map/all_to_all | solution.py:173
  23.7 0.0 copy-done.2
  23.7 0.0 copy-done.1
  23.7 1.9 %collective-permute-start = (bf16[128,2048]{1,0:T(8,128)(2,1)S(1)}, bf16[128,2048]{1,0:T(8,128)(2,1)S(1)}, u32[]{:S(2)}, u32[]{:S(2)}) collective-permute-start(bf16[128,2048]{1,0:T(8,128)(2,1)S(1)} %shard_map.68.refs_0_), channel_id=1, source_target_pairs={{0,2},{1,3},{2,0},{3,1},{4,6},{5,7},{6,4},{7,5},{8,10},{9,11},{10,... | collective-permute-start | bytes 1572872 | tf_op jit(solution)/shard_map/ppermute | solution.py:204
  25.7 1.9 %all-to-all-done = f32[64,4,128]{2,1,0:T(4,128)S(1)} async-done(((f32[64,4,128]{2,1,0:T(4,128)}), f32[64,4,128]{2,1,0:T(4,128)S(1)}, u32[]{:S(2)}, u32[]{:S(2)}) %all-to-all-start) | async-done | bytes 131104 | tf_op jit(solution)/shard_map/all_to_all | solution.py:173
  27.6 0.0 copy-done.3
  27.6 0.0 copy-done
  27.6 0.3 shard_map.65
  27.9 2.2 %all-gather = f32[64,256]{1,0:T(8,128)S(1)} all-gather(f32[32,256]{1,0:T(8,128)S(1)} %shard_map.65), channel_id=2, replica_groups={{0,1},{2,3},{4,5},{6,7},{8,9},{10,11},{12,13},{14,15},{16,17},{18,19},{..., dimensions={0}, use_global_device_ids=true | all-gather | bytes 98304 | tf_op jit(solution)/shard_map/all_gather | solution.py:176
  30.2 0.8 %shard_map.66 = (bf16[16,256]{1,0:T(8,128)(2,1)S(1)}, bf16[64,16,128]{2,1,0:T(8,128)(2,1)}) custom-call(s32[1]{0:T(128)} %bitcast.1.core_ref, s32[1]{0:T(128)} %bitcast.group_ref, f32[2,32,256]{2,1,0:T(8,128)S(1)} %bitcast.8), custom_call_target="tpu_custom_call" | custom-call | tf_op jit(solution)/shard_map/pallas_call | solution.py:211
  31.0 12.1 %all-to-all-start.1 = ((bf16[64,16,128]{2,1,0:T(8,128)(2,1)}), bf16[64,16,128]{2,1,0:T(8,128)(2,1)S(1)}, u32[]{:S(2)}, u32[]{:S(2)}) async-start(bf16[64,16,128]{2,1,0:T(8,128)(2,1)} %get-tuple-element.7), calls=%async_computation.1 | async-start | bytes 524288 | tf_op jit(solution)/shard_map/all_to_all | solution.py:173
  43.1 1.9 %collective-permute-start.1 = (bf16[128,2048]{1,0:T(8,128)(2,1)S(1)}, bf16[128,2048]{1,0:T(8,128)(2,1)S(1)}, u32[]{:S(2)}, u32[]{:S(2)}) collective-permute-start(bf16[128,2048]{1,0:T(8,128)(2,1)S(1)} %shard_map.68.refs_0_), channel_id=1, source_target_pairs={{0,1},{1,0},{2,3},{3,2},{4,5},{5,4},{6,7},{7,6},{8,9},{9,8},{10,11... | collective-permute-start | bytes 1572872 | tf_op jit(solution)/shard_map/ppermute | solution.py:206
  45.0 0.0 collective-permute-done.refs_1_
  45.0 2.4 %collective-permute-start.2 = (bf16[128,2048]{1,0:T(8,128)(2,1)S(1)}, bf16[128,2048]{1,0:T(8,128)(2,1)S(1)}, u32[]{:S(2)}, u32[]{:S(2)}) collective-permute-start(bf16[128,2048]{1,0:T(8,128)(2,1)S(1)} %collective-permute-done.refs_1_), channel_id=1, source_target_pairs={{0,1},{1,0},{2,3},{3,2},{4,5},{5,4},{6,7},{7,6},{8,9},{9,8},{10,11... | collective-permute-start | bytes 1572872 | tf_op jit(solution)/shard_map/ppermute | solution.py:206
  47.5 2.5 %all-to-all-done.1.packed_ref = bf16[64,16,128]{2,1,0:T(8,128)(2,1)S(1)} async-done(((bf16[64,16,128]{2,1,0:T(8,128)(2,1)}), bf16[64,16,128]{2,1,0:T(8,128)(2,1)S(1)}, u32[]{:S(2)}, u32[]{:S(2)}) %all-to-all-start.1) | async-done | bytes 262176 | tf_op jit(solution)/shard_map/all_to_all | solution.py:173
  49.9 0.2 shard_map.67.scale_ref
  50.1 0.0 collective-permute-done.1.refs_2_
  50.1 0.0 collective-permute-done.2.refs_3_
  50.1 1.1 %shard_map.69 = bf16[128,8,128]{2,1,0:T(8,128)(2,1)S(1)} custom-call(s32[1]{0:T(128)} %bitcast.group_ref, bf16[64,16,128]{2,1,0:T(8,128)(2,1)S(1)} %all-to-all-done.1.packed_ref, f32[1,128]{1,0:T(1,128)S(1)} %shard_map.67.scale_ref, bf16[128,2048]{1,0:T(8,128)(2,1)S(1)} %shard_map.68.refs_0_, bf16[128,2048]{1,0:T(8,128)(2,1)S(1)} %collective-permute-done.refs_1_, ...), custom_call_target="tpu_custom_call" | custom-call | tf_op jit(solution)/shard_map/pallas_call | solution.py:226
  51.3 20.0 %all_to_all.15.parts_ref = bf16[128,8,128]{2,1,0:T(8,128)(2,1)S(1)} all-to-all(bf16[128,8,128]{2,1,0:T(8,128)(2,1)S(1)} %shard_map.69), channel_id=1, replica_groups={{73,72,75,74,77,76,79,78,81,80,83,82,85,84,87,86,89,88,91,90,93,92,95,9..., dimensions={0} | all-to-all | bytes 524288 | tf_op jit(solution)/shard_map/all_to_all | solution.py:173
  71.3 0.7 shard_map.70
  (3 shorter events, 0.0 us)
Async XLA Ops:
  0.0 27.6 %copy-start.3 = (f32[16,256]{1,0:T(8,128)S(1)}, f32[16,256]{1,0:T(8,128)}, u32[]{:S(2)}) copy-start(f32[16,256]{1,0:T(8,128)} %constant.40.clone.expand_ref) | copy-start | bytes 49156
  0.0 27.6 %copy-start = (bf16[2,256,512]{2,1,0:T(8,128)(2,1)S(1)}, bf16[2,256,512]{2,1,0:T(8,128)(2,1)}, u32[]{:S(2)}) copy-start(bf16[2,256,512]{2,1,0:T(8,128)(2,1)} %constant.39.clone.trig_ref) | copy-start | bytes 1572868
  0.0 23.7 %copy-start.2 = (bf16[64,2048]{1,0:T(8,128)(2,1)S(1)}, bf16[64,2048]{1,0:T(8,128)(2,1)}, u32[]{:S(2)}) copy-start(bf16[64,2048]{1,0:T(8,128)(2,1)} %contract_ref.1) | copy-start | bytes 786436
  0.0 23.7 %copy-start.1 = (bf16[2048,64]{0,1:T(8,128)(2,1)S(1)}, bf16[2048,64]{0,1:T(8,128)(2,1)}, u32[]{:S(2)}) copy-start(bf16[2048,64]{0,1:T(8,128)(2,1)} %param.7) | copy-start | bytes 786436
  3.0 24.6 %all-to-all-start = ((f32[64,4,128]{2,1,0:T(4,128)}), f32[64,4,128]{2,1,0:T(4,128)S(1)}, u32[]{:S(2)}, u32[]{:S(2)}) async-start(f32[64,4,128]{2,1,0:T(4,128)} %bitcast.10), calls=%async_computation | async-start | bytes 262144 | tf_op jit(solution)/shard_map/all_to_all | solution.py:173
  23.7 21.3 %collective-permute-start = (bf16[128,2048]{1,0:T(8,128)(2,1)S(1)}, bf16[128,2048]{1,0:T(8,128)(2,1)S(1)}, u32[]{:S(2)}, u32[]{:S(2)}) collective-permute-start(bf16[128,2048]{1,0:T(8,128)(2,1)S(1)} %shard_map.68.refs_0_), channel_id=1, source_target_pairs={{0,2},{1,3},{2,0},{3,1},{4,6},{5,7},{6,4},{7,5},{8,10},{9,11},{10,... | collective-permute-start | bytes 1572872 | tf_op jit(solution)/shard_map/ppermute | solution.py:204
  31.0 19.0 %all-to-all-start.1 = ((bf16[64,16,128]{2,1,0:T(8,128)(2,1)}), bf16[64,16,128]{2,1,0:T(8,128)(2,1)S(1)}, u32[]{:S(2)}, u32[]{:S(2)}) async-start(bf16[64,16,128]{2,1,0:T(8,128)(2,1)} %get-tuple-element.7), calls=%async_computation.1 | async-start | bytes 524288 | tf_op jit(solution)/shard_map/all_to_all | solution.py:173
  43.1 7.0 %collective-permute-start.1 = (bf16[128,2048]{1,0:T(8,128)(2,1)S(1)}, bf16[128,2048]{1,0:T(8,128)(2,1)S(1)}, u32[]{:S(2)}, u32[]{:S(2)}) collective-permute-start(bf16[128,2048]{1,0:T(8,128)(2,1)S(1)} %shard_map.68.refs_0_), channel_id=1, source_target_pairs={{0,1},{1,0},{2,3},{3,2},{4,5},{5,4},{6,7},{7,6},{8,9},{9,8},{10,11... | collective-permute-start | bytes 1572872 | tf_op jit(solution)/shard_map/ppermute | solution.py:206
  45.0 5.1 %collective-permute-start.2 = (bf16[128,2048]{1,0:T(8,128)(2,1)S(1)}, bf16[128,2048]{1,0:T(8,128)(2,1)S(1)}, u32[]{:S(2)}, u32[]{:S(2)}) collective-permute-start(bf16[128,2048]{1,0:T(8,128)(2,1)S(1)} %collective-permute-done.refs_1_), channel_id=1, source_target_pairs={{0,1},{1,0},{2,3},{3,2},{4,5},{5,4},{6,7},{7,6},{8,9},{9,8},{10,11... | collective-permute-start | bytes 1572872 | tf_op jit(solution)/shard_map/ppermute | solution.py:206
